TPU v7x, 32 devices: a whole 2x2x4 slice. The times are simulated.
32 devices in a mesh: dp: 8 (over z, core), mp: 4 (over y, x).
Axes of the slice: x: 2, y: 2, z: 4, core: 2. Of those that a mesh axis runs over, the one named last changes fastest.
Arguments:
- tokens: bfloat16 [6144, 8192], P('dp', 'mp'), may hold values from -6 to 6
- frozen_weight: bfloat16 [8192, 2048], P('mp', 'dp'), may hold values from -0.0625 to 0.0625
- adapter_down_weight: bfloat16 [8192, 1024], P(None, 'mp'), may hold values from -0.0625 to 0.0625
- adapter_up_weight: bfloat16 [2, 32, 16, 1024], P(None, 'mp'), may hold values from -1.5 to 1.5
- token_adapter_index: int32 [6144], P('dp'), may hold values from 0 to 31, as said below
Outputs:
- projected: bfloat16 [6144, 2048], P(('dp', 'mp'))
Inputs may be any that keep to these rules, and one draw needn't show every extreme that they name: `token_adapter_index`: A token's owner is its adapter id divided by 8, rounded down. Of the 192 tokens of each aligned block of rows (the rows of one device's output), at most 96 have the same owner; in each run of 4 such blocks that one dp index holds, one owner has exactly 96 tokens in every block.
All inputs are finite; a program needn't handle non-finite values.
Results may differ from a plain program's by a relative error of at most 0.0055.
Values may be sent and summed in bfloat16 or wider, within the bound.
No kernel may reach another device: no remote copies, remote signals or barrier semaphores. Data moves between devices by JAX's collectives and lax.ppermute only.
A program may use at most 128 MiB of HBM per device.

v0:
```python
import jax
import jax.numpy as jnp
from jax import lax
from jax.sharding import PartitionSpec as P

ADAPTER_SCALE = 2.0


def local(tokens, frozen_weight, adapter_down_weight, adapter_up_weight, token_adapter_index):
    mp_count = lax.axis_size("mp")
    position = lax.axis_index("mp")
    group_rows, feature_cols = tokens.shape
    own_rows = group_rows // mp_count
    capacity = 2 * own_rows // mp_count
    hidden_width = adapter_down_weight.shape[0]
    present_adapters = adapter_up_weight.shape[1]
    rank_extent = adapter_up_weight.shape[2]
    key_value_span = adapter_up_weight.shape[3]
    both_width = 2 * key_value_span
    per_owner = mp_count * capacity
    slot_total = mp_count * per_owner
    owners_of = token_adapter_index // present_adapters
    local_adapter = token_adapter_index % present_adapters
    owner_hits = (owners_of[:, None] == jnp.arange(mp_count, dtype=jnp.int32)[None, :]).astype(
        jnp.int32
    )
    running = jnp.cumsum(owner_hits.reshape(mp_count, own_rows, mp_count), axis=1).reshape(
        group_rows, mp_count
    )
    order_in = jnp.sum(running * owner_hits, axis=1) - 1
    block_index = jnp.arange(group_rows, dtype=jnp.int32) // own_rows
    slot_index = owners_of * per_owner + block_index * capacity + order_in
    slot_token = (
        jnp.full((slot_total,), group_rows, jnp.int32)
        .at[slot_index]
        .set(jnp.arange(group_rows, dtype=jnp.int32))
    )
    slot_adapter = jnp.full((slot_total,), -1, jnp.int32).at[slot_index].set(local_adapter)
    padded = jnp.concatenate([tokens, jnp.zeros((1, feature_cols), tokens.dtype)], axis=0)
    outgoing = jnp.take(padded, slot_token, axis=0).reshape(
        mp_count, mp_count, capacity, feature_cols
    )
    labels = slot_adapter.reshape(mp_count, mp_count, capacity, 1)
    key_up_weight = adapter_up_weight[0].reshape(present_adapters * rank_extent, key_value_span)
    value_up_weight = adapter_up_weight[1].reshape(present_adapters * rank_extent, key_value_span)
    received = lax.all_to_all(outgoing, "mp", split_axis=0, concat_axis=3, tiled=True)
    tags = lax.all_to_all(labels, "mp", split_axis=0, concat_axis=3, tiled=True)
    items = received.shape[2]
    flat_tokens = received.reshape(-1, hidden_width)
    adapter_tag = tags[..., 0].reshape(-1)
    full_projection = jnp.dot(flat_tokens, adapter_down_weight, preferred_element_type=jnp.float32)
    selector = (
        adapter_tag[:, None] == jnp.arange(present_adapters, dtype=jnp.int32)[None, :]
    ).astype(jnp.float32)
    low_rows = (
        full_projection.reshape(-1, present_adapters, 2, rank_extent) * selector[:, :, None, None]
    ).astype(jnp.bfloat16)
    key_section = jnp.dot(
        low_rows[:, :, 0, :].reshape(-1, present_adapters * rank_extent),
        key_up_weight,
        preferred_element_type=jnp.float32,
    )
    value_section = jnp.dot(
        low_rows[:, :, 1, :].reshape(-1, present_adapters * rank_extent),
        value_up_weight,
        preferred_element_type=jnp.float32,
    )
    adapter_updates = (
        ADAPTER_SCALE * jnp.concatenate([key_section, value_section], axis=1)
    ).astype(jnp.bfloat16)
    adapter_updates = adapter_updates.reshape(1, mp_count, items, both_width)
    arrived = lax.all_to_all(adapter_updates, "mp", split_axis=1, concat_axis=0, tiled=True)
    weight_full = lax.all_gather(frozen_weight, "dp", axis=1, tiled=True)
    own_owner = lax.dynamic_slice_in_dim(owners_of, position * own_rows, own_rows)
    own_order = lax.dynamic_slice_in_dim(order_in, position * own_rows, own_rows)
    own_delta = arrived[own_owner, 0, own_order]
    base_rows = lax.psum_scatter(
        jnp.dot(tokens, weight_full, preferred_element_type=jnp.float32),
        "mp",
        scatter_dimension=0,
        tiled=True,
    )
    return (base_rows + own_delta.astype(jnp.float32)).astype(jnp.bfloat16)


def solution(mesh):
    placed = (P("dp", "mp"), P("mp", "dp"), P(None, "mp"), P(None, "mp", None, None), P("dp"))
    return jax.shard_map(
        local, mesh=mesh, in_specs=placed, out_specs=P(("dp", "mp"), None), check_vma=False
    )
```

profile of v0, /device:TPU:0, one launch (start us, length us, event | category | flops | bytes accessed | tf_op | source)
XLA Modules:
  0.0 298.3 jit_solution(12083798574666965195)
XLA Ops:
  6.5 0.7 all-gather.2.cloned.1.call-update
  7.3 0.7 add_select_fusion.2
  8.1 4.8 %reduce-window.6 = s32[4,4,2,128]{3,2,1,0:T(2,128)S(1)} reduce-window(s32[4,4,2,128]{3,2,1,0:T(2,128)S(1)} %reshape.134, s32[]{:T(128)} %constant.65.clone.1), window={size=1x1x1x128 pad=0_0x0_0x0_0x127_0}, to_apply=%region_1.2 | reduce-window | flops 520192 | bytes 32772 | tf_op jit(solution)/shard_map/reduce-window
  13.3 80.9 %all-gather.2.cloned.1.call-done = bf16[2048,2048]{1,0:T(8,128)(2,1)} async-done(((bf16[2048,256]{1,0:T(8,128)(2,1)}), bf16[2048,2048]{1,0:T(8,128)(2,1)}) %all-gather.2.cloned.1.call-update) | async-done | bytes 8388624 | tf_op jit(solution)/shard_map/all_gather | solution.py:73
  94.2 11.7 %fusion.35 = f32[768,2048]{1,0:T(8,128)} fusion(bf16[768,2048]{1,0:T(8,128)(2,1)} %param.5, bf16[2048,2048]{1,0:T(8,128)(2,1)} %all-gather.2.cloned.1.call-done), kind=kOutput, calls=%fused_computation.63 | convolution fusion | flops 6442450944 | bytes 17825792 | tf_op jit(solution)/shard_map/dot_general | solution.py:78
  106.1 0.4 copy-done.1
  106.6 3.4 %scatter_custom_fusion.1 = s32[1536]{0:T(1024)S(1)} fusion(s32[768]{0:T(1024)S(1)} %get-tuple-element.10, s32[768]{0:T(1024)S(1)} %get-tuple-element.9, s32[]{:T(128)} %constant.68.clone.1), kind=kCustom, calls=%fused_computation.45 | custom fusion | bytes 6148 | tf_op jit(solution)/shard_map/scatter | solution.py:38
  110.0 0.7 reshape.131
  110.6 3.6 %all-to-all-start.1 = ((s32[4,4,96,1]{2,1,3,0:T(4,128)}), s32[4,4,96,1]{2,1,3,0:T(4,128)S(1)}, u32[]{:S(2)}, u32[]{:S(2)}) async-start(s32[4,4,96,1]{2,1,3,0:T(4,128)} %bitcast.8), calls=%async_computation.2 | async-start | bytes 16384 | tf_op jit(solution)/shard_map/all_to_all | solution.py:47
  114.3 3.4 %scatter_custom_fusion = s32[1536]{0:T(1024)S(1)} fusion(s32[768]{0:T(1024)S(1)} %get-tuple-element.10, s32[768]{0:T(1024)S(1)} %iota.26, s32[]{:T(128)} %constant.63.clone.1), kind=kCustom, calls=%fused_computation.48 | custom fusion | bytes 6148 | tf_op jit(solution)/shard_map/scatter | solution.py:36
  117.8 2.5 concatenate.20
  120.3 7.1 %gather_fusion = bf16[1536,2048]{1,0:T(8,128)(2,1)} fusion(bf16[769,2048]{1,0:T(8,128)(2,1)S(1)} %concatenate.20, s32[2048]{0:T(1024)S(1)} %pad_clamp_fusion), kind=kCustom, calls=%fused_computation | custom fusion | bytes 12589056 | tf_op jit(solution)/shard_map/jit(_take)/gather | solution.py:40
  127.4 6.1 %broadcast_select_fusion = bf16[4,4,96,2048]{3,2,1,0:T(8,128)(2,1)} fusion(bf16[4,4,96,2048]{3,2,1,0:T(8,128)(2,1)} %bitcast.55, pred[4,4,96]{2,1,0:T(4,128)(4,1)S(1)} %broadcast_in_dim.40), kind=kLoop, calls=%fused_computation.6 | loop fusion | flops 3145728 | bytes 12584448 | tf_op jit(solution)/shard_map/jit(_take)/select_n | solution.py:40
  133.5 5.5 %all-to-all-start = ((bf16[4,4,96,2048]{3,2,1,0:T(8,128)(2,1)}), bf16[4,4,96,2048]{3,2,1,0:T(8,128)(2,1)}, u32[]{:S(2)}, u32[]{:S(2)}) async-start(bf16[4,4,96,2048]{3,2,1,0:T(8,128)(2,1)} %broadcast_select_fusion), calls=%async_computation.1 | async-start | bytes 12582912 | tf_op jit(solution)/shard_map/all_to_all | solution.py:46
  139.1 6.5 %copy.24 = bf16[8192,256]{0,1:T(8,128)(2,1)} copy(bf16[8192,256]{1,0:T(8,128)(2,1)} %param.7) | data formatting | bytes 8388608 | tf_op args[2]
  145.7 85.2 %all-to-all-done = bf16[4,4,96,2048]{3,2,1,0:T(8,128)(2,1)} async-done(((bf16[4,4,96,2048]{3,2,1,0:T(8,128)(2,1)}), bf16[4,4,96,2048]{3,2,1,0:T(8,128)(2,1)}, u32[]{:S(2)}, u32[]{:S(2)}) %all-to-all-start) | async-done | bytes 6291488 | tf_op jit(solution)/shard_map/all_to_all | solution.py:46
  230.9 10.4 %copy.23 = bf16[1,4,96,4,2048]{4,3,2,1,0:T(4,128)(2,1)} copy(bf16[1,4,96,4,2048]{4,2,1,3,0:T(8,128)(2,1)} %bitcast.4) | data formatting | bytes 12582912 | tf_op jit(solution)/shard_map/all_to_all | solution.py:46
  241.3 11.1 %reshape.180 = bf16[384,8192,1,1]{1,0,2,3:T(8,128)(2,1)} reshape(bf16[1,4,96,4,2048]{4,3,2,1,0:T(4,128)(2,1)} %copy.23) | data formatting | bytes 12582912 | tf_op jit(solution)/shard_map/reshape | solution.py:49
  252.4 6.4 %fusion.7 = bf16[384,8,2,16]{0,3,2,1:T(8,128)(2,1)S(1)} fusion(bf16[8,2,16,8192]{3,2,1,0:T(8,128)(2,1)} %bitcast.56, bf16[384,8192,1,1]{1,0,2,3:T(8,128)(2,1)} %reshape.180, f32[384,8]{0,1:T(8,128)S(1)} %fusion.13), kind=kOutput, calls=%fused_computation.14 | convolution fusion | flops 1610809344 | bytes 10694656 | tf_op jit(solution)/shard_map/dot_general | solution.py:51
  259.8 1.5 fusion.3
  261.3 3.8 %all-to-all-start.2 = ((bf16[1,4,96,2048]{3,2,0,1:T(8,128)(2,1)}), bf16[1,4,96,2048]{3,2,0,1:T(8,128)(2,1)S(1)}, u32[]{:S(2)}, u32[]{:S(2)}) async-start(bf16[1,4,96,2048]{3,2,0,1:T(8,128)(2,1)} %fusion.3), calls=%async_computation.3 | async-start | bytes 3145728 | tf_op jit(solution)/shard_map/all_to_all | solution.py:72
  265.1 19.2 %all-to-all-done.2 = bf16[1,4,96,2048]{3,2,0,1:T(8,128)(2,1)S(1)} async-done(((bf16[1,4,96,2048]{3,2,0,1:T(8,128)(2,1)}), bf16[1,4,96,2048]{3,2,0,1:T(8,128)(2,1)S(1)}, u32[]{:S(2)}, u32[]{:S(2)}) %all-to-all-start.2) | async-done | bytes 1572896 | tf_op jit(solution)/shard_map/all_to_all | solution.py:72
  284.3 4.7 %gather_fusion.1 = bf16[192,2048]{1,0:T(8,128)(2,1)S(1)} fusion(bf16[4,1,96,2048]{3,2,1,0:T(8,128)(2,1)S(1)} %bitcast.54, s32[192]{0:T(256)S(1)} %fusion.30), kind=kCustom, calls=%fused_computation.1 | custom fusion | bytes 1575168 | tf_op jit(solution)/shard_map/gather | solution.py:76
  289.0 2.5 add_convert_fusion
  (38 shorter events, 2.1 us)
Async XLA Ops:
  6.5 87.7 %all-gather.2.cloned.1.call-start = ((), (), s32[]{:S(2)}) async-start(), calls=%async_computation.4 | async-start | bytes 9437184 | tf_op jit(solution)/shard_map/all_gather | solution.py:73
  7.3 281.7 %reduce-scatter.2.cloned.1.call-start = ((), (), s32[]{:S(2)}) async-start(), calls=%async_computation.5 | async-start | bytes 7864320 | tf_op jit(solution)/shard_map/reduce_scatter | solution.py:77
  105.9 0.7 copy-start.1
  110.6 22.9 %all-to-all-start.1 = ((s32[4,4,96,1]{2,1,3,0:T(4,128)}), s32[4,4,96,1]{2,1,3,0:T(4,128)S(1)}, u32[]{:S(2)}, u32[]{:S(2)}) async-start(s32[4,4,96,1]{2,1,3,0:T(4,128)} %bitcast.8), calls=%async_computation.2 | async-start | bytes 16384 | tf_op jit(solution)/shard_map/all_to_all | solution.py:47
  133.5 97.4 %all-to-all-start = ((bf16[4,4,96,2048]{3,2,1,0:T(8,128)(2,1)}), bf16[4,4,96,2048]{3,2,1,0:T(8,128)(2,1)}, u32[]{:S(2)}, u32[]{:S(2)}) async-start(bf16[4,4,96,2048]{3,2,1,0:T(8,128)(2,1)} %broadcast_select_fusion), calls=%async_computation.1 | async-start | bytes 12582912 | tf_op jit(solution)/shard_map/all_to_all | solution.py:46
  139.1 6.5 %copy-start = (bf16[2,8,16,1024]{3,2,1,0:T(8,128)(2,1)S(1)}, bf16[2,8,16,1024]{3,2,1,0:T(8,128)(2,1)}, u32[]{:S(2)}) copy-start(bf16[2,8,16,1024]{3,2,1,0:T(8,128)(2,1)} %param.8) | copy-start | bytes 1572868
  261.3 23.0 %all-to-all-start.2 = ((bf16[1,4,96,2048]{3,2,0,1:T(8,128)(2,1)}), bf16[1,4,96,2048]{3,2,0,1:T(8,128)(2,1)S(1)}, u32[]{:S(2)}, u32[]{:S(2)}) async-start(bf16[1,4,96,2048]{3,2,0,1:T(8,128)(2,1)} %fusion.3), calls=%async_computation.3 | async-start | bytes 3145728 | tf_op jit(solution)/shard_map/all_to_all | solution.py:72
Sparse Core Ops, SparseCore 0:
  8.9 85.2 all-gather.1
  106.0 125.7 reduce-scatter.1
where the time goes:
time: 299 us; the launch traced here: 298 us
  waiting for transfers between devices  186 us (62%)
  local copies, waits for them, and re-layouts  51.1 us (17%)
  matrix products  18.8 us (6%)
  other arithmetic  15.9 us (5%)
  between operations  13.6 us (5%)
  starting transfers between devices  13 us (4%)
    all_to_all x1, waiting for transfers between devices, local(): lax.all_to_all(outgoing, 'mp', split_axis=0, concat_axis=3, tiled=True)  85.2 us
    all_gather x1, waiting for transfers between devices, local(): weight_full = lax.all_gather(frozen_weight, 'dp', axis=1, tiled=True)  80.9 us
    all_to_all x1, waiting for transfers between devices, local(): lax.all_to_all(adapter_updates, 'mp', split_axis=1, concat_axis=0, tiled=...  19.2 us
    dot_general x1, matrix products, local(): jnp.dot(tokens, weight_full, preferred_element_type=jnp.float32)  11.7 us
    reshape x1, local copies, waits for them, and re-layouts, local(): flat_tokens = received.reshape(-1, hidden_width)  11.1 us
    all_to_all x1, local copies, waits for them, and re-layouts, local(): lax.all_to_all(outgoing, 'mp', split_axis=0, concat_axis=3, tiled=True)  10.4 us
    gather x1, local copies, waits for them, and re-layouts, local(): jnp.take(padded, slot_token, axis=0)  7.15 us
    unnamed x5, local copies, waits for them, and re-layouts  6.91 us
  transfers between devices with their start and end apart: 5, of which 3 were waited for; matrix products, arithmetic and copies ran while one was open for 24% of the time, Pallas kernels for 0%

commit v1 on v0

v1 whole, which is shorter than its diff:
```python
import functools

import jax
import jax.numpy as jnp
from jax import lax
from jax.experimental import pallas as pl
from jax.experimental.pallas import tpu as pltpu
from jax.sharding import PartitionSpec as P

ADAPTER_SCALE = 2.0
CORES = 2
LANES = 128
VMEM_BYTES = 40 * 1024 * 1024


def params():
    return pltpu.CompilerParams(vmem_limit_bytes=VMEM_BYTES)


def load_all(pairs, sems):
    copies = [pltpu.make_async_copy(src, dst, sems.at[n]) for n, (src, dst) in enumerate(pairs)]
    for copy in copies:
        copy.start()
    for copy in copies:
        copy.wait()


def base_kernel(peers_ref, tokens_ref, mine_ref, other_ref, *rest):
    outs, (weight, sems) = rest[:-2], rest[-2:]
    step = pl.program_id(0)
    span = mine_ref.shape[1]

    @pl.when(step == 0)
    def _():
        load_all([(mine_ref, weight.at[:, :span]), (other_ref, weight.at[:, span:])], sems)

    product = jnp.dot(tokens_ref[...], weight[...], preferred_element_type=jnp.float32)
    for number, out in enumerate(outs):

        @pl.when(step == number)
        def _(out=out):
            out[...] = product.astype(out.dtype)


def base_products(peers, tokens, mine, other, mp_count):
    group_rows, features = tokens.shape
    rows, span = group_rows // mp_count, mine.shape[1]
    types = [jnp.float32] + [jnp.bfloat16] * (mp_count - 1)
    return pl.pallas_call(
        base_kernel,
        grid_spec=pltpu.PrefetchScalarGridSpec(
            num_scalar_prefetch=1,
            grid=(mp_count,),
            in_specs=[
                pl.BlockSpec((rows, features), lambda i, peers_ref: (peers_ref[i], 0)),
                pl.BlockSpec(memory_space=pl.ANY),
                pl.BlockSpec(memory_space=pl.ANY),
            ],
            out_specs=[pl.BlockSpec((rows, 2 * span), lambda i, peers_ref: (0, 0)) for _ in types],
            scratch_shapes=[pltpu.VMEM((features, 2 * span), mine.dtype), pltpu.SemaphoreType.DMA((2,))],
        ),
        out_shape=[jax.ShapeDtypeStruct((rows, 2 * span), kind) for kind in types],
        compiler_params=params(),
        cost_estimate=pl.CostEstimate(
            flops=4 * group_rows * features * span,
            bytes_accessed=2 * group_rows * features + 4 * features * span,
            transcendentals=0,
        ),
    )(peers, tokens, mine, other)


def low_kernel(mp_count, adapters, peers_ref, core_ref, tokens_ref, ids_ref, down_ref, *rest):
    pieces = rest[: 2 * (mp_count - 1)]
    outs = rest[2 * (mp_count - 1) : -2]
    weight, sems = rest[-2:]
    step, core = pl.program_id(0), core_ref[0]
    features = tokens_ref.shape[1]
    width = down_ref.shape[1]
    half = width // 2

    @pl.when(step == 0)
    def _():
        first = pl.multiple_of(peers_ref[0] * features, features)
        pairs = [(down_ref.at[pl.ds(first, features), :], weight.at[:, :width])]
        for number, piece in enumerate(pieces):
            pairs.append((piece, weight.at[:, width + number * half : width + (number + 1) * half]))
        load_all(pairs, sems)

    product = jnp.dot(tokens_ref[...], weight[...], preferred_element_type=jnp.float32)
    ids = ids_ref[...]
    rank_pair = width // adapters
    rows = ids.shape[0]
    lane_adapter = lax.broadcasted_iota(jnp.int32, (rows, half), 1) // rank_pair
    total = jnp.zeros((rows, half), jnp.float32)
    for number in range(2 * mp_count):
        owner = peers_ref[number // 2]
        if number < 2:
            part = number
        else:
            part = core if number % 2 == 0 else 1 - core
        wanted = ids - (owner * adapters + part * (adapters // 2))
        total += jnp.where(lane_adapter == wanted, product[:, number * half : (number + 1) * half], 0.0)
    shift = half // 2
    while shift >= rank_pair:
        total = total + pltpu.roll(total, shift, 1)
        shift //= 2
    for number, out in enumerate(outs):

        @pl.when(step == number)
        def _(out=out):
            out[...] = total


def low_sums(peers, core, tokens, ids, down, pieces, mp_count, adapters):
    group_rows, features = tokens.shape
    rows, width = group_rows // mp_count, down.shape[1]
    return pl.pallas_call(
        functools.partial(low_kernel, mp_count, adapters),
        grid_spec=pltpu.PrefetchScalarGridSpec(
            num_scalar_prefetch=2,
            grid=(mp_count,),
            in_specs=[
                pl.BlockSpec((rows, features), lambda i, peers_ref, core_ref: (peers_ref[i], 0)),
                pl.BlockSpec((rows, 1), lambda i, peers_ref, core_ref: (peers_ref[i], 0)),
            ]
            + [pl.BlockSpec(memory_space=pl.ANY)] * (1 + len(pieces)),
            out_specs=[
                pl.BlockSpec((rows, width // 2), lambda i, peers_ref, core_ref: (0, 0)) for _ in range(mp_count)
            ],
            scratch_shapes=[
                pltpu.VMEM((features, mp_count * width), down.dtype),
                pltpu.SemaphoreType.DMA((1 + len(pieces),)),
            ],
        ),
        out_shape=[jax.ShapeDtypeStruct((rows, width // 2), jnp.float32)] * mp_count,
        compiler_params=params(),
        cost_estimate=pl.CostEstimate(
            flops=2 * group_rows * features * mp_count * width,
            bytes_accessed=2 * group_rows * features + 2 * features * mp_count * width,
            transcendentals=0,
        ),
    )(peers, core, tokens, ids, down, *pieces)


def delta_kernel(mp_count, adapters, rank, peers_ref, core_ref, ids_ref, up_ref, *rest):
    sums = rest[:mp_count]
    pieces = rest[mp_count : mp_count + 2 * (mp_count - 1)]
    out = rest[-1]
    core = core_ref[0]
    span = up_ref.shape[2]
    low = sums[0][...]
    for number in range(1, mp_count):
        low = low + sums[number][...]
    rows, lanes = low.shape
    ids = ids_ref[...]
    lane_block = lax.broadcasted_iota(jnp.int32, (rows, lanes), 1) // rank
    even = lane_block % 2 == 0
    key_low = jnp.where(even, low, pltpu.roll(low, rank, 1))
    value_low = jnp.where(even, pltpu.roll(low, lanes - rank, 1), low)

    def spread(values, owner):
        return jnp.where(lane_block == ids - owner * adapters, values, 0.0).astype(jnp.bfloat16)

    def times(values, weights):
        return jnp.dot(values, weights, preferred_element_type=jnp.float32)

    mine_low = jnp.where(core == 0, key_low, value_low)
    other_low = jnp.where(core == 0, value_low, key_low)
    own = peers_ref[0]
    mine = times(spread(mine_low, own), up_ref[core])
    other = times(spread(other_low, own), up_ref[1 - core])
    for number in range(1, mp_count):
        owner = peers_ref[number]
        mine += times(spread(mine_low, owner), pieces[2 * number - 2][...])
        other += times(spread(other_low, owner), pieces[2 * number - 1][...])
    mine_at = pl.multiple_of(core * span, span)
    other_at = pl.multiple_of((1 - core) * span, span)
    out[:, pl.ds(mine_at, span)] = (ADAPTER_SCALE * mine).astype(out.dtype)
    out[:, pl.ds(other_at, span)] = (ADAPTER_SCALE * other).astype(out.dtype)


def deltas_of(peers, core, ids, up, sums, pieces, adapters, rank):
    mp_count = len(sums)
    rows = sums[0].shape[0]
    span = up.shape[2]
    vmem = pl.BlockSpec(memory_space=pltpu.VMEM)
    smem = pl.BlockSpec(memory_space=pltpu.SMEM)
    return pl.pallas_call(
        functools.partial(delta_kernel, mp_count, adapters, rank),
        in_specs=[smem, smem] + [vmem] * (2 + mp_count + len(pieces)),
        out_specs=vmem,
        out_shape=jax.ShapeDtypeStruct((rows, 2 * span), jnp.bfloat16),
        compiler_params=params(),
        cost_estimate=pl.CostEstimate(
            flops=4 * rows * mp_count * adapters * rank * span,
            bytes_accessed=4 * mp_count * adapters * rank * span + 4 * rows * span,
            transcendentals=0,
        ),
    )(peers, core, ids, up, *sums, *pieces)


def finish_kernel(mp_count, columns_ref, delta_ref, *rest):
    parts = rest[:mp_count]
    out, delta, done, sems = rest[-4:]
    span = done.shape[1] // 2
    places = [pl.ds(pl.multiple_of(columns_ref[n], span), span) for n in range(2)]
    load_all([(delta_ref.at[:, places[n]], delta.at[:, n * span : (n + 1) * span]) for n in range(2)], sems)
    total = parts[0][...]
    for part in parts[1:]:
        total = total + part[...].astype(jnp.float32)
    done[...] = (total + delta[...].astype(jnp.float32)).astype(done.dtype)
    load_all([(done.at[:, n * span : (n + 1) * span], out.at[:, places[n]]) for n in range(2)], sems)


def finish(columns, delta, parts, held):
    rows, span = parts[0].shape
    vmem = pl.BlockSpec(memory_space=pltpu.VMEM)
    anywhere = pl.BlockSpec(memory_space=pl.ANY)
    operands = [columns, delta, *parts] + ([] if held is None else [held])
    return pl.pallas_call(
        functools.partial(finish_kernel, len(parts)),
        in_specs=[pl.BlockSpec(memory_space=pltpu.SMEM), anywhere]
        + [vmem] * len(parts)
        + ([] if held is None else [anywhere]),
        out_specs=anywhere,
        out_shape=jax.ShapeDtypeStruct(delta.shape, delta.dtype),
        scratch_shapes=[
            pltpu.VMEM((rows, span), delta.dtype),
            pltpu.VMEM((rows, span), delta.dtype),
            pltpu.SemaphoreType.DMA((2,)),
        ],
        input_output_aliases={} if held is None else {len(operands) - 1: 0},
        compiler_params=params(),
        cost_estimate=pl.CostEstimate(flops=4 * rows * span, bytes_accessed=12 * rows * span, transcendentals=0),
    )(*operands)


def by_plane(plane, values):
    return sum(jnp.where(plane == n, value, 0) for n, value in enumerate(values)).astype(jnp.int32)


def arrival_order(plane, planes):
    sides = (1, -1) if 2 * plane < planes else (-1, 1)
    return [
        (side, distance)
        for distance in range(1, planes)
        for side in sides
        if 0 <= plane + side * distance < planes
    ]


def local(tokens, frozen_weight, adapter_down_weight, adapter_up_weight, token_adapter_index):
    mp_count, dp_count = lax.axis_size("mp"), lax.axis_size("dp")
    position, replica = lax.axis_index("mp"), lax.axis_index("dp")
    planes = dp_count // CORES
    plane, core = replica // CORES, replica % CORES
    group_rows, features = tokens.shape
    rows = group_rows // mp_count
    width = frozen_weight.shape[1]
    chunk = min(width, LANES)
    chunks = width // chunk
    adapters, rank, span = adapter_up_weight.shape[1:]
    down_width = adapter_down_weight.shape[1]

    peers = (position ^ jnp.arange(mp_count, dtype=jnp.int32)).astype(jnp.int32)
    core_of = core.astype(jnp.int32).reshape(1)
    swap_pairs = [(n, n ^ 1) for n in range(dp_count)]

    def swap(array):
        return lax.ppermute(array, "dp", swap_pairs)

    def trade(array, number):
        return lax.ppermute(array, "mp", [(n, n ^ number) for n in range(mp_count)])

    def hop(array, side, step):
        if side > 0:
            sources = range(1, planes - step + 1)
        else:
            sources = range(step - 1, planes - 1)
        pairs = [
            (CORES * n + part, CORES * (n - side) + part) for n in sources for part in range(CORES)
        ]
        return lax.ppermute(array, "dp", pairs)

    own_chunks = [frozen_weight[:, n * chunk : (n + 1) * chunk] for n in range(chunks)]
    held = {}
    for n in range(chunks):
        for side in (1, -1):
            held[side, 1, n] = hop(own_chunks[n], side, 1)

    down_mine = []
    for number in range(1, mp_count):
        piece = lax.dynamic_slice(
            adapter_down_weight,
            (peers[number] * features, core * (down_width // 2)),
            (features, down_width // 2),
        )
        down_mine.append(trade(piece, number))
    up_flat = adapter_up_weight.reshape(2, adapters * rank, span)
    up_piece = lax.dynamic_index_in_dim(up_flat, core, 0, keepdims=False)

    def exchange(mine):
        parts = base_products(peers, tokens, mine, swap(mine), mp_count)
        return [parts[0]] + [trade(parts[number], number) for number in range(1, mp_count)]

    gathered = [(by_plane(plane, range(planes)), n, exchange(own_chunks[n])) for n in range(chunks)]

    for step in range(2, planes):
        for n in range(chunks):
            for side in (1, -1):
                held[side, step, n] = hop(held[side, step - 1, n], side, step)

    up_mine = [trade(up_piece, number) for number in range(1, mp_count)]

    down_pieces = [piece for mine in down_mine for piece in (mine, swap(mine))]
    ids = token_adapter_index.reshape(group_rows, 1)
    sums = low_sums(peers, core_of, tokens, ids, adapter_down_weight, down_pieces, mp_count, adapters)
    sums = [sums[0]] + [trade(sums[number], number) for number in range(1, mp_count)]
    up_pieces = [piece for mine in up_mine for piece in (mine, swap(mine))]
    own_ids = lax.dynamic_slice_in_dim(ids, position * rows, rows)
    delta = deltas_of(peers, core_of, own_ids, up_flat, sums, up_pieces, adapters, rank)

    orders = [arrival_order(n, planes) for n in range(planes)]
    for turn in range(planes - 1):
        wanted = [order[turn] for order in orders]
        options = sorted(set(wanted))
        choice = by_plane(plane, [options.index(item) for item in wanted])
        group = by_plane(plane, [n + side * distance for n, (side, distance) in enumerate(wanted)])
        for n in range(chunks):
            mine = held[(*options[0], n)]
            for number, option in enumerate(options[1:], 1):
                mine = jnp.where(choice == number, held[(*option, n)], mine)
            gathered.append((group, n, exchange(mine)))

    out = None
    for group, n, parts in gathered:
        first = group * (CORES * width) + n * chunk
        columns = jnp.stack([first + core * width, first + (1 - core) * width]).astype(jnp.int32)
        out = finish(columns, delta, parts, out)
    return out


def solution(mesh):
    placed = (P("dp", "mp"), P("mp", "dp"), P(None, "mp"), P(None, "mp", None, None), P("dp"))
    return jax.shard_map(
        local, mesh=mesh, in_specs=placed, out_specs=P(("dp", "mp"), None), check_vma=False
    )
```

time: 299 us -> 196 us (0.66)
  waiting for transfers between devices: 186 us -> 49.5 us
  starting transfers between devices: 13 us -> 68.3 us
  Pallas kernels: 0 us -> 41.7 us
  local copies, waits for them, and re-layouts: 51.1 us -> 29 us
  matrix products: 18.8 us -> 0 us
  other arithmetic: 15.9 us -> 2.59 us
  between operations: 13.6 us -> 3.6 us
    all_to_all x3 -> x0, waiting for transfers between devices: 104 us -> none  [the longest x1 85.2 us: local(): lax.all_to_all(outgoing, 'mp', split_axis=0, concat_axis=3, tiled=True)]
    all_gather x1 -> x0, waiting for transfers between devices: 80.9 us -> none  [local(): weight_full = lax.all_gather(frozen_weight, 'dp', axis=1, tiled=True)]
    ppermute x0 -> x59, starting transfers between devices: none -> 68.3 us  [the longest x33 44 us: trade(): return lax.ppermute(array, 'mp', [(n, n ^ number) for n in range(mp_count)])]
    ppermute x0 -> x59, waiting for transfers between devices: none -> 49.5 us  [the longest x33 29.5 us: trade(): return lax.ppermute(array, 'mp', [(n, n ^ number) for n in range(mp_count)])]
    pallas_call x0 -> x18, Pallas kernels: none -> 41.7 us  [the longest x8 21.2 us: base_products(): pl.pallas_call(base_kernel, grid_spec=pltpu.PrefetchScalarGridSpec(num_sc...]
    dot_general x4 -> x0, matrix products: 18.8 us -> none  [the longest x1 11.7 us: local(): jnp.dot(tokens, weight_full, preferred_element_type=jnp.float32)]
    unnamed x5 -> x172, local copies, waits for them, and re-layouts: 6.91 us -> 23.2 us
    all_to_all x3 -> x0, starting transfers between devices: 13 us -> none  [the longest x1 5.54 us: local(): lax.all_to_all(outgoing, 'mp', split_axis=0, concat_axis=3, tiled=True)]
  transfers between devices with their start and end apart: 5 -> 59, of which waited for: 3 -> 8; matrix products, arithmetic and copies ran while one was open for 24% -> 3% of each run, Pallas kernels for 0% -> 21%
where the time goes in v1:
time: 196 us; the launch traced here: 195 us
  starting transfers between devices  68.3 us (35%)
  waiting for transfers between devices  49.5 us (25%)
  Pallas kernels  41.7 us (21%)
  local copies, waits for them, and re-layouts  29 us (15%)
  between operations  3.6 us (2%)
  other arithmetic  2.59 us (1%)
    ppermute x33, starting transfers between devices, trade(): return lax.ppermute(array, 'mp', [(n, n ^ number) for n in range(mp_count)])  44 us
    ppermute x33, waiting for transfers between devices, trade(): return lax.ppermute(array, 'mp', [(n, n ^ number) for n in range(mp_count)])  29.5 us
    unnamed x172, local copies, waits for them, and re-layouts  23.2 us
    ppermute x12, starting transfers between devices, hop(): return lax.ppermute(array, 'dp', pairs)  21.5 us
    pallas_call x8, Pallas kernels, base_products(): pl.pallas_call(base_kernel, grid_spec=pltpu.PrefetchScalarGridSpec(num_sc...  21.2 us
    ppermute x12, waiting for transfers between devices, hop(): return lax.ppermute(array, 'dp', pairs)  20 us
    pallas_call x8, Pallas kernels, finish(): pl.pallas_call(functools.partial(finish_kernel, len(parts)), in_specs=[pl...  11.6 us
    pallas_call x1, Pallas kernels, low_sums(): pl.pallas_call(functools.partial(low_kernel, mp_count, adapters), grid_sp...  7.34 us
  transfers between devices with their start and end apart: 59, of which 8 were waited for; matrix products, arithmetic and copies ran while one was open for 3% of the time, Pallas kernels for 21%

profile of v1, /device:TPU:0, one launch (start us, length us, event | category | flops | bytes accessed | tf_op | source)
XLA Modules:
  0.0 194.6 jit_solution(16644831250514602228)
XLA Ops:
  2.9 2.6 %fusion = (bf16[2048,128]{1,0:T(8,128)(2,1)}, bf16[2048,128]{1,0:T(8,128)(2,1)}, bf16[2048,128]{1,0:T(8,128)(2,1)}) fusion(bf16[8192,256]{1,0:T(8,128)(2,1)} %down_ref.1, s32[]{:T(128)S(6)} %select_n.169, s32[]{:T(128)S(6)} %select_n.167, s32[]{:T(128)S(6)} %select_n.168, s32[]{:T(128)S(6)} %select_n.166), kind=kLoop, calls=%fused_computation.16 | loop fusion | bytes 3145744 | tf_op jit(solution)/shard_map/dynamic_slice | solution.py:293
  5.5 2.9 %collective-permute-start = (bf16[2048,128]{1,0:T(8,128)(2,1)}, bf16[2048,128]{1,0:T(8,128)(2,1)}, u32[]{:S(2)}, u32[]{:S(2)}) collective-permute-start(bf16[2048,128]{1,0:T(8,128)(2,1)} %get-tuple-element.79), channel_id=1, source_target_pairs={{0,1},{1,0},{2,3},{3,2},{4,5},{5,4},{6,7},{7,6},{8,9},{9,8},{10,11... | collective-permute-start | bytes 1572872 | tf_op jit(solution)/shard_map/ppermute | solution.py:273
  9.5 2.0 %collective-permute-start.11 = (bf16[128,1024]{1,0:T(8,128)(2,1)S(1)}, bf16[128,1024]{1,0:T(8,128)(2,1)S(1)}, u32[]{:S(2)}, u32[]{:S(2)}) collective-permute-start(bf16[128,1024]{1,0:T(8,128)(2,1)S(1)} %dynamic-slice_bitcast_fusion), channel_id=1, source_target_pairs={{0,2},{1,3},{2,0},{3,1},{4,6},{5,7},{6,4},{7,5},{8,10},{9,11},{10,... | collective-permute-start | bytes 786440 | tf_op jit(solution)/shard_map/ppermute | solution.py:273
  14.5 12.5 %collective-permute-done.9.rest_4_ = bf16[128,1024]{1,0:T(8,128)(2,1)S(1)} collective-permute-done((bf16[128,1024]{1,0:T(8,128)(2,1)S(1)}, bf16[128,1024]{1,0:T(8,128)(2,1)S(1)}, u32[]{:S(2)}, u32[]{:S(2)}) %collective-permute-start.9) | collective-permute-done | bytes 262176 | tf_op jit(solution)/shard_map/ppermute | solution.py:273
  27.0 3.0 %collective-permute-start.4 = (bf16[2048,128]{1,0:T(8,128)(2,1)}, bf16[2048,128]{1,0:T(8,128)(2,1)}, u32[]{:S(2)}, u32[]{:S(2)}) collective-permute-start(bf16[2048,128]{1,0:T(8,128)(2,1)} %get-tuple-element.77), channel_id=1, source_target_pairs={{0,3},{1,2},{2,1},{3,0},{4,7},{5,6},{6,5},{7,4},{8,11},{9,10},{10,... | collective-permute-start | bytes 1572872 | tf_op jit(solution)/shard_map/ppermute | solution.py:273
  30.0 4.2 %collective-permute-done.13.rest_8_ = bf16[128,1024]{1,0:T(8,128)(2,1)S(1)} collective-permute-done((bf16[128,1024]{1,0:T(8,128)(2,1)S(1)}, bf16[128,1024]{1,0:T(8,128)(2,1)S(1)}, u32[]{:S(2)}, u32[]{:S(2)}) %collective-permute-start.13) | collective-permute-done | bytes 262176 | tf_op jit(solution)/shard_map/ppermute | solution.py:273
  36.0 9.5 %collective-permute-done.2.rest_2_ = bf16[2048,128]{1,0:T(8,128)(2,1)} collective-permute-done((bf16[2048,128]{1,0:T(8,128)(2,1)}, bf16[2048,128]{1,0:T(8,128)(2,1)}, u32[]{:S(2)}, u32[]{:S(2)}) %collective-permute-start.2) | collective-permute-done | bytes 524320 | tf_op jit(solution)/shard_map/ppermute | solution.py:273
  48.7 5.4 %collective-permute-start.28 = (bf16[2048,128]{1,0:T(8,128)(2,1)S(1)}, bf16[2048,128]{1,0:T(8,128)(2,1)}, u32[]{:S(2)}, u32[]{:S(2)}) collective-permute-start(bf16[2048,128]{1,0:T(8,128)(2,1)S(1)} %get-tuple-element.86.mine_ref), channel_id=1, source_target_pairs={{0,8},{4,12},{8,16},{12,20},{16,24},{20,28},{1,9},{5,13},{9,17},{1... | collective-permute-start | bytes 1572872 | tf_op jit(solution)/shard_map/ppermute | solution.py:283
  57.7 4.6 %collective-permute-start.18 = (bf16[2048,128]{1,0:T(8,128)(2,1)S(1)}, bf16[2048,128]{1,0:T(8,128)(2,1)S(1)}, u32[]{:S(2)}, u32[]{:S(2)}) collective-permute-start(bf16[2048,128]{1,0:T(8,128)(2,1)S(1)} %get-tuple-element.87.mine_ref), channel_id=1, source_target_pairs={{0,8},{4,12},{8,16},{12,20},{16,24},{20,28},{1,9},{5,13},{9,17},{1... | collective-permute-start | bytes 1572872 | tf_op jit(solution)/shard_map/ppermute | solution.py:283
  66.9 7.7 %collective-permute-done.15 = bf16[2048,128]{1,0:T(8,128)(2,1)S(1)} collective-permute-done((bf16[2048,128]{1,0:T(8,128)(2,1)S(1)}, bf16[2048,128]{1,0:T(8,128)(2,1)S(1)}, u32[]{:S(2)}, u32[]{:S(2)}) %collective-permute-start.15) | collective-permute-done | bytes 524320 | tf_op jit(solution)/shard_map/ppermute | solution.py:283
  79.3 6.1 %collective-permute-done.26 = bf16[2048,128]{1,0:T(8,128)(2,1)} collective-permute-done((bf16[2048,128]{1,0:T(8,128)(2,1)}, bf16[2048,128]{1,0:T(8,128)(2,1)}, u32[]{:S(2)}, u32[]{:S(2)}) %collective-permute-start.26) | collective-permute-done | bytes 524320 | tf_op jit(solution)/shard_map/ppermute | solution.py:283
  89.6 2.4 %shard_map.64 = (f32[192,256]{1,0:T(8,128)S(1)}, bf16[192,256]{1,0:T(8,128)(2,1)S(1)}, bf16[192,256]{1,0:T(8,128)(2,1)S(1)}, bf16[192,256]{1,0:T(8,128)(2,1)S(1)}) custom-call(s32[4]{0:T(128)S(1)} %iota_xor_fusion.peers_ref, bf16[768,2048]{1,0:T(8,128)(2,1)S(1)} %copy-done, bf16[2048,128]{1,0:T(8,128)(2,1)S(1)} %copy-done.6, bf16[2048,128]{1,0:T(8,128)(2,1)S(1)} %copy-done.10), custom_call_target="tpu_custom_call" | custom-call | flops 805306368 | bytes 4194304 | tf_op jit(solution)/shard_map/pallas_call | solution.py:49
  93.1 2.4 %shard_map.63 = (f32[192,256]{1,0:T(8,128)S(1)}, bf16[192,256]{1,0:T(8,128)(2,1)S(1)}, bf16[192,256]{1,0:T(8,128)(2,1)S(1)}, bf16[192,256]{1,0:T(8,128)(2,1)S(1)}) custom-call(s32[4]{0:T(128)S(1)} %iota_xor_fusion.peers_ref, bf16[768,2048]{1,0:T(8,128)(2,1)S(1)} %copy-done, bf16[2048,128]{1,0:T(8,128)(2,1)S(1)} %copy-done.4, bf16[2048,128]{1,0:T(8,128)(2,1)S(1)} %copy-done.12), custom_call_target="tpu_custom_call" | custom-call | flops 805306368 | bytes 4194304 | tf_op jit(solution)/shard_map/pallas_call | solution.py:49
  95.5 1.9 collective-permute-start.56
  97.4 7.3 %shard_map.55 = (f32[192,128]{1,0:T(8,128)S(1)}, f32[192,128]{1,0:T(8,128)S(1)}, f32[192,128]{1,0:T(8,128)S(1)}, f32[192,128]{1,0:T(8,128)S(1)}) custom-call(s32[4]{0:T(128)S(1)} %iota_xor_fusion.peers_ref, s32[1]{0:T(128)} %bitcast.2.core_ref, bf16[768,2048]{1,0:T(8,128)(2,1)S(1)} %copy-done, s32[768,1]{1,0:T(8,128)S(1)} %reshape.19.ids_ref, ...), custom_call_target="tpu_custom_call" | custom-call | flops 3221225472 | bytes 7340032 | tf_op jit(solution)/shard_map/pallas_call | solution.py:117
  110.5 1.8 broadcast_select_fusion
  117.8 5.0 %collective-permute-done.17 = bf16[2048,128]{1,0:T(8,128)(2,1)S(1)} collective-permute-done((bf16[2048,128]{1,0:T(8,128)(2,1)S(1)}, bf16[2048,128]{1,0:T(8,128)(2,1)S(1)}, u32[]{:S(2)}, u32[]{:S(2)}) %collective-permute-start.17) | collective-permute-done | bytes 524320 | tf_op jit(solution)/shard_map/ppermute | solution.py:283
  128.2 3.2 %collective-permute-done.8.rest_3_ = f32[192,128]{1,0:T(8,128)S(1)} collective-permute-done((f32[192,128]{1,0:T(8,128)S(1)}, f32[192,128]{1,0:T(8,128)S(1)}, u32[]{:S(2)}, u32[]{:S(2)}) %collective-permute-start.8) | collective-permute-done | bytes 98336 | tf_op jit(solution)/shard_map/ppermute | solution.py:273
  132.8 2.4 %shard_map.62 = (f32[192,256]{1,0:T(8,128)S(1)}, bf16[192,256]{1,0:T(8,128)(2,1)S(1)}, bf16[192,256]{1,0:T(8,128)(2,1)S(1)}, bf16[192,256]{1,0:T(8,128)(2,1)S(1)}) custom-call(s32[4]{0:T(128)S(1)} %iota_xor_fusion.peers_ref, bf16[768,2048]{1,0:T(8,128)(2,1)S(1)} %copy-done, bf16[2048,128]{1,0:T(8,128)(2,1)S(1)} %get-tuple-element.80.mine_ref, ...), custom_call_target="tpu_custom_call" | custom-call | flops 805306368 | bytes 4194304 | tf_op jit(solution)/shard_map/pallas_call | solution.py:49
  139.4 2.4 %shard_map.61 = (f32[192,256]{1,0:T(8,128)S(1)}, bf16[192,256]{1,0:T(8,128)(2,1)S(1)}, bf16[192,256]{1,0:T(8,128)(2,1)S(1)}, bf16[192,256]{1,0:T(8,128)(2,1)S(1)}) custom-call(s32[4]{0:T(128)S(1)} %iota_xor_fusion.peers_ref, bf16[768,2048]{1,0:T(8,128)(2,1)S(1)} %copy-done, bf16[2048,128]{1,0:T(8,128)(2,1)S(1)} %get-tuple-element.83.mine_ref, ...), custom_call_target="tpu_custom_call" | custom-call | flops 805306368 | bytes 4194304 | tf_op jit(solution)/shard_map/pallas_call | solution.py:49
  141.8 3.0 %shard_map.60 = (f32[192,256]{1,0:T(8,128)S(1)}, bf16[192,256]{1,0:T(8,128)(2,1)S(1)}, bf16[192,256]{1,0:T(8,128)(2,1)S(1)}, bf16[192,256]{1,0:T(8,128)(2,1)}) custom-call(s32[4]{0:T(128)S(1)} %iota_xor_fusion.peers_ref, bf16[768,2048]{1,0:T(8,128)(2,1)S(1)} %copy-done, bf16[2048,128]{1,0:T(8,128)(2,1)S(1)} %get-tuple-element.81.mine_ref, ...), custom_call_target="tpu_custom_call" | custom-call | flops 805306368 | bytes 4194304 | tf_op jit(solution)/shard_map/pallas_call | solution.py:49
  152.4 3.1 %shard_map.59 = (f32[192,256]{1,0:T(8,128)S(1)}, bf16[192,256]{1,0:T(8,128)(2,1)}, bf16[192,256]{1,0:T(8,128)(2,1)}, bf16[192,256]{1,0:T(8,128)(2,1)}) custom-call(s32[4]{0:T(128)S(1)} %iota_xor_fusion.peers_ref, bf16[768,2048]{1,0:T(8,128)(2,1)S(1)} %copy-done, bf16[2048,128]{1,0:T(8,128)(2,1)S(1)} %get-tuple-element.84.mine_ref, ...), custom_call_target="tpu_custom_call" | custom-call | flops 805306368 | bytes 4194304 | tf_op jit(solution)/shard_map/pallas_call | solution.py:49
  155.5 3.0 %shard_map.58 = (f32[192,256]{1,0:T(8,128)S(1)}, bf16[192,256]{1,0:T(8,128)(2,1)}, bf16[192,256]{1,0:T(8,128)(2,1)S(1)}, bf16[192,256]{1,0:T(8,128)(2,1)S(1)}) custom-call(s32[4]{0:T(128)S(1)} %iota_xor_fusion.peers_ref, bf16[768,2048]{1,0:T(8,128)(2,1)S(1)} %copy-done, bf16[2048,128]{1,0:T(8,128)(2,1)S(1)} %get-tuple-element.82.mine_ref, ...), custom_call_target="tpu_custom_call" | custom-call | flops 805306368 | bytes 4194304 | tf_op jit(solution)/shard_map/pallas_call | solution.py:49
  172.8 2.4 %shard_map.57 = (f32[192,256]{1,0:T(8,128)S(1)}, bf16[192,256]{1,0:T(8,128)(2,1)S(1)}, bf16[192,256]{1,0:T(8,128)(2,1)S(1)}, bf16[192,256]{1,0:T(8,128)(2,1)S(1)}) custom-call(s32[4]{0:T(128)S(1)} %iota_xor_fusion.peers_ref, bf16[768,2048]{1,0:T(8,128)(2,1)S(1)} %copy-done, bf16[2048,128]{1,0:T(8,128)(2,1)S(1)} %copy-done.2, bf16[2048,128]{1,0:T(8,128)(2,1)S(1)} %copy-done.14), custom_call_target="tpu_custom_call" | custom-call | flops 805306368 | bytes 4194304 | tf_op jit(solution)/shard_map/pallas_call | solution.py:49
  (302 shorter events, 90.1 us)
Async XLA Ops:
  5.5 28.8 %collective-permute-start = (bf16[2048,128]{1,0:T(8,128)(2,1)}, bf16[2048,128]{1,0:T(8,128)(2,1)}, u32[]{:S(2)}, u32[]{:S(2)}) collective-permute-start(bf16[2048,128]{1,0:T(8,128)(2,1)} %get-tuple-element.79), channel_id=1, source_target_pairs={{0,1},{1,0},{2,3},{3,2},{4,5},{5,4},{6,7},{7,6},{8,9},{9,8},{10,11... | collective-permute-start | bytes 1572872 | tf_op jit(solution)/shard_map/ppermute | solution.py:273
  9.4 17.6 %collective-permute-start.9 = (bf16[128,1024]{1,0:T(8,128)(2,1)S(1)}, bf16[128,1024]{1,0:T(8,128)(2,1)S(1)}, u32[]{:S(2)}, u32[]{:S(2)}) collective-permute-start(bf16[128,1024]{1,0:T(8,128)(2,1)S(1)} %dynamic-slice_bitcast_fusion), channel_id=1, source_target_pairs={{0,1},{1,0},{2,3},{3,2},{4,5},{5,4},{6,7},{7,6},{8,9},{9,8},{10,11... | collective-permute-start | bytes 786440 | tf_op jit(solution)/shard_map/ppermute | solution.py:273
  9.5 20.6 %collective-permute-start.11 = (bf16[128,1024]{1,0:T(8,128)(2,1)S(1)}, bf16[128,1024]{1,0:T(8,128)(2,1)S(1)}, u32[]{:S(2)}, u32[]{:S(2)}) collective-permute-start(bf16[128,1024]{1,0:T(8,128)(2,1)S(1)} %dynamic-slice_bitcast_fusion), channel_id=1, source_target_pairs={{0,2},{1,3},{2,0},{3,1},{4,6},{5,7},{6,4},{7,5},{8,10},{9,11},{10,... | collective-permute-start | bytes 786440 | tf_op jit(solution)/shard_map/ppermute | solution.py:273
  11.5 22.7 %collective-permute-start.13 = (bf16[128,1024]{1,0:T(8,128)(2,1)S(1)}, bf16[128,1024]{1,0:T(8,128)(2,1)S(1)}, u32[]{:S(2)}, u32[]{:S(2)}) collective-permute-start(bf16[128,1024]{1,0:T(8,128)(2,1)S(1)} %dynamic-slice_bitcast_fusion), channel_id=1, source_target_pairs={{0,3},{1,2},{2,1},{3,0},{4,7},{5,6},{6,5},{7,4},{8,11},{9,10},{10,... | collective-permute-start | bytes 786440 | tf_op jit(solution)/shard_map/ppermute | solution.py:273
  12.9 32.5 %collective-permute-start.2 = (bf16[2048,128]{1,0:T(8,128)(2,1)}, bf16[2048,128]{1,0:T(8,128)(2,1)}, u32[]{:S(2)}, u32[]{:S(2)}) collective-permute-start(bf16[2048,128]{1,0:T(8,128)(2,1)} %get-tuple-element.78), channel_id=1, source_target_pairs={{0,2},{1,3},{2,0},{3,1},{4,6},{5,7},{6,4},{7,5},{8,10},{9,11},{10,... | collective-permute-start | bytes 1572872 | tf_op jit(solution)/shard_map/ppermute | solution.py:273
  27.0 18.5 %collective-permute-start.4 = (bf16[2048,128]{1,0:T(8,128)(2,1)}, bf16[2048,128]{1,0:T(8,128)(2,1)}, u32[]{:S(2)}, u32[]{:S(2)}) collective-permute-start(bf16[2048,128]{1,0:T(8,128)(2,1)} %get-tuple-element.77), channel_id=1, source_target_pairs={{0,3},{1,2},{2,1},{3,0},{4,7},{5,6},{6,5},{7,4},{8,11},{9,10},{10,... | collective-permute-start | bytes 1572872 | tf_op jit(solution)/shard_map/ppermute | solution.py:273
  30.0 16.0 %collective-permute-start.10 = (bf16[128,1024]{1,0:T(8,128)(2,1)S(1)}, bf16[128,1024]{1,0:T(8,128)(2,1)S(1)}, u32[]{:S(2)}, u32[]{:S(2)}) collective-permute-start(bf16[128,1024]{1,0:T(8,128)(2,1)S(1)} %collective-permute-done.9.rest_4_), channel_id=1, source_target_pairs={{0,4},{4,0},{8,12},{12,8},{16,20},{20,16},{24,28},{28,24},{1,5},{5... | collective-permute-start | bytes 786440 | tf_op jit(solution)/shard_map/ppermute | solution.py:270
  34.2 20.7 %collective-permute-start.14 = (bf16[128,1024]{1,0:T(8,128)(2,1)S(1)}, bf16[128,1024]{1,0:T(8,128)(2,1)S(1)}, u32[]{:S(2)}, u32[]{:S(2)}) collective-permute-start(bf16[128,1024]{1,0:T(8,128)(2,1)S(1)} %collective-permute-done.13.rest_8_), channel_id=1, source_target_pairs={{0,4},{4,0},{8,12},{12,8},{16,20},{20,16},{24,28},{28,24},{1,5},{5... | collective-permute-start | bytes 786440 | tf_op jit(solution)/shard_map/ppermute | solution.py:270
  45.5 17.7 %collective-permute-start.51 = (bf16[2048,128]{1,0:T(8,128)(2,1)S(1)}, bf16[2048,128]{1,0:T(8,128)(2,1)S(1)}, u32[]{:S(2)}, u32[]{:S(2)}) collective-permute-start(bf16[2048,128]{1,0:T(8,128)(2,1)S(1)} %get-tuple-element.87.mine_ref), channel_id=1, source_target_pairs={{0,4},{4,0},{8,12},{12,8},{16,20},{20,16},{24,28},{28,24},{1,5},{5... | collective-permute-start | bytes 1572872 | tf_op jit(solution)/shard_map/ppermute | solution.py:270
  46.7 17.3 %collective-permute-start.25 = (bf16[2048,128]{1,0:T(8,128)(2,1)S(1)}, bf16[2048,128]{1,0:T(8,128)(2,1)}, u32[]{:S(2)}, u32[]{:S(2)}) collective-permute-start(bf16[2048,128]{1,0:T(8,128)(2,1)S(1)} %get-tuple-element.86.mine_ref), channel_id=1, source_target_pairs={{8,0},{12,4},{16,8},{20,12},{24,16},{28,20},{9,1},{13,5},{17,9},{2... | collective-permute-start | bytes 1572872 | tf_op jit(solution)/shard_map/ppermute | solution.py:283
  48.7 16.9 %collective-permute-start.28 = (bf16[2048,128]{1,0:T(8,128)(2,1)S(1)}, bf16[2048,128]{1,0:T(8,128)(2,1)}, u32[]{:S(2)}, u32[]{:S(2)}) collective-permute-start(bf16[2048,128]{1,0:T(8,128)(2,1)S(1)} %get-tuple-element.86.mine_ref), channel_id=1, source_target_pairs={{0,8},{4,12},{8,16},{12,20},{16,24},{20,28},{1,9},{5,13},{9,17},{1... | collective-permute-start | bytes 1572872 | tf_op jit(solution)/shard_map/ppermute | solution.py:283
  55.6 19.0 %collective-permute-start.15 = (bf16[2048,128]{1,0:T(8,128)(2,1)S(1)}, bf16[2048,128]{1,0:T(8,128)(2,1)S(1)}, u32[]{:S(2)}, u32[]{:S(2)}) collective-permute-start(bf16[2048,128]{1,0:T(8,128)(2,1)S(1)} %get-tuple-element.87.mine_ref), channel_id=1, source_target_pairs={{8,0},{12,4},{16,8},{20,12},{24,16},{28,20},{9,1},{13,5},{17,9},{2... | collective-permute-start | bytes 1572872 | tf_op jit(solution)/shard_map/ppermute | solution.py:283
  57.7 18.4 %collective-permute-start.18 = (bf16[2048,128]{1,0:T(8,128)(2,1)S(1)}, bf16[2048,128]{1,0:T(8,128)(2,1)S(1)}, u32[]{:S(2)}, u32[]{:S(2)}) collective-permute-start(bf16[2048,128]{1,0:T(8,128)(2,1)S(1)} %get-tuple-element.87.mine_ref), channel_id=1, source_target_pairs={{0,8},{4,12},{8,16},{12,20},{16,24},{20,28},{1,9},{5,13},{9,17},{1... | collective-permute-start | bytes 1572872 | tf_op jit(solution)/shard_map/ppermute | solution.py:283
  65.6 19.9 %collective-permute-start.26 = (bf16[2048,128]{1,0:T(8,128)(2,1)}, bf16[2048,128]{1,0:T(8,128)(2,1)}, u32[]{:S(2)}, u32[]{:S(2)}) collective-permute-start(bf16[2048,128]{1,0:T(8,128)(2,1)} %collective-permute-done.25), channel_id=1, source_target_pairs={{8,0},{12,4},{16,8},{20,12},{9,1},{13,5},{17,9},{21,13},{10,2},{14... | collective-permute-start | bytes 1572872 | tf_op jit(solution)/shard_map/ppermute | solution.py:283
  76.9 18.6 %collective-permute-start.5 = (bf16[2048,128]{1,0:T(8,128)(2,1)}, bf16[2048,128]{1,0:T(8,128)(2,1)}, u32[]{:S(2)}, u32[]{:S(2)}) collective-permute-start(bf16[2048,128]{1,0:T(8,128)(2,1)} %collective-permute-done.4.rest_4_), channel_id=1, source_target_pairs={{0,4},{4,0},{8,12},{12,8},{16,20},{20,16},{24,28},{28,24},{1,5},{5... | collective-permute-start | bytes 1572872 | tf_op jit(solution)/shard_map/ppermute | solution.py:270
  77.2 29.2 %collective-permute-start.16 = (bf16[2048,128]{1,0:T(8,128)(2,1)}, bf16[2048,128]{1,0:T(8,128)(2,1)S(1)}, u32[]{:S(2)}, u32[]{:S(2)}) collective-permute-start(bf16[2048,128]{1,0:T(8,128)(2,1)} %copy-done.81), channel_id=1, source_target_pairs={{8,0},{12,4},{16,8},{20,12},{9,1},{13,5},{17,9},{21,13},{10,2},{14... | collective-permute-start | bytes 1572872 | tf_op jit(solution)/shard_map/ppermute | solution.py:283
  78.6 28.0 %collective-permute-start.19 = (bf16[2048,128]{1,0:T(8,128)(2,1)}, bf16[2048,128]{1,0:T(8,128)(2,1)S(1)}, u32[]{:S(2)}, u32[]{:S(2)}) collective-permute-start(bf16[2048,128]{1,0:T(8,128)(2,1)} %copy-done.83), channel_id=1, source_target_pairs={{8,16},{12,20},{16,24},{20,28},{9,17},{13,21},{17,25},{21,29},{10,... | collective-permute-start | bytes 1572872 | tf_op jit(solution)/shard_map/ppermute | solution.py:283
  85.5 22.9 %collective-permute-start.27 = (bf16[2048,128]{1,0:T(8,128)(2,1)}, bf16[2048,128]{1,0:T(8,128)(2,1)S(1)}, u32[]{:S(2)}, u32[]{:S(2)}) collective-permute-start(bf16[2048,128]{1,0:T(8,128)(2,1)} %collective-permute-done.26), channel_id=1, source_target_pairs={{8,0},{12,4},{9,1},{13,5},{10,2},{14,6},{11,3},{15,7}} | collective-permute-start | bytes 1572872 | tf_op jit(solution)/shard_map/ppermute | solution.py:283
  86.8 22.9 %collective-permute-start.30 = (bf16[2048,128]{1,0:T(8,128)(2,1)}, bf16[2048,128]{1,0:T(8,128)(2,1)S(1)}, u32[]{:S(2)}, u32[]{:S(2)}) collective-permute-start(bf16[2048,128]{1,0:T(8,128)(2,1)} %collective-permute-done.29), channel_id=1, source_target_pairs={{16,24},{20,28},{17,25},{21,29},{18,26},{22,30},{19,27},{23,31}} | collective-permute-start | bytes 1572872 | tf_op jit(solution)/shard_map/ppermute | solution.py:283
  146.4 16.2 %collective-permute-start.45 = (bf16[192,256]{1,0:T(8,128)(2,1)S(1)}, bf16[192,256]{1,0:T(8,128)(2,1)S(1)}, u32[]{:S(2)}, u32[]{:S(2)}) collective-permute-start(bf16[192,256]{1,0:T(8,128)(2,1)S(1)} %get-tuple-element.63), channel_id=1, source_target_pairs={{0,2},{1,3},{2,0},{3,1},{4,6},{5,7},{6,4},{7,5},{8,10},{9,11},{10,... | collective-permute-start | bytes 294920 | tf_op jit(solution)/shard_map/ppermute | solution.py:273
  147.6 17.2 %collective-permute-start.46 = (bf16[192,256]{1,0:T(8,128)(2,1)S(1)}, bf16[192,256]{1,0:T(8,128)(2,1)S(1)}, u32[]{:S(2)}, u32[]{:S(2)}) collective-permute-start(bf16[192,256]{1,0:T(8,128)(2,1)S(1)} %get-tuple-element.64), channel_id=1, source_target_pairs={{0,3},{1,2},{2,1},{3,0},{4,7},{5,6},{6,5},{7,4},{8,11},{9,10},{10,... | collective-permute-start | bytes 294920 | tf_op jit(solution)/shard_map/ppermute | solution.py:273
  149.7 16.3 %collective-permute-start.40 = (bf16[192,256]{1,0:T(8,128)(2,1)S(1)}, bf16[192,256]{1,0:T(8,128)(2,1)S(1)}, u32[]{:S(2)}, u32[]{:S(2)}) collective-permute-start(bf16[192,256]{1,0:T(8,128)(2,1)S(1)} %get-tuple-element.58), channel_id=1, source_target_pairs={{0,1},{1,0},{2,3},{3,2},{4,5},{5,4},{6,7},{7,6},{8,9},{9,8},{10,11... | collective-permute-start | bytes 294920 | tf_op jit(solution)/shard_map/ppermute | solution.py:273
  151.8 16.2 %collective-permute-start.41 = (bf16[192,256]{1,0:T(8,128)(2,1)S(1)}, bf16[192,256]{1,0:T(8,128)(2,1)S(1)}, u32[]{:S(2)}, u32[]{:S(2)}) collective-permute-start(bf16[192,256]{1,0:T(8,128)(2,1)S(1)} %get-tuple-element.59), channel_id=1, source_target_pairs={{0,2},{1,3},{2,0},{3,1},{4,6},{5,7},{6,4},{7,5},{8,10},{9,11},{10,... | collective-permute-start | bytes 294920 | tf_op jit(solution)/shard_map/ppermute | solution.py:273
  175.2 16.2 %collective-permute-start.33 = (bf16[192,256]{1,0:T(8,128)(2,1)S(1)}, bf16[192,256]{1,0:T(8,128)(2,1)S(1)}, u32[]{:S(2)}, u32[]{:S(2)}) collective-permute-start(bf16[192,256]{1,0:T(8,128)(2,1)S(1)} %copy-done.80), channel_id=1, source_target_pairs={{0,2},{1,3},{2,0},{3,1},{4,6},{5,7},{6,4},{7,5},{8,10},{9,11},{10,... | collective-permute-start | bytes 294920 | tf_op jit(solution)/shard_map/ppermute | solution.py:273
  (121 other events, 1215.8 us)

commit v2 on v0

v2 whole, which is shorter than its diff:
```python
import functools

import jax
import jax.numpy as jnp
from jax import lax
from jax.experimental import pallas as pl
from jax.experimental.pallas import tpu as pltpu
from jax.sharding import PartitionSpec as P

ADAPTER_SCALE = 2.0
CORES = 2
LANES = 128
VMEM_BYTES = 60 * 1024 * 1024
ANYWHERE = pl.BlockSpec(memory_space=pl.ANY)
WHOLE = pl.BlockSpec(memory_space=pltpu.VMEM)
SCALARS = pl.BlockSpec(memory_space=pltpu.SMEM)


def params():
    return pltpu.CompilerParams(vmem_limit_bytes=VMEM_BYTES)


def cost(flops, bytes_accessed):
    return pl.CostEstimate(flops=flops, bytes_accessed=bytes_accessed, transcendentals=0)


def load_all(pairs, sems):
    copies = [pltpu.make_async_copy(src, dst, sems.at[n]) for n, (src, dst) in enumerate(pairs)]
    for copy in copies:
        copy.start()
    for copy in copies:
        copy.wait()


def base_kernel(mp_count, first, info_ref, tokens_ref, shards_ref, *rest):
    outs, (weight, block, done, own, sems) = rest[:mp_count], rest[mp_count:]
    pairs, _, span = weight.shape
    width = shards_ref.shape[2]
    rows = block.shape[1]
    each = span // width
    loads = []
    for n in range(pairs * each):
        target = weight.at[n // each, :, n % each * width : (n % each + 1) * width]
        loads.append(pltpu.make_async_copy(shards_ref.at[first + n], target, sems.at[n]))
        loads[-1].start()
    order = list(reversed(range(mp_count)))
    copies = []
    for number in order:
        place = pl.ds(pl.multiple_of((info_ref[0] ^ number) * rows, rows), rows)
        copies.append(pltpu.make_async_copy(tokens_ref.at[place, :], block.at[number], sems.at[len(loads) + number]))
        copies[-1].start()
    for load in loads:
        load.wait()
    stores = []
    for number, copy in zip(order, copies):
        copy.wait()
        target = done.at[number] if number else own
        for n in range(pairs):
            product = jnp.dot(block[number], weight[n], preferred_element_type=jnp.float32)
            target[:, n * span : (n + 1) * span] = product.astype(target.dtype)
        stores.append(pltpu.make_async_copy(target, outs[number], sems.at[len(loads) + mp_count + number]))
        stores[-1].start()
    for store in stores:
        store.wait()


def base_products(info, tokens, shards, first, count, mp_count):
    group_rows, features = tokens.shape
    rows, width = group_rows // mp_count, shards.shape[2]
    span = width * count
    wide = min(span, 2 * LANES)
    return pl.pallas_call(
        functools.partial(base_kernel, mp_count, first),
        in_specs=[SCALARS, ANYWHERE, ANYWHERE],
        out_specs=[ANYWHERE] * mp_count,
        scratch_shapes=[
            pltpu.VMEM((span // wide, features, wide), tokens.dtype),
            pltpu.VMEM((mp_count, rows, features), tokens.dtype),
            pltpu.VMEM((mp_count, rows, span), jnp.bfloat16),
            pltpu.VMEM((rows, span), jnp.float32),
            pltpu.SemaphoreType.DMA((count + 2 * mp_count,)),
        ],
        out_shape=[
            jax.ShapeDtypeStruct((rows, span), jnp.bfloat16 if number else jnp.float32) for number in range(mp_count)
        ],
        compiler_params=params(),
        cost_estimate=cost(
            2 * group_rows * features * span, 2 * (group_rows * (features + span) + features * span) + 4 * rows * span
        ),
    )(info, tokens, shards)


def low_kernel(adapters, rank_pair, info_ref, tokens_hbm, ids_ref, mine_hbm, other_hbm, out, tokens_ref, pieces, sems):
    mp_count, half, width = mine_hbm.shape
    mine_ref, other_ref = pieces.at[0], pieces.at[1]
    load_all([(tokens_hbm, tokens_ref), (mine_hbm, mine_ref), (other_hbm, other_ref)], sems)
    core = info_ref[0]
    rows = tokens_ref.shape[0] // mp_count
    lane_adapter = lax.broadcasted_iota(jnp.int32, (rows, width), 1) // rank_pair
    for block in range(mp_count):
        place = slice(block * rows, (block + 1) * rows)
        ids = ids_ref[place, :]
        parts = [
            (tokens_ref[place, pl.ds(pl.multiple_of(part * half, half), half)], ref)
            for part, ref in ((core, mine_ref), (1 - core, other_ref))
        ]
        total = jnp.zeros((rows, width), jnp.float32)
        for number in range(mp_count):
            product = sum(
                jnp.dot(values, ref[number], preferred_element_type=jnp.float32) for values, ref in parts
            )
            total += jnp.where(lane_adapter == ids - number * adapters, product, 0.0)
        while total.shape[1] > LANES:
            fold = total.shape[1] // 2
            total = total[:, :fold] + total[:, fold:]
        shift = total.shape[1] // 2
        while shift >= rank_pair:
            total = total + pltpu.roll(total, shift, 1)
            shift //= 2
        out[block] = total


def low_sums(core, tokens, ids, mine, other, adapters, rank):
    group_rows, features = tokens.shape
    mp_count, _, width = mine.shape
    rows = group_rows // mp_count
    return pl.pallas_call(
        functools.partial(low_kernel, adapters, 2 * rank),
        in_specs=[SCALARS, ANYWHERE, WHOLE, ANYWHERE, ANYWHERE],
        out_specs=WHOLE,
        out_shape=jax.ShapeDtypeStruct((mp_count, rows, min(width, LANES)), jnp.float32),
        scratch_shapes=[
            pltpu.VMEM(tokens.shape, tokens.dtype),
            pltpu.VMEM((CORES, *mine.shape), mine.dtype),
            pltpu.SemaphoreType.DMA((3,)),
        ],
        compiler_params=params(),
        cost_estimate=cost(
            2 * group_rows * features * mp_count * width, 2 * features * (group_rows + mp_count * width)
        ),
    )(core, tokens, ids, mine, other)


def delta_kernel(adapters, rank, info_ref, ids_ref, sums_ref, mine_ref, other_ref, out):
    mp_count, rows, lanes = sums_ref.shape
    core = info_ref[0]
    span = mine_ref.shape[2]
    low = sums_ref[0]
    for number in range(1, mp_count):
        low = low + sums_ref[number]
    ids = ids_ref[...]
    lane_block = lax.broadcasted_iota(jnp.int32, (rows, lanes), 1) // rank
    even = lane_block % 2 == 0
    key_low = jnp.where(even, low, pltpu.roll(low, rank, 1))
    value_low = jnp.where(even, pltpu.roll(low, lanes - rank, 1), low)
    mine_low = jnp.where(core == 0, key_low, value_low)
    other_low = jnp.where(core == 0, value_low, key_low)
    for part, values, weights in ((core, mine_low, mine_ref), (1 - core, other_low, other_ref)):
        total = jnp.zeros((rows, span), jnp.float32)
        for owner in range(mp_count):
            spread = jnp.where(lane_block == ids - owner * adapters, values, 0.0).astype(jnp.bfloat16)
            total += jnp.dot(spread, weights[owner], preferred_element_type=jnp.float32)
        out[:, pl.ds(pl.multiple_of(part * span, span), span)] = (ADAPTER_SCALE * total).astype(out.dtype)


def deltas_of(core, ids, sums, mine, other, adapters, rank):
    mp_count, rows, _ = sums.shape
    span = mine.shape[2]
    return pl.pallas_call(
        functools.partial(delta_kernel, adapters, rank),
        in_specs=[SCALARS] + [WHOLE] * 4,
        out_specs=WHOLE,
        out_shape=jax.ShapeDtypeStruct((rows, 2 * span), jnp.bfloat16),
        compiler_params=params(),
        cost_estimate=cost(4 * rows * mine.size, 4 * mine.size + 4 * sums.size + 4 * rows * span),
    )(core, ids, sums, mine, other)


def finish_kernel(mp_count, columns, delta_hbm, *rest):
    parts, (out, delta, own, others, done, sems) = rest[:mp_count], rest[-6:]
    count, _, width = done.shape
    pairs = [(parts[0], own)] + [(part, others.at[n]) for n, part in enumerate(parts[1:])]
    pairs += [(delta_hbm.at[:, columns[n] : columns[n] + width], delta.at[n]) for n in range(count)]
    load_all(pairs, sems)
    stores = []
    for place in range(count):
        span = slice(place * width, (place + 1) * width)
        total = own[:, span]
        for n in range(mp_count - 1):
            total = total + others[n, :, span].astype(jnp.float32)
        done[place] = (total + delta[place].astype(jnp.float32)).astype(done.dtype)
        target = out.at[:, columns[place] : columns[place] + width]
        stores.append(pltpu.make_async_copy(done.at[place], target, sems.at[place]))
        stores[-1].start()
    for store in stores:
        store.wait()


def finish(columns, delta, parts, held):
    rows, span = parts[0].shape
    count, mp_count = len(columns), len(parts)
    width = span // count
    operands = [delta, *parts] + ([] if held is None else [held])
    return pl.pallas_call(
        functools.partial(finish_kernel, mp_count, columns),
        in_specs=[ANYWHERE] * len(operands),
        out_specs=ANYWHERE,
        out_shape=jax.ShapeDtypeStruct(delta.shape, delta.dtype),
        scratch_shapes=[
            pltpu.VMEM((count, rows, width), delta.dtype),
            pltpu.VMEM((rows, span), jnp.float32),
            pltpu.VMEM((mp_count - 1, rows, span), delta.dtype),
            pltpu.VMEM((count, rows, width), delta.dtype),
            pltpu.SemaphoreType.DMA((mp_count + count,)),
        ],
        input_output_aliases={} if held is None else {len(operands) - 1: 0},
        compiler_params=params(),
        cost_estimate=cost(4 * rows * span, 12 * rows * span),
    )(*operands)


def local(tokens, frozen_weight, adapter_down_weight, adapter_up_weight, token_adapter_index):
    mp_count, dp_count = lax.axis_size("mp"), lax.axis_size("dp")
    position, replica = lax.axis_index("mp"), lax.axis_index("dp")
    planes = dp_count // CORES
    plane, core = replica // CORES, replica % CORES
    group_rows, features = tokens.shape
    rows = group_rows // mp_count
    width = frozen_weight.shape[1]
    adapters, rank, up_span = adapter_up_weight.shape[1:]
    core_of = core.astype(jnp.int32).reshape(1)

    def info_of(*values):
        return jnp.stack([jnp.asarray(value, jnp.int32) for value in values])

    def after(array, *others):
        return lax.optimization_barrier((array, *others))[0]

    def after_all(*arrays):
        return lax.optimization_barrier(arrays)

    def swap(array):
        return lax.ppermute(array, "dp", [(n, n ^ 1) for n in range(dp_count)])

    def trade(array):
        return lax.all_to_all(array, "mp", 0, 0)

    def pass_round(blocks):
        return [
            lax.ppermute(block, "mp", [(m, m ^ n) for m in range(mp_count)]) for n, block in enumerate(blocks, 1)
        ]

    chunk = min(width, LANES)
    gathered = [
        lax.all_gather(frozen_weight[:, n * chunk : (n + 1) * chunk], "dp") for n in range(width // chunk)
    ]

    down_halves = adapter_down_weight.reshape(mp_count, CORES, features // CORES, -1)
    down_mine = trade(lax.dynamic_index_in_dim(down_halves, core, 1, keepdims=False))
    up_flat = adapter_up_weight.reshape(2, adapters * rank, up_span)
    up_half = lax.dynamic_index_in_dim(up_flat, core, 0, keepdims=False)
    ids = token_adapter_index.reshape(group_rows, 1)
    own_ids = lax.dynamic_slice_in_dim(ids, position * rows, rows)
    down_other = swap(down_mine)
    sums = trade(low_sums(core_of, tokens, ids, down_mine, down_other, adapters, rank))
    up_mine = trade(jnp.broadcast_to(up_half, (mp_count, *up_half.shape)))
    up_other = swap(up_mine)
    delta = deltas_of(core_of, own_ids, sums, up_mine, up_other, adapters, rank)

    out = None
    pieces = 2
    count = dp_count // pieces
    info = info_of(position)
    for n, shards in enumerate(gathered):
        finished = []
        if out is not None:
            shards, out = after_all(shards, out)
        for piece in range(pieces):
            own, *sent = base_products(info, tokens, shards, piece * count, count, mp_count)
            columns = [(piece * count + m) * width + n * chunk for m in range(count)]
            finished.append((columns, [own] + pass_round(sent)))
        for columns, parts in finished:
            out = finish(columns, delta, parts, out)
    return out


def solution(mesh):
    placed = (P("dp", "mp"), P("mp", "dp"), P(None, "mp"), P(None, "mp", None, None), P("dp"))
    return jax.shard_map(
        local, mesh=mesh, in_specs=placed, out_specs=P(("dp", "mp"), None), check_vma=False
    )
```

time: 299 us -> 145 us (0.48)
  waiting for transfers between devices: 186 us -> 15.4 us
  blocking collectives: 0 us -> 48 us
  local copies, waits for them, and re-layouts: 51.1 us -> 9.01 us
  Pallas kernels: 0 us -> 40.1 us
  matrix products: 18.8 us -> 0 us
  other arithmetic: 15.9 us -> 0 us
  starting transfers between devices: 13 us -> 18.6 us
    all_to_all x3 -> x1, waiting for transfers between devices: 104 us -> 0.01 us  [trade(): return lax.all_to_all(array, 'mp', 0, 0)]
    all_gather x1 -> x2, waiting for transfers between devices: 80.9 us -> 0.98 us  [local(): lax.all_gather(frozen_weight[:, n * chunk:(n + 1) * chunk], 'dp')]
    all_to_all x0 -> x2, blocking collectives: none -> 48 us  [trade(): return lax.all_to_all(array, 'mp', 0, 0)]
    pallas_call x0 -> x10, Pallas kernels: none -> 40.1 us  [the longest x4 19.9 us: base_products(): pl.pallas_call(functools.partial(base_kernel, mp_count, first), in_specs=...]
    dot_general x4 -> x0, matrix products: 18.8 us -> none  [the longest x1 11.7 us: local(): jnp.dot(tokens, weight_full, preferred_element_type=jnp.float32)]
    ppermute x0 -> x14, starting transfers between devices: none -> 14.9 us  [the longest x12 14.9 us: pass_round(): lax.ppermute(block, 'mp', [(m, m ^ n) for m in range(mp_count)])]
    ppermute x0 -> x14, waiting for transfers between devices: none -> 13.7 us  [the longest x12 13.7 us: pass_round(): lax.ppermute(block, 'mp', [(m, m ^ n) for m in range(mp_count)])]
    gather x2 -> x0, local copies, waits for them, and re-layouts: 11.8 us -> none  [the longest x1 7.15 us: local(): jnp.take(padded, slot_token, axis=0)]
  transfers between devices with their start and end apart: 5 -> 17, of which waited for: 3 -> 6; matrix products, arithmetic and copies ran while one was open for 24% -> 3% of each run, Pallas kernels for 0% -> 23%
where the time goes in v2:
time: 145 us
  blocking collectives  48 us (33%)
  Pallas kernels  40.1 us (28%)
  starting transfers between devices  18.6 us (13%)
  waiting for transfers between devices  15.4 us (11%)
  between operations  13.6 us (9%)
  local copies, waits for them, and re-layouts  9.01 us (6%)
    all_to_all x2, blocking collectives, trade(): return lax.all_to_all(array, 'mp', 0, 0)  48 us
    pallas_call x4, Pallas kernels, base_products(): pl.pallas_call(functools.partial(base_kernel, mp_count, first), in_specs=...  19.9 us
    ppermute x12, starting transfers between devices, pass_round(): lax.ppermute(block, 'mp', [(m, m ^ n) for m in range(mp_count)])  14.9 us
    ppermute x12, waiting for transfers between devices, pass_round(): lax.ppermute(block, 'mp', [(m, m ^ n) for m in range(mp_count)])  13.7 us
    pallas_call x1, Pallas kernels, low_sums(): pl.pallas_call(functools.partial(low_kernel, adapters, 2 * rank), in_spec...  8.54 us
    pallas_call x4, Pallas kernels, finish(): pl.pallas_call(functools.partial(finish_kernel, mp_count, columns), in_sp...  8.04 us
    pallas_call x1, Pallas kernels, deltas_of(): pl.pallas_call(functools.partial(delta_kernel, adapters, rank), in_specs=...  3.66 us
    all_to_all x1, starting transfers between devices, trade(): return lax.all_to_all(array, 'mp', 0, 0)  3.65 us
  transfers between devices with their start and end apart: 17, of which 6 were waited for; matrix products, arithmetic and copies ran while one was open for 3% of the time, Pallas kernels for 23%

profile of v2, /device:TPU:0, one launch (start us, length us, event | category | flops | bytes accessed | tf_op | source)
XLA Modules:
  0.0 144.7 jit_solution(12575020652471474115)
XLA Ops:
  6.5 2.3 %fusion = (bf16[2048,128]{1,0:T(8,128)(2,1)}, bf16[2048,128]{1,0:T(8,128)(2,1)}) fusion(bf16[2048,256]{1,0:T(8,128)(2,1)} %param.6), kind=kLoop, calls=%fused_computation.2 | loop fusion | bytes 2097152 | tf_op jit(solution)/shard_map/slice | solution.py:255
  9.6 1.7 %dynamic-slice_bitcast_fusion = bf16[4,1024,256]{2,1,0:T(8,128)(2,1)S(1)} fusion(bf16[4,2,1024,256]{3,2,1,0:T(8,128)(2,1)} %bitcast.18, s32[]{:T(128)S(6)} %select_n.18), kind=kLoop, calls=%fused_computation | loop fusion | bytes 4194308 | tf_op jit(solution)/shard_map/jit(dynamic_index_in_dim)/squeeze | solution.py:259
  11.4 30.4 %all_to_all.15.mine_hbm = bf16[4,1024,256]{2,1,0:T(8,128)(2,1)} all-to-all(bf16[4,1024,256]{2,1,0:T(8,128)(2,1)S(1)} %dynamic-slice_bitcast_fusion), channel_id=1, replica_groups=mesh['dp'=8,'mp'=4] {'mp'}, dimensions={0} | all-to-all | bytes 4194304 | tf_op jit(solution)/shard_map/all_to_all | solution.py:246
  42.0 17.5 %all_to_all.16.mine_ref = bf16[4,128,1024]{2,1,0:T(8,128)(2,1)S(1)} all-to-all(bf16[4,128,1024]{2,1,0:T(8,128)(2,1)S(1)} %broadcast_in_dim.3), channel_id=1, replica_groups=mesh['dp'=8,'mp'=4] {'mp'}, dimensions={0} | all-to-all | bytes 2097152 | tf_op jit(solution)/shard_map/all_to_all | solution.py:246
  60.6 5.0 %shard_map.58 = (f32[192,512]{1,0:T(8,128)}, bf16[192,512]{1,0:T(8,128)(2,1)}, bf16[192,512]{1,0:T(8,128)(2,1)}, bf16[192,512]{1,0:T(8,128)(2,1)}) custom-call(s32[1]{0:T(128)} %bitcast.6.info_ref, bf16[768,2048]{1,0:T(8,128)(2,1)} %tokens_ref.7, bf16[8,2048,128]{2,1,0:T(8,128)(2,1)} %bitcast.16), custom_call_target="tpu_custom_call" | custom-call | flops 1610612736 | bytes 6422528 | tf_op jit(solution)/shard_map/pallas_call | solution.py:72
  66.6 8.5 %shard_map.55 = f32[4,192,128]{2,1,0:T(8,128)} custom-call(s32[1]{0:T(128)} %bitcast.info_ref, bf16[768,2048]{1,0:T(8,128)(2,1)} %tokens_ref.7, s32[768,1]{1,0:T(8,128)} %reshape.19.ids_ref, bf16[4,1024,256]{2,1,0:T(8,128)(2,1)} %all_to_all.15.mine_hbm, bf16[4,1024,256]{2,1,0:T(8,128)(2,1)} %collective-permute-done.other_hbm), custom_call_target="tpu_custom_call" | custom-call | flops 3221225472 | bytes 7340032 | tf_op jit(solution)/shard_map/pallas_call | solution.py:127
  75.1 3.7 %all-to-all-start.1 = ((f32[4,192,128]{2,1,0:T(8,128)}), f32[4,192,128]{2,1,0:T(8,128)S(1)}, u32[]{:S(2)}, u32[]{:S(2)}) async-start(f32[4,192,128]{2,1,0:T(8,128)} %shard_map.55), calls=%async_computation.1 | async-start | bytes 786432 | tf_op jit(solution)/shard_map/all_to_all | solution.py:246
  78.8 1.8 %collective-permute-start.6 = (bf16[192,512]{1,0:T(8,128)(2,1)}, bf16[192,512]{1,0:T(8,128)(2,1)}, u32[]{:S(2)}, u32[]{:S(2)}) collective-permute-start(bf16[192,512]{1,0:T(8,128)(2,1)} %get-tuple-element.29), channel_id=1, source_target_pairs={{0,2},{1,3},{2,0},{3,1},{4,6},{5,7},{6,4},{7,5},{8,10},{9,11},{10,... | collective-permute-start | bytes 589832 | tf_op jit(solution)/shard_map/ppermute | solution.py:250
  82.0 5.0 %shard_map.57 = (f32[192,512]{1,0:T(8,128)}, bf16[192,512]{1,0:T(8,128)(2,1)}, bf16[192,512]{1,0:T(8,128)(2,1)}, bf16[192,512]{1,0:T(8,128)(2,1)}) custom-call(s32[1]{0:T(128)} %bitcast.6.info_ref, bf16[768,2048]{1,0:T(8,128)(2,1)} %tokens_ref.7, bf16[8,2048,128]{2,1,0:T(8,128)(2,1)} %bitcast.17), custom_call_target="tpu_custom_call" | custom-call | flops 1610612736 | bytes 6422528 | tf_op jit(solution)/shard_map/pallas_call | solution.py:72
  87.4 1.7 %collective-permute-start.3 = (bf16[192,512]{1,0:T(8,128)(2,1)}, bf16[192,512]{1,0:T(8,128)(2,1)S(1)}, u32[]{:S(2)}, u32[]{:S(2)}) collective-permute-start(bf16[192,512]{1,0:T(8,128)(2,1)} %get-tuple-element.25), channel_id=1, source_target_pairs={{0,2},{1,3},{2,0},{3,1},{4,6},{5,7},{6,4},{7,5},{8,10},{9,11},{10,... | collective-permute-start | bytes 589832 | tf_op jit(solution)/shard_map/ppermute | solution.py:250
  89.1 1.5 %collective-permute-start.4 = (bf16[192,512]{1,0:T(8,128)(2,1)}, bf16[192,512]{1,0:T(8,128)(2,1)S(1)}, u32[]{:S(2)}, u32[]{:S(2)}) collective-permute-start(bf16[192,512]{1,0:T(8,128)(2,1)} %get-tuple-element.26), channel_id=1, source_target_pairs={{0,3},{1,2},{2,1},{3,0},{4,7},{5,6},{6,5},{7,4},{8,11},{9,10},{10,... | collective-permute-start | bytes 589832 | tf_op jit(solution)/shard_map/ppermute | solution.py:250
  92.2 3.7 %shard_map.56.delta_hbm = bf16[192,2048]{1,0:T(8,128)(2,1)} custom-call(s32[1]{0:T(128)} %bitcast.info_ref, s32[192,1]{1,0:T(8,128)} %copy.12.ids_ref, f32[4,192,128]{2,1,0:T(8,128)} %copy-done.2, bf16[4,128,1024]{2,1,0:T(8,128)(2,1)} %copy-done.1, bf16[4,128,1024]{2,1,0:T(8,128)(2,1)} %copy-done.3), custom_call_target="tpu_custom_call" | custom-call | flops 402653184 | bytes 3276800 | tf_op jit(solution)/shard_map/pallas_call | solution.py:169
  95.9 2.0 %shard_map.59.rest_4_ = bf16[192,2048]{1,0:T(8,128)(2,1)} custom-call(bf16[192,2048]{1,0:T(8,128)(2,1)} %shard_map.56.delta_hbm, f32[192,512]{1,0:T(8,128)} %get-tuple-element.27.rest_0_, bf16[192,512]{1,0:T(8,128)(2,1)} %copy-done.4, bf16[192,512]{1,0:T(8,128)(2,1)} %collective-permute-done.6.rest_2_, bf16[192,512]{1,0:T(8,128)(2,1)} %collective-permute-done.7.rest_3_), custom_call_target="tpu_custom_call" | custom-call | flops 393216 | bytes 1179648 | tf_op jit(solution)/shard_map/pallas_call | solution.py:204
  97.9 4.6 %collective-permute-done.3.rest_2_ = bf16[192,512]{1,0:T(8,128)(2,1)S(1)} collective-permute-done((bf16[192,512]{1,0:T(8,128)(2,1)}, bf16[192,512]{1,0:T(8,128)(2,1)S(1)}, u32[]{:S(2)}, u32[]{:S(2)}) %collective-permute-start.3) | collective-permute-done | bytes 196640 | tf_op jit(solution)/shard_map/ppermute | solution.py:250
  103.3 2.0 %shard_map.60.rest_4_ = bf16[192,2048]{1,0:T(8,128)(2,1)} custom-call(bf16[192,2048]{1,0:T(8,128)(2,1)} %shard_map.56.delta_hbm, f32[192,512]{1,0:T(8,128)} %get-tuple-element.23.rest_0_, bf16[192,512]{1,0:T(8,128)(2,1)} %copy-done.5, bf16[192,512]{1,0:T(8,128)(2,1)} %copy-done.6, bf16[192,512]{1,0:T(8,128)(2,1)} %copy-done.7, ...), custom_call_target="tpu_custom_call", output_to_operand_aliasing={{}: (5, {})} | custom-call | flops 393216 | bytes 1179648 | tf_op jit(solution)/shard_map/pallas_call | solution.py:204
  106.3 4.9 %shard_map.62 = (f32[192,512]{1,0:T(8,128)}, bf16[192,512]{1,0:T(8,128)(2,1)}, bf16[192,512]{1,0:T(8,128)(2,1)}, bf16[192,512]{1,0:T(8,128)(2,1)}) custom-call(s32[1]{0:T(128)} %bitcast.6.info_ref, bf16[768,2048]{1,0:T(8,128)(2,1)} %tokens_ref.7, bf16[8,2048,128]{2,1,0:T(8,128)(2,1)} %bitcast.14), custom_call_target="tpu_custom_call" | custom-call | flops 1610612736 | bytes 6422528 | tf_op jit(solution)/shard_map/pallas_call | solution.py:72
  111.3 1.5 %collective-permute-start.11 = (bf16[192,512]{1,0:T(8,128)(2,1)}, bf16[192,512]{1,0:T(8,128)(2,1)S(1)}, u32[]{:S(2)}, u32[]{:S(2)}) collective-permute-start(bf16[192,512]{1,0:T(8,128)(2,1)} %get-tuple-element.37), channel_id=1, source_target_pairs={{0,1},{1,0},{2,3},{3,2},{4,5},{5,4},{6,7},{7,6},{8,9},{9,8},{10,11... | collective-permute-start | bytes 589832 | tf_op jit(solution)/shard_map/ppermute | solution.py:250
  112.8 1.5 %collective-permute-start.12 = (bf16[192,512]{1,0:T(8,128)(2,1)}, bf16[192,512]{1,0:T(8,128)(2,1)S(1)}, u32[]{:S(2)}, u32[]{:S(2)}) collective-permute-start(bf16[192,512]{1,0:T(8,128)(2,1)} %get-tuple-element.38), channel_id=1, source_target_pairs={{0,2},{1,3},{2,0},{3,1},{4,6},{5,7},{6,4},{7,5},{8,10},{9,11},{10,... | collective-permute-start | bytes 589832 | tf_op jit(solution)/shard_map/ppermute | solution.py:250
  114.3 5.0 %shard_map.61 = (f32[192,512]{1,0:T(8,128)}, bf16[192,512]{1,0:T(8,128)(2,1)}, bf16[192,512]{1,0:T(8,128)(2,1)}, bf16[192,512]{1,0:T(8,128)(2,1)}) custom-call(s32[1]{0:T(128)} %bitcast.6.info_ref, bf16[768,2048]{1,0:T(8,128)(2,1)} %tokens_ref.7, bf16[8,2048,128]{2,1,0:T(8,128)(2,1)} %bitcast.15), custom_call_target="tpu_custom_call" | custom-call | flops 1610612736 | bytes 6422528 | tf_op jit(solution)/shard_map/pallas_call | solution.py:72
  119.9 2.4 %collective-permute-start.10 = (bf16[192,512]{1,0:T(8,128)(2,1)}, bf16[192,512]{1,0:T(8,128)(2,1)S(1)}, u32[]{:S(2)}, u32[]{:S(2)}) collective-permute-start(bf16[192,512]{1,0:T(8,128)(2,1)} %get-tuple-element.35), channel_id=1, source_target_pairs={{0,3},{1,2},{2,1},{3,0},{4,7},{5,6},{6,5},{7,4},{8,11},{9,10},{10,... | collective-permute-start | bytes 589832 | tf_op jit(solution)/shard_map/ppermute | solution.py:250
  123.4 4.8 %collective-permute-done.13.rest_3_ = bf16[192,512]{1,0:T(8,128)(2,1)S(1)} collective-permute-done((bf16[192,512]{1,0:T(8,128)(2,1)S(1)}, bf16[192,512]{1,0:T(8,128)(2,1)S(1)}, u32[]{:S(2)}, u32[]{:S(2)}) %collective-permute-start.13) | collective-permute-done | bytes 196640 | tf_op jit(solution)/shard_map/ppermute | solution.py:250
  128.8 2.0 %shard_map.63.rest_4_ = bf16[192,2048]{1,0:T(8,128)(2,1)} custom-call(bf16[192,2048]{1,0:T(8,128)(2,1)} %shard_map.56.delta_hbm, f32[192,512]{1,0:T(8,128)} %get-tuple-element.36.rest_0_, bf16[192,512]{1,0:T(8,128)(2,1)} %copy-done.8, bf16[192,512]{1,0:T(8,128)(2,1)} %copy-done.10, bf16[192,512]{1,0:T(8,128)(2,1)} %copy-done.13, ...), custom_call_target="tpu_custom_call", output_to_operand_aliasing={{}: (5, {})} | custom-call | flops 393216 | bytes 1179648 | tf_op jit(solution)/shard_map/pallas_call | solution.py:204
  132.3 2.0 %collective-permute-done.8.rest_1_ = bf16[192,512]{1,0:T(8,128)(2,1)S(1)} collective-permute-done((bf16[192,512]{1,0:T(8,128)(2,1)}, bf16[192,512]{1,0:T(8,128)(2,1)S(1)}, u32[]{:S(2)}, u32[]{:S(2)}) %collective-permute-start.8) | collective-permute-done | bytes 196640 | tf_op jit(solution)/shard_map/ppermute | solution.py:250
  135.8 2.0 %shard_map.64 = bf16[192,2048]{1,0:T(8,128)(2,1)} custom-call(bf16[192,2048]{1,0:T(8,128)(2,1)} %shard_map.56.delta_hbm, f32[192,512]{1,0:T(8,128)} %get-tuple-element.32.rest_0_, bf16[192,512]{1,0:T(8,128)(2,1)} %copy-done.11, bf16[192,512]{1,0:T(8,128)(2,1)} %copy-done.12, bf16[192,512]{1,0:T(8,128)(2,1)} %copy-done.9, ...), custom_call_target="tpu_custom_call", output_to_operand_aliasing={{}: (5, {})} | custom-call | flops 393216 | bytes 1179648 | tf_op jit(solution)/shard_map/pallas_call | solution.py:204
  (63 shorter events, 13.6 us)
Async XLA Ops:
  6.5 35.3 %copy-start = (bf16[2,8,16,1024]{3,2,1,0:T(8,128)(2,1)S(1)}, bf16[2,8,16,1024]{3,2,1,0:T(8,128)(2,1)}, u32[]{:S(2)}) copy-start(bf16[2,8,16,1024]{3,2,1,0:T(8,128)(2,1)} %param.8) | copy-start | bytes 1572868
  6.5 54.1 %all-gather.7.cloned.1.call-start = ((), (), s32[]{:S(2)}) async-start(), calls=%async_computation.4 | async-start | bytes 4718592 | tf_op jit(solution)/shard_map/all_gather | solution.py:255
  8.9 97.5 %all-gather.5.cloned.1.call-start = ((), (), s32[]{:S(2)}) async-start(), calls=%async_computation.3 | async-start | bytes 4718592 | tf_op jit(solution)/shard_map/all_gather | solution.py:255
  11.4 48.1 %copy-start.14 = (s32[768]{0:T(1024)S(1)}, s32[768]{0:T(1024)}, u32[]{:S(2)}) copy-start(s32[768]{0:T(1024)} %param.9) | copy-start | bytes 9220
  41.8 24.7 %collective-permute-start = (bf16[4,1024,256]{2,1,0:T(8,128)(2,1)}, bf16[4,1024,256]{2,1,0:T(8,128)(2,1)}, u32[]{:S(2)}, u32[]{:S(2)}) collective-permute-start(bf16[4,1024,256]{2,1,0:T(8,128)(2,1)} %all_to_all.15.mine_hbm), channel_id=1, source_target_pairs={{0,4},{4,0},{8,12},{12,8},{16,20},{20,16},{24,28},{28,24},{1,5},{5... | collective-permute-start | bytes 6291464 | tf_op jit(solution)/shard_map/ppermute | solution.py:243
  59.5 6.1 %copy-start.1 = (bf16[4,128,1024]{2,1,0:T(8,128)(2,1)}, bf16[4,128,1024]{2,1,0:T(8,128)(2,1)S(1)}, u32[]{:S(2)}) copy-start(bf16[4,128,1024]{2,1,0:T(8,128)(2,1)S(1)} %all_to_all.16.mine_ref) | copy-start | bytes 3145732
  59.5 27.9 %collective-permute-start.1 = (bf16[4,128,1024]{2,1,0:T(8,128)(2,1)S(1)}, bf16[4,128,1024]{2,1,0:T(8,128)(2,1)S(1)}, u32[]{:S(2)}, u32[]{:S(2)}) collective-permute-start(bf16[4,128,1024]{2,1,0:T(8,128)(2,1)S(1)} %all_to_all.16.mine_ref), channel_id=1, source_target_pairs={{0,4},{4,0},{8,12},{12,8},{16,20},{20,16},{24,28},{28,24},{1,5},{5... | collective-permute-start | bytes 3145736 | tf_op jit(solution)/shard_map/ppermute | solution.py:243
  65.6 23.6 %collective-permute-start.5 = (bf16[192,512]{1,0:T(8,128)(2,1)}, bf16[192,512]{1,0:T(8,128)(2,1)S(1)}, u32[]{:S(2)}, u32[]{:S(2)}) collective-permute-start(bf16[192,512]{1,0:T(8,128)(2,1)} %get-tuple-element.28), channel_id=1, source_target_pairs={{0,1},{1,0},{2,3},{3,2},{4,5},{5,4},{6,7},{7,6},{8,9},{9,8},{10,11... | collective-permute-start | bytes 589832 | tf_op jit(solution)/shard_map/ppermute | solution.py:250
  75.1 16.4 %all-to-all-start.1 = ((f32[4,192,128]{2,1,0:T(8,128)}), f32[4,192,128]{2,1,0:T(8,128)S(1)}, u32[]{:S(2)}, u32[]{:S(2)}) async-start(f32[4,192,128]{2,1,0:T(8,128)} %shard_map.55), calls=%async_computation.1 | async-start | bytes 786432 | tf_op jit(solution)/shard_map/all_to_all | solution.py:246
  78.8 17.1 %collective-permute-start.6 = (bf16[192,512]{1,0:T(8,128)(2,1)}, bf16[192,512]{1,0:T(8,128)(2,1)}, u32[]{:S(2)}, u32[]{:S(2)}) collective-permute-start(bf16[192,512]{1,0:T(8,128)(2,1)} %get-tuple-element.29), channel_id=1, source_target_pairs={{0,2},{1,3},{2,0},{3,1},{4,6},{5,7},{6,4},{7,5},{8,10},{9,11},{10,... | collective-permute-start | bytes 589832 | tf_op jit(solution)/shard_map/ppermute | solution.py:250
  80.6 15.3 %collective-permute-start.7 = (bf16[192,512]{1,0:T(8,128)(2,1)}, bf16[192,512]{1,0:T(8,128)(2,1)}, u32[]{:S(2)}, u32[]{:S(2)}) collective-permute-start(bf16[192,512]{1,0:T(8,128)(2,1)} %get-tuple-element.30), channel_id=1, source_target_pairs={{0,3},{1,2},{2,1},{3,0},{4,7},{5,6},{6,5},{7,4},{8,11},{9,10},{10,... | collective-permute-start | bytes 589832 | tf_op jit(solution)/shard_map/ppermute | solution.py:250
  87.0 10.9 %collective-permute-start.2 = (bf16[192,512]{1,0:T(8,128)(2,1)}, bf16[192,512]{1,0:T(8,128)(2,1)S(1)}, u32[]{:S(2)}, u32[]{:S(2)}) collective-permute-start(bf16[192,512]{1,0:T(8,128)(2,1)} %get-tuple-element.24), channel_id=1, source_target_pairs={{0,1},{1,0},{2,3},{3,2},{4,5},{5,4},{6,7},{7,6},{8,9},{9,8},{10,11... | collective-permute-start | bytes 589832 | tf_op jit(solution)/shard_map/ppermute | solution.py:250
  87.4 15.1 %collective-permute-start.3 = (bf16[192,512]{1,0:T(8,128)(2,1)}, bf16[192,512]{1,0:T(8,128)(2,1)S(1)}, u32[]{:S(2)}, u32[]{:S(2)}) collective-permute-start(bf16[192,512]{1,0:T(8,128)(2,1)} %get-tuple-element.25), channel_id=1, source_target_pairs={{0,2},{1,3},{2,0},{3,1},{4,6},{5,7},{6,4},{7,5},{8,10},{9,11},{10,... | collective-permute-start | bytes 589832 | tf_op jit(solution)/shard_map/ppermute | solution.py:250
  89.1 6.7 %copy-start.4 = (bf16[192,512]{1,0:T(8,128)(2,1)}, bf16[192,512]{1,0:T(8,128)(2,1)S(1)}, u32[]{:S(2)}) copy-start(bf16[192,512]{1,0:T(8,128)(2,1)S(1)} %collective-permute-done.5.rest_1_) | copy-start | bytes 589828
  89.1 13.4 %collective-permute-start.4 = (bf16[192,512]{1,0:T(8,128)(2,1)}, bf16[192,512]{1,0:T(8,128)(2,1)S(1)}, u32[]{:S(2)}, u32[]{:S(2)}) collective-permute-start(bf16[192,512]{1,0:T(8,128)(2,1)} %get-tuple-element.26), channel_id=1, source_target_pairs={{0,3},{1,2},{2,1},{3,0},{4,7},{5,6},{6,5},{7,4},{8,11},{9,10},{10,... | collective-permute-start | bytes 589832 | tf_op jit(solution)/shard_map/ppermute | solution.py:250
  111.3 11.5 %collective-permute-start.11 = (bf16[192,512]{1,0:T(8,128)(2,1)}, bf16[192,512]{1,0:T(8,128)(2,1)S(1)}, u32[]{:S(2)}, u32[]{:S(2)}) collective-permute-start(bf16[192,512]{1,0:T(8,128)(2,1)} %get-tuple-element.37), channel_id=1, source_target_pairs={{0,1},{1,0},{2,3},{3,2},{4,5},{5,4},{6,7},{7,6},{8,9},{9,8},{10,11... | collective-permute-start | bytes 589832 | tf_op jit(solution)/shard_map/ppermute | solution.py:250
  112.8 6.4 %copy-start.15 = (bf16[192,512]{1,0:T(8,128)(2,1)S(1)}, bf16[192,512]{1,0:T(8,128)(2,1)}, u32[]{:S(2)}) copy-start(bf16[192,512]{1,0:T(8,128)(2,1)} %get-tuple-element.39) | copy-start | bytes 589828
  112.8 10.6 %collective-permute-start.12 = (bf16[192,512]{1,0:T(8,128)(2,1)}, bf16[192,512]{1,0:T(8,128)(2,1)S(1)}, u32[]{:S(2)}, u32[]{:S(2)}) collective-permute-start(bf16[192,512]{1,0:T(8,128)(2,1)} %get-tuple-element.38), channel_id=1, source_target_pairs={{0,2},{1,3},{2,0},{3,1},{4,6},{5,7},{6,4},{7,5},{8,10},{9,11},{10,... | collective-permute-start | bytes 589832 | tf_op jit(solution)/shard_map/ppermute | solution.py:250
  119.3 8.9 %collective-permute-start.13 = (bf16[192,512]{1,0:T(8,128)(2,1)S(1)}, bf16[192,512]{1,0:T(8,128)(2,1)S(1)}, u32[]{:S(2)}, u32[]{:S(2)}) collective-permute-start(bf16[192,512]{1,0:T(8,128)(2,1)S(1)} %copy-done.15), channel_id=1, source_target_pairs={{0,3},{1,2},{2,1},{3,0},{4,7},{5,6},{6,5},{7,4},{8,11},{9,10},{10,... | collective-permute-start | bytes 589832 | tf_op jit(solution)/shard_map/ppermute | solution.py:250
  119.9 12.4 %collective-permute-start.10 = (bf16[192,512]{1,0:T(8,128)(2,1)}, bf16[192,512]{1,0:T(8,128)(2,1)S(1)}, u32[]{:S(2)}, u32[]{:S(2)}) collective-permute-start(bf16[192,512]{1,0:T(8,128)(2,1)} %get-tuple-element.35), channel_id=1, source_target_pairs={{0,3},{1,2},{2,1},{3,0},{4,7},{5,6},{6,5},{7,4},{8,11},{9,10},{10,... | collective-permute-start | bytes 589832 | tf_op jit(solution)/shard_map/ppermute | solution.py:250
  122.3 12.0 %collective-permute-start.8 = (bf16[192,512]{1,0:T(8,128)(2,1)}, bf16[192,512]{1,0:T(8,128)(2,1)S(1)}, u32[]{:S(2)}, u32[]{:S(2)}) collective-permute-start(bf16[192,512]{1,0:T(8,128)(2,1)} %get-tuple-element.33), channel_id=1, source_target_pairs={{0,1},{1,0},{2,3},{3,2},{4,5},{5,4},{6,7},{7,6},{8,9},{9,8},{10,11... | collective-permute-start | bytes 589832 | tf_op jit(solution)/shard_map/ppermute | solution.py:250
  122.8 5.3 %copy-start.8 = (bf16[192,512]{1,0:T(8,128)(2,1)}, bf16[192,512]{1,0:T(8,128)(2,1)S(1)}, u32[]{:S(2)}) copy-start(bf16[192,512]{1,0:T(8,128)(2,1)S(1)} %collective-permute-done.11.rest_1_) | copy-start | bytes 589828
  122.8 12.3 %collective-permute-start.9 = (bf16[192,512]{1,0:T(8,128)(2,1)}, bf16[192,512]{1,0:T(8,128)(2,1)S(1)}, u32[]{:S(2)}, u32[]{:S(2)}) collective-permute-start(bf16[192,512]{1,0:T(8,128)(2,1)} %get-tuple-element.34), channel_id=1, source_target_pairs={{0,2},{1,3},{2,0},{3,1},{4,6},{5,7},{6,4},{7,5},{8,10},{9,11},{10,... | collective-permute-start | bytes 589832 | tf_op jit(solution)/shard_map/ppermute | solution.py:250
  123.4 4.8 %copy-start.10 = (bf16[192,512]{1,0:T(8,128)(2,1)}, bf16[192,512]{1,0:T(8,128)(2,1)S(1)}, u32[]{:S(2)}) copy-start(bf16[192,512]{1,0:T(8,128)(2,1)S(1)} %collective-permute-done.12.rest_2_) | copy-start | bytes 589828
  (9 other events, 16.0 us)
Sparse Core Ops, SparseCore 0:
  9.0 49.8 all-gather.6
  60.5 45.8 all-gather.4

commit v3 on v0

v3 whole, which is shorter than its diff:
```python
import functools

import jax
import jax.numpy as jnp
from jax import lax
from jax.experimental import pallas as pl
from jax.experimental.pallas import tpu as pltpu
from jax.sharding import PartitionSpec as P

ADAPTER_SCALE = 2.0
CORES = 2
LANES = 128
COVER = 64
VMEM_BYTES = 60 * 1024 * 1024
ANYWHERE = pl.BlockSpec(memory_space=pl.ANY)
WHOLE = pl.BlockSpec(memory_space=pltpu.VMEM)
SCALARS = pl.BlockSpec(memory_space=pltpu.SMEM)


def params():
    return pltpu.CompilerParams(vmem_limit_bytes=VMEM_BYTES)


def cost(flops, bytes_accessed):
    return pl.CostEstimate(flops=flops, bytes_accessed=bytes_accessed, transcendentals=0)


def start_all(pairs, sems):
    copies = [pltpu.make_async_copy(src, dst, sems.at[n]) for n, (src, dst) in enumerate(pairs)]
    for copy in copies:
        copy.start()
    return copies


def load_all(pairs, sems):
    for copy in start_all(pairs, sems):
        copy.wait()


def base_kernel(mp_count, count, info_ref, mine_ref, other_ref, *rest):
    choices, outs, (weight, block, done, own, sems) = rest[:count], rest[-5 - mp_count : -5], rest[-5:]
    rows = block.shape[1]
    for number, choice in enumerate(choices):

        @pl.when(info_ref[1] == number)
        def _(choice=choice):
            pltpu.make_async_copy(choice, weight, sems.at[0]).start()

    order = [(number, part) for number in reversed(range(mp_count)) for part in range(CORES)]
    copies = {}
    for number, part in order:
        place = pl.ds(pl.multiple_of((info_ref[0] ^ number) * rows, rows), rows)
        n = CORES * number + part
        source = (mine_ref, other_ref)[part].at[place, :]
        copies[n] = pltpu.make_async_copy(source, block.at[n], sems.at[1 + n])
        copies[n].start()
    pltpu.make_async_copy(choices[0], weight, sems.at[0]).wait()
    stores = []
    for number, part in order:
        n = CORES * number + part
        copies[n].wait()
        target = done.at[number] if number else own
        product = jnp.dot(block[n], weight[...], preferred_element_type=jnp.float32)
        target[part * rows : (part + 1) * rows, :] = product.astype(target.dtype)
        if part:
            stores.append(pltpu.make_async_copy(target, outs[number], sems.at[1 + CORES * mp_count + number]))
            stores[-1].start()
    for store in stores:
        store.wait()


def base_products(info, mine, other, choices, mp_count, cover, *before):
    group_rows, features = mine.shape
    rows, span = group_rows // mp_count, choices[0].shape[1]
    return pl.pallas_call(
        functools.partial(base_kernel, mp_count, len(choices)),
        in_specs=[SCALARS] + [ANYWHERE] * (2 + len(choices) + len(before)),
        out_specs=[ANYWHERE] * mp_count,
        scratch_shapes=[
            pltpu.VMEM((features, span), mine.dtype),
            pltpu.VMEM((CORES * mp_count, rows, features), mine.dtype),
            pltpu.VMEM((mp_count, CORES * rows, span), jnp.bfloat16),
            pltpu.VMEM((CORES * rows, span), jnp.float32),
            pltpu.SemaphoreType.DMA((1 + (1 + CORES) * mp_count,)),
        ],
        out_shape=[
            jax.ShapeDtypeStruct((CORES * rows, span), jnp.bfloat16 if number else jnp.float32)
            for number in range(mp_count)
        ],
        compiler_params=params(),
        cost_estimate=cost(
            cover * 2 * CORES * group_rows * features * span,
            2 * (CORES * group_rows * (features + span) + features * span),
        ),
    )(info, mine, other, *choices, *before)


def cut_down_kernel(info_ref, down_ref, out, block, sems):
    mp_count, features, lanes = block.shape
    mine = pl.ds(pl.multiple_of(info_ref[0] * lanes, lanes), lanes)
    loads = start_all(
        [(down_ref.at[n * features : (n + 1) * features, mine], block.at[n]) for n in range(mp_count)], sems
    )
    stores = []
    for n, load in enumerate(loads):
        load.wait()
        stores.append(pltpu.make_async_copy(block.at[n], out.at[n], sems.at[mp_count + n]))
        stores[-1].start()
    for store in stores:
        store.wait()


def cut_down(core, down, mp_count):
    shape = mp_count, down.shape[0] // mp_count, down.shape[1] // CORES
    return pl.pallas_call(
        cut_down_kernel,
        in_specs=[SCALARS, ANYWHERE],
        out_specs=ANYWHERE,
        out_shape=jax.ShapeDtypeStruct(shape, down.dtype),
        scratch_shapes=[pltpu.VMEM(shape, down.dtype), pltpu.SemaphoreType.DMA((2 * mp_count,))],
        compiler_params=params(),
        cost_estimate=cost(0, 2 * down.size),
    )(core, down)


def cut_up_kernel(width, info_ref, up_ref, out, block, sems):
    parts, ranks, span = up_ref.shape
    lanes = block.shape[1]
    pairs = []
    for part in range(parts):
        for place in range(0, span, CORES * width):
            for first in range(place, place + width, lanes):
                columns = pl.ds(pl.multiple_of(first + info_ref[0] * width, lanes), lanes)
                row = len(pairs) * ranks
                pairs.append((up_ref.at[part, :, columns], block.at[row : row + ranks, :]))
    load_all(pairs, sems)
    load_all([(block, out.at[n]) for n in range(out.shape[0])], sems)


def cut_up(core, up, mp_count, width, lanes):
    parts, ranks, span = up.shape
    blocks = parts * span // CORES // lanes
    return pl.pallas_call(
        functools.partial(cut_up_kernel, width),
        in_specs=[SCALARS, ANYWHERE],
        out_specs=ANYWHERE,
        out_shape=jax.ShapeDtypeStruct((mp_count, blocks * ranks, lanes), up.dtype),
        scratch_shapes=[
            pltpu.VMEM((blocks * ranks, lanes), up.dtype),
            pltpu.SemaphoreType.DMA((max(blocks, mp_count),)),
        ],
        compiler_params=params(),
        cost_estimate=cost(0, 4 * mp_count * blocks * ranks * lanes),
    )(core, up)


def low_kernel(adapters, rank_pair, info_ref, mine_ref, other_ref, ids_ref, maps_ref, *rest):
    out, block, maps, sems = rest[-4:]
    mp_count, features, lanes = maps.shape
    rows = block.shape[1]
    order = [(number, part) for number in range(mp_count) for part in range(CORES)]
    pairs = [(maps_ref.at[number, :features, :], maps.at[number]) for number in range(mp_count)]
    for number, part in order:
        pairs.append(((mine_ref, other_ref)[part].at[number * rows : (number + 1) * rows, :], block.at[CORES * number + part]))
    copies = start_all(pairs, sems)
    for copy in copies[:mp_count]:
        copy.wait()
    lane_adapter = lax.broadcasted_iota(jnp.int32, (rows, lanes), 1) // rank_pair
    groups = lanes // rank_pair
    depth = CORES * rows // groups
    lane_group = lax.broadcasted_iota(jnp.int32, (depth, lanes), 1) // rank_pair
    for number in range(mp_count):
        halves = []
        for part in range(CORES):
            n = CORES * number + part
            copies[mp_count + n].wait()
            ids = ids_ref[part, number * rows : (number + 1) * rows, :]
            total = jnp.zeros((rows, lanes), jnp.float32)
            for owner in range(0, mp_count, CORES):
                both = jnp.concatenate([maps[owner], maps[owner + 1]], axis=1)
                product = jnp.dot(block[n], both, preferred_element_type=jnp.float32)
                for m in range(CORES):
                    wanted = ids - (owner + m) * adapters - info_ref[0] * groups
                    total += jnp.where(lane_adapter == wanted, product[:, m * lanes : (m + 1) * lanes], 0.0)
            shift = lanes // 2
            while shift >= rank_pair:
                total = total + pltpu.roll(total, shift, 1)
                shift //= 2
            halves.append(total)
        both = jnp.concatenate(halves, axis=0)
        packed = jnp.zeros((depth, lanes), jnp.float32)
        for group in range(groups):
            packed += jnp.where(lane_group == group, both[group * depth : (group + 1) * depth, :], 0.0)
        out[number] = packed


def low_sums(core, mine, other, ids, maps, adapters, rank, *before):
    group_rows, features = mine.shape
    mp_count, _, lanes = maps.shape
    rows = group_rows // mp_count
    depth = CORES * rows * 2 * rank // lanes
    return pl.pallas_call(
        functools.partial(low_kernel, adapters, 2 * rank),
        in_specs=[SCALARS, ANYWHERE, ANYWHERE, WHOLE, ANYWHERE] + [ANYWHERE] * len(before),
        out_specs=WHOLE,
        out_shape=jax.ShapeDtypeStruct((mp_count, depth, lanes), jnp.float32),
        scratch_shapes=[
            pltpu.VMEM((CORES * mp_count, rows, features), mine.dtype),
            pltpu.VMEM((mp_count, features, lanes), maps.dtype),
            pltpu.SemaphoreType.DMA(((1 + CORES) * mp_count,)),
        ],
        compiler_params=params(),
        cost_estimate=cost(
            2 * CORES * group_rows * features * mp_count * lanes, 2 * features * (CORES * group_rows + mp_count * lanes)
        ),
    )(core, mine, other, ids, maps, *before)


def delta_kernel(adapters, rank, ids_ref, mine_ref, other_ref, maps_ref, out, maps, sem):
    copy = pltpu.make_async_copy(maps_ref.at[:, maps_ref.shape[1] - maps.shape[1] :, :], maps, sem)
    copy.start()
    mp_count = maps.shape[0]
    planes, rows, span = out.shape
    lanes = mine_ref.shape[2]
    rank_pair = 2 * rank
    groups = lanes // rank_pair
    depth = rows // groups
    packed = sum(mine_ref[n] for n in range(mp_count))
    packed = packed + pltpu.roll(sum(other_ref[n] for n in range(mp_count)), lanes // 2, 1)
    lane_group = lax.broadcasted_iota(jnp.int32, (depth, lanes), 1) // rank_pair
    spread = []
    for group in range(groups):
        values = jnp.where(lane_group == group, packed, 0.0)
        shift = lanes // 2
        while shift >= rank_pair:
            values = values + pltpu.roll(values, shift, 1)
            shift //= 2
        spread.append(values)
    low = jnp.concatenate(spread, axis=0)
    ids = ids_ref[...]
    lane_block = lax.broadcasted_iota(jnp.int32, (rows, lanes), 1) // rank
    even = lane_block % 2 == 0
    lows = [jnp.where(even, low, pltpu.roll(low, rank, 1)), jnp.where(even, pltpu.roll(low, lanes - rank, 1), low)]
    copy.wait()
    ranks = adapters * rank
    for part in range(2):
        spreads = [
            jnp.where(lane_block == ids - owner * adapters, lows[part], 0.0).astype(jnp.bfloat16)
            for owner in range(mp_count)
        ]
        for plane in range(part * planes // 2, (part + 1) * planes // 2):
            for piece in range(span // lanes):
                first = (plane * (span // lanes) + piece) * ranks
                total = jnp.zeros((rows, lanes), jnp.float32)
                for owner in range(mp_count):
                    weights = maps[owner, first : first + ranks, :]
                    total += jnp.dot(spreads[owner], weights, preferred_element_type=jnp.float32)
                out[plane, :, piece * lanes : (piece + 1) * lanes] = (ADAPTER_SCALE * total).astype(out.dtype)


def deltas_of(ids, mine, other, maps, adapters, rank, planes, span):
    mp_count, _, lanes = maps.shape
    rows = ids.shape[0]
    depth = planes * span // lanes * adapters * rank
    return pl.pallas_call(
        functools.partial(delta_kernel, adapters, rank),
        in_specs=[WHOLE] * 3 + [ANYWHERE],
        out_specs=WHOLE,
        out_shape=jax.ShapeDtypeStruct((planes, rows, span), jnp.bfloat16),
        scratch_shapes=[pltpu.VMEM((mp_count, depth, lanes), maps.dtype), pltpu.SemaphoreType.DMA],
        compiler_params=params(),
        cost_estimate=cost(2 * rows * mp_count * depth * lanes, 2 * mp_count * depth * lanes),
    )(ids, mine, other, maps)


def finish_kernel(mp_count, turns, info_ref, delta_ref, *rest):
    parts, (delta, own, others, done, sems) = rest[: mp_count * turns], rest[-5:]
    out, *away = rest[-6 - turns : -5]
    rows, span = away[0].shape
    each = mp_count + 1
    loads = []
    for turn in range(turns):
        first, *peers = parts[mp_count * turn : mp_count * (turn + 1)]
        pairs = [(first, own.at[turn]), (delta_ref.at[info_ref[2 * turn]], delta.at[turn])]
        pairs += [(part, others.at[turn, n]) for n, part in enumerate(peers)]
        loads.append(start_all(pairs, sems.at[pl.ds(turn * each, each)]))
    stores = []
    for turn in range(turns):
        for load in loads[turn]:
            load.wait()
        total = own[turn]
        for n in range(mp_count - 1):
            total = total + others[turn, n].astype(jnp.float32)
        done[turn] = (total + delta[turn].astype(jnp.float32)).astype(done.dtype)
        place = pl.ds(pl.multiple_of(info_ref[2 * turn + 1] * span, span), span)
        pairs = [(done.at[turn, rows:, :], away[turn]), (done.at[turn, :rows, :], out.at[:, place])]
        stores += start_all(pairs, sems.at[pl.ds(turns * each + 2 * turn, 2)])
    for store in stores:
        store.wait()


def finish(info, delta, parts, held, width):
    turns, mp_count = len(parts), len(parts[0])
    rows, span = parts[0][0].shape
    operands = [info, delta, *sum(parts, [])] + ([] if held is None else [held])
    away = jax.ShapeDtypeStruct((rows // CORES, span), delta.dtype)
    return pl.pallas_call(
        functools.partial(finish_kernel, mp_count, turns),
        in_specs=[SCALARS] + [ANYWHERE] * (len(operands) - 1),
        out_specs=[ANYWHERE] * (1 + turns),
        out_shape=[jax.ShapeDtypeStruct((rows // CORES, width), delta.dtype)] + [away] * turns,
        scratch_shapes=[
            pltpu.VMEM((turns, rows, span), delta.dtype),
            pltpu.VMEM((turns, rows, span), jnp.float32),
            pltpu.VMEM((turns, mp_count - 1, rows, span), delta.dtype),
            pltpu.VMEM((turns, rows, span), delta.dtype),
            pltpu.SemaphoreType.DMA((turns * (mp_count + 3),)),
        ],
        input_output_aliases={} if held is None else {len(operands) - 1: 0},
        compiler_params=params(),
        cost_estimate=cost(4 * rows * span * turns, 12 * rows * span * turns),
    )(*operands)


def settle_kernel(info_ref, *rest):
    pieces, (out, sems) = rest[:-3], rest[-2:]
    span = pieces[0].shape[1]
    load_all(
        [
            (piece, out.at[:, pl.ds(pl.multiple_of(info_ref[n] * span, span), span)])
            for n, piece in enumerate(pieces)
        ],
        sems,
    )


def settle(info, pieces, held):
    operands = [info, *pieces, held]
    return pl.pallas_call(
        settle_kernel,
        in_specs=[SCALARS] + [WHOLE] * len(pieces) + [ANYWHERE],
        out_specs=ANYWHERE,
        out_shape=jax.ShapeDtypeStruct(held.shape, held.dtype),
        scratch_shapes=[pltpu.SemaphoreType.DMA((len(pieces),))],
        input_output_aliases={len(operands) - 1: 0},
        compiler_params=params(),
        cost_estimate=cost(0, 4 * len(pieces) * pieces[0].size),
    )(*operands)


def by_plane(plane, values):
    return sum(jnp.where(plane == n, value, 0) for n, value in enumerate(values)).astype(jnp.int32)


def arrival_order(plane, planes):
    sides = (1, -1) if 2 * plane < planes else (-1, 1)
    return [
        (side, distance)
        for distance in range(1, planes)
        for side in sides
        if 0 <= plane + side * distance < planes
    ]


def local(tokens, frozen_weight, adapter_down_weight, adapter_up_weight, token_adapter_index):
    mp_count, dp_count = lax.axis_size("mp"), lax.axis_size("dp")
    position, replica = lax.axis_index("mp"), lax.axis_index("dp")
    planes = dp_count // CORES
    plane, core = replica // CORES, replica % CORES
    group_rows, features = tokens.shape
    rows = group_rows // mp_count
    width = frozen_weight.shape[1]
    adapters, rank, up_span = adapter_up_weight.shape[1:]
    ranks = adapters * rank

    def info_of(*values):
        return jnp.stack([jnp.asarray(value, jnp.int32) for value in values])

    def after_all(*arrays):
        return lax.optimization_barrier(arrays)

    def swap(array):
        return lax.ppermute(array, "dp", [(n, n ^ 1) for n in range(dp_count)])

    def trade(array):
        return lax.all_to_all(array, "mp", 0, 0)

    def pass_round(blocks):
        return [
            lax.ppermute(block, "mp", [(m, m ^ n) for m in range(mp_count)]) for n, block in enumerate(blocks, 1)
        ]

    def hop(array, side, step):
        sources = range(1, planes - step + 1) if side > 0 else range(step - 1, planes - 1)
        return lax.ppermute(
            array, "dp", [(CORES * n + m, CORES * (n - side) + m) for n in sources for m in range(CORES)]
        )

    got = {(side, 1): hop(frozen_weight, side, 1) for side in (1, -1)}
    other = swap(tokens)
    ids = token_adapter_index.reshape(group_rows, 1)
    ids = jnp.stack([ids, swap(token_adapter_index).reshape(group_rows, 1)])
    own_ids = lax.dynamic_slice_in_dim(ids, position * rows, rows, axis=1).reshape(CORES * rows, 1)

    core_of = core.astype(jnp.int32).reshape(1)
    down = trade(cut_down(core_of, adapter_down_weight, mp_count))
    up = cut_up(core_of, adapter_up_weight.reshape(2, ranks, up_span), mp_count, width, down.shape[2])

    own, *sent = base_products(info_of(position, 0), tokens, other, [frozen_weight], mp_count, COVER, up, ids, own_ids)
    parts = [own] + pass_round(sent)
    finished = []
    group = plane
    orders = [arrival_order(n, planes) for n in range(planes)]
    for turn in range(1, planes):
        if turn < planes - 1:
            got[1, turn], got[-1, turn], parts[0] = after_all(got[1, turn], got[-1, turn], parts[0])
            for side in (1, -1):
                got[side, turn + 1] = hop(got[side, turn], side, turn + 1)
        wanted = [order[turn - 1] for order in orders]
        options = sorted(set(wanted))
        choice = by_plane(plane, [options.index(item) for item in wanted])
        before = []
        if turn == planes - 1:
            sums = trade(sums)
            before = [sums]
        elif turn == 1:
            before = [down]
        else:
            before = finished[turn - 2][1][1:]
        finished.append((group, parts))
        group = by_plane(plane, [n + side * distance for n, (side, distance) in enumerate(wanted)])
        info = info_of(position, choice)
        shards = [got[option] for option in options]
        last = turn == planes - 1
        own, *sent = base_products(info, tokens, other, shards, mp_count, COVER, *before)
        parts = [own] + pass_round(sent)
        if turn == 1:
            up, own = after_all(up, own)
            up = trade(up)
            parts[0] = own
        elif turn == 2 and not last:
            sums = low_sums(core_of, tokens, other, ids, down, adapters, rank, own, up, *finished[1][1][1:])
    finished.append((group, parts))

    delta = deltas_of(own_ids, sums, swap(sums), up, adapters, rank, planes, width)
    out, places, pieces = None, [], []
    for some in (finished[:-1], finished[-1:]):
        info = info_of(*[value for group, _ in some for value in (group, CORES * group + core)])
        out, *away = finish(info, delta, [parts for _, parts in some], out, dp_count * width)
        places.append(info_of(*[CORES * group + 1 - core for group, _ in some]))
        pieces.append([swap(piece) for piece in away])
    for place, some in zip(places, pieces):
        out = settle(place, some, out)
    return out


def solution(mesh):
    placed = (P("dp", "mp"), P("mp", "dp"), P(None, "mp"), P(None, "mp", None, None), P("dp"))
    return jax.shard_map(
        local, mesh=mesh, in_specs=placed, out_specs=P(("dp", "mp"), None), check_vma=False
    )
```

time: 299 us -> 132 us (0.44)
  waiting for transfers between devices: 186 us -> 19.5 us
  Pallas kernels: 0 us -> 57.5 us
  local copies, waits for them, and re-layouts: 51.1 us -> 8.32 us
  starting transfers between devices: 13 us -> 40.6 us
  matrix products: 18.8 us -> 0 us
  between operations: 13.6 us -> 0.6 us
  other arithmetic: 15.9 us -> 3.69 us
    all_to_all x3, waiting for transfers between devices: 104 us -> 7.4 us  [trade(): return lax.all_to_all(array, 'mp', 0, 0)]
    all_gather x1 -> x0, waiting for transfers between devices: 80.9 us -> none  [local(): weight_full = lax.all_gather(frozen_weight, 'dp', axis=1, tiled=True)]
    pallas_call x0 -> x12, Pallas kernels: none -> 57.5 us  [the longest x4 29.7 us: base_products(): pl.pallas_call(functools.partial(base_kernel, mp_count, len(choices)), in...]
    ppermute x0 -> x25, starting transfers between devices: none -> 29.8 us  [the longest x12 15.5 us: pass_round(): lax.ppermute(block, 'mp', [(m, m ^ n) for m in range(mp_count)])]
    dot_general x4 -> x0, matrix products: 18.8 us -> none  [the longest x1 11.7 us: local(): jnp.dot(tokens, weight_full, preferred_element_type=jnp.float32)]
    ppermute x0 -> x25, waiting for transfers between devices: none -> 12.1 us  [the longest x6 12 us: hop(): lax.ppermute(array, 'dp', [(CORES * n + m, CORES * (n - side) + m) for n...]
    gather x2 -> x0, local copies, waits for them, and re-layouts: 11.8 us -> none  [the longest x1 7.15 us: local(): jnp.take(padded, slot_token, axis=0)]
    reshape x2 -> x0, local copies, waits for them, and re-layouts: 11.7 us -> none  [the longest x1 11.1 us: local(): flat_tokens = received.reshape(-1, hidden_width)]
  transfers between devices with their start and end apart: 5 -> 28, of which waited for: 3 -> 5; matrix products, arithmetic and copies ran while one was open for 24% -> 4% of each run, Pallas kernels for 0% -> 43%
where the time goes in v3:
time: 132 us; the launch traced here: 130 us
  Pallas kernels  57.5 us (44%)
  starting transfers between devices  40.6 us (31%)
  waiting for transfers between devices  19.5 us (15%)
  local copies, waits for them, and re-layouts  8.32 us (6%)
  other arithmetic  3.69 us (3%)
    pallas_call x4, Pallas kernels, base_products(): pl.pallas_call(functools.partial(base_kernel, mp_count, len(choices)), in...  29.7 us
    ppermute x12, starting transfers between devices, pass_round(): lax.ppermute(block, 'mp', [(m, m ^ n) for m in range(mp_count)])  15.5 us
    ppermute x6, starting transfers between devices, hop(): lax.ppermute(array, 'dp', [(CORES * n + m, CORES * (n - side) + m) for n...  12.5 us
    ppermute x6, waiting for transfers between devices, hop(): lax.ppermute(array, 'dp', [(CORES * n + m, CORES * (n - side) + m) for n...  12 us
    all_to_all x3, starting transfers between devices, trade(): return lax.all_to_all(array, 'mp', 0, 0)  10.8 us
    pallas_call x1, Pallas kernels, low_sums(): pl.pallas_call(functools.partial(low_kernel, adapters, 2 * rank), in_spec...  9.54 us
    all_to_all x3, waiting for transfers between devices, trade(): return lax.all_to_all(array, 'mp', 0, 0)  7.4 us
    unnamed x51, local copies, waits for them, and re-layouts  6.8 us
  transfers between devices with their start and end apart: 28, of which 5 were waited for; matrix products, arithmetic and copies ran while one was open for 4% of the time, Pallas kernels for 43%

profile of v3, /device:TPU:0, one launch (start us, length us, event | category | flops | bytes accessed | tf_op | source)
XLA Modules:
  0.0 130.3 jit_solution(9872489393952982537)
XLA Ops:
  1.7 6.1 %collective-permute-start.3 = (bf16[2048,256]{1,0:T(8,128)(2,1)}, bf16[2048,256]{1,0:T(8,128)(2,1)}, u32[]{:S(2)}, u32[]{:S(2)}) collective-permute-start(bf16[2048,256]{1,0:T(8,128)(2,1)} %rest_0_.1), channel_id=1, source_target_pairs={{0,8},{4,12},{8,16},{12,20},{16,24},{20,28},{1,9},{5,13},{9,17},{1... | collective-permute-start | bytes 3145736 | tf_op jit(solution)/shard_map/ppermute | solution.py:395
  8.1 2.4 %shard_map.55 = bf16[4,2048,128]{2,1,0:T(8,128)(2,1)} custom-call(s32[1]{0:T(128)} %bitcast.4.info_ref, bf16[8192,256]{1,0:T(8,128)(2,1)} %down_ref.1), custom_call_target="tpu_custom_call" | custom-call | bytes 4194304 | tf_op jit(solution)/shard_map/pallas_call | solution.py:115
  10.5 3.9 %all-to-all-start = ((bf16[4,2048,128]{2,1,0:T(8,128)(2,1)}), bf16[4,2048,128]{2,1,0:T(8,128)(2,1)S(1)}, u32[]{:S(2)}, u32[]{:S(2)}) async-start(bf16[4,2048,128]{2,1,0:T(8,128)(2,1)} %shard_map.55), calls=%async_computation | async-start | bytes 4194304 | tf_op jit(solution)/shard_map/all_to_all | solution.py:386
  16.6 1.9 %shard_map.56.rest_1_ = bf16[4,1024,128]{2,1,0:T(8,128)(2,1)} custom-call(s32[1]{0:T(128)} %bitcast.4.info_ref, bf16[2,128,1024]{2,1,0:T(8,128)(2,1)} %bitcast.21), custom_call_target="tpu_custom_call" | custom-call | bytes 2097152 | tf_op jit(solution)/shard_map/pallas_call | solution.py:143
  19.7 7.4 %shard_map.57 = (f32[384,256]{1,0:T(8,128)}, bf16[384,256]{1,0:T(8,128)(2,1)}, bf16[384,256]{1,0:T(8,128)(2,1)}, bf16[384,256]{1,0:T(8,128)(2,1)}) custom-call(s32[2]{0:T(128)} %pad_add_fusion.2.info_ref, bf16[768,2048]{1,0:T(8,128)(2,1)} %mine_ref.9, bf16[768,2048]{1,0:T(8,128)(2,1)} %collective-permute-done.1.other_ref, bf16[2048,256]{1,0:T(8,128)(2,1)} %rest_0_.1, ...), custom_call_target="tpu_custom_call" | custom-call | flops 103079215104 | bytes 8126464 | tf_op jit(solution)/shard_map/pallas_call | solution.py:75
  27.1 2.0 %collective-permute-done.2.rest_1_.rest_2_ = bf16[2048,256]{1,0:T(8,128)(2,1)} collective-permute-done((bf16[2048,256]{1,0:T(8,128)(2,1)}, bf16[2048,256]{1,0:T(8,128)(2,1)}, u32[]{:S(2)}, u32[]{:S(2)}) %collective-permute-start.2) | collective-permute-done | bytes 1048608 | tf_op jit(solution)/shard_map/ppermute | solution.py:395
  30.3 1.6 %collective-permute-start.6 = (bf16[384,256]{1,0:T(8,128)(2,1)}, bf16[384,256]{1,0:T(8,128)(2,1)S(1)}, u32[]{:S(2)}, u32[]{:S(2)}) collective-permute-start(bf16[384,256]{1,0:T(8,128)(2,1)} %get-tuple-element.42), channel_id=1, source_target_pairs={{0,1},{1,0},{2,3},{3,2},{4,5},{5,4},{6,7},{7,6},{8,9},{9,8},{10,11... | collective-permute-start | bytes 589832 | tf_op jit(solution)/shard_map/ppermute | solution.py:390
  35.8 5.0 %all-to-all-done.rest_2_.maps_ref = bf16[4,2048,128]{2,1,0:T(8,128)(2,1)S(1)} async-done(((bf16[4,2048,128]{2,1,0:T(8,128)(2,1)}), bf16[4,2048,128]{2,1,0:T(8,128)(2,1)S(1)}, u32[]{:S(2)}, u32[]{:S(2)}) %all-to-all-start) | async-done | bytes 2097184 | tf_op jit(solution)/shard_map/all_to_all | solution.py:386
  42.1 7.4 %shard_map.58 = (f32[384,256]{1,0:T(8,128)}, bf16[384,256]{1,0:T(8,128)(2,1)}, bf16[384,256]{1,0:T(8,128)(2,1)}, bf16[384,256]{1,0:T(8,128)(2,1)}) custom-call(s32[2]{0:T(128)} %pad_add_fusion.3.info_ref, bf16[768,2048]{1,0:T(8,128)(2,1)} %mine_ref.9, bf16[768,2048]{1,0:T(8,128)(2,1)} %collective-permute-done.1.other_ref, ...), custom_call_target="tpu_custom_call" | custom-call | flops 103079215104 | bytes 8126464 | tf_op jit(solution)/shard_map/pallas_call | solution.py:75
  49.5 3.5 %all-to-all-start.1 = ((bf16[4,1024,128]{2,1,0:T(8,128)(2,1)}), bf16[4,1024,128]{2,1,0:T(8,128)(2,1)S(1)}, u32[]{:S(2)}, u32[]{:S(2)}) async-start(bf16[4,1024,128]{2,1,0:T(8,128)(2,1)} %shard_map.56.rest_1_), calls=%async_computation.1 | async-start | bytes 2097152 | tf_op jit(solution)/shard_map/all_to_all | solution.py:386
  53.1 2.0 %collective-permute-start.9 = (bf16[384,256]{1,0:T(8,128)(2,1)}, bf16[384,256]{1,0:T(8,128)(2,1)S(1)}, u32[]{:S(2)}, u32[]{:S(2)}) collective-permute-start(bf16[384,256]{1,0:T(8,128)(2,1)} %get-tuple-element.47), channel_id=1, source_target_pairs={{0,1},{1,0},{2,3},{3,2},{4,5},{5,4},{6,7},{7,6},{8,9},{9,8},{10,11... | collective-permute-start | bytes 589832 | tf_op jit(solution)/shard_map/ppermute | solution.py:390
  55.0 8.9 %collective-permute-done.4.rest_3_.rest_2_ = bf16[2048,256]{1,0:T(8,128)(2,1)} collective-permute-done((bf16[2048,256]{1,0:T(8,128)(2,1)}, bf16[2048,256]{1,0:T(8,128)(2,1)}, u32[]{:S(2)}, u32[]{:S(2)}) %collective-permute-start.4) | collective-permute-done | bytes 1048608 | tf_op jit(solution)/shard_map/ppermute | solution.py:395
  66.9 1.6 %collective-permute-start.13 = (bf16[2048,256]{1,0:T(8,128)(2,1)S(1)}, bf16[2048,256]{1,0:T(8,128)(2,1)}, u32[]{:S(2)}, u32[]{:S(2)}) collective-permute-start(bf16[2048,256]{1,0:T(8,128)(2,1)S(1)} %collective-permute-done.5.rest_1_.rest_0_), channel_id=1, source_target_pairs={{16,24},{20,28},{17,25},{21,29},{18,26},{22,30},{19,27},{23,31}} | collective-permute-start | bytes 3145736 | tf_op jit(solution)/shard_map/ppermute | solution.py:395
  70.0 7.4 %shard_map.59 = (f32[384,256]{1,0:T(8,128)}, bf16[384,256]{1,0:T(8,128)(2,1)}, bf16[384,256]{1,0:T(8,128)(2,1)}, bf16[384,256]{1,0:T(8,128)(2,1)}) custom-call(s32[2]{0:T(128)} %pad_add_fusion.1.info_ref, bf16[768,2048]{1,0:T(8,128)(2,1)} %mine_ref.9, bf16[768,2048]{1,0:T(8,128)(2,1)} %collective-permute-done.1.other_ref, ...), custom_call_target="tpu_custom_call" | custom-call | flops 103079215104 | bytes 8126464 | tf_op jit(solution)/shard_map/pallas_call | solution.py:75
  78.6 9.5 %shard_map.60 = f32[4,96,128]{2,1,0:T(8,128)} custom-call(s32[1]{0:T(128)} %bitcast.4.info_ref, bf16[768,2048]{1,0:T(8,128)(2,1)} %mine_ref.9, bf16[768,2048]{1,0:T(8,128)(2,1)} %collective-permute-done.1.other_ref, s32[2,768,1]{2,1,0:T(8,128)} %copy-done.3, bf16[4,2048,128]{2,1,0:T(8,128)(2,1)} %copy-done.1, f32[384,256]{1,0:T(8,128)} %get-tuple-element.45.rest_0_.rest_8_, ...), custom_call_target="tpu_custom_call" | custom-call | flops 3221225472 | bytes 8388608 | tf_op jit(solution)/shard_map/pallas_call | solution.py:202
  88.2 3.4 %all-to-all-start.2 = ((f32[4,96,128]{2,1,0:T(8,128)}), f32[4,96,128]{2,1,0:T(8,128)S(1)}, u32[]{:S(2)}, u32[]{:S(2)}) async-start(f32[4,96,128]{2,1,0:T(8,128)} %shard_map.60), calls=%async_computation.2 | async-start | bytes 393216 | tf_op jit(solution)/shard_map/all_to_all | solution.py:386
  92.2 2.0 %collective-permute-start.18 = (bf16[384,256]{1,0:T(8,128)(2,1)S(1)}, bf16[384,256]{1,0:T(8,128)(2,1)S(1)}, u32[]{:S(2)}, u32[]{:S(2)}) collective-permute-start(bf16[384,256]{1,0:T(8,128)(2,1)S(1)} %copy-done.24), channel_id=1, source_target_pairs={{0,1},{1,0},{2,3},{3,2},{4,5},{5,4},{6,7},{7,6},{8,9},{9,8},{10,11... | collective-permute-start | bytes 589832 | tf_op jit(solution)/shard_map/ppermute | solution.py:390
  95.7 2.4 %all-to-all-done.2.mine_ref.rest_4_ = f32[4,96,128]{2,1,0:T(8,128)S(1)} async-done(((f32[4,96,128]{2,1,0:T(8,128)}), f32[4,96,128]{2,1,0:T(8,128)S(1)}, u32[]{:S(2)}, u32[]{:S(2)}) %all-to-all-start.2) | async-done | bytes 196640 | tf_op jit(solution)/shard_map/all_to_all | solution.py:386
  98.8 7.4 %shard_map.62 = (f32[384,256]{1,0:T(8,128)}, bf16[384,256]{1,0:T(8,128)(2,1)}, bf16[384,256]{1,0:T(8,128)(2,1)}, bf16[384,256]{1,0:T(8,128)(2,1)}) custom-call(s32[2]{0:T(128)} %pad_add_fusion.4.info_ref, bf16[768,2048]{1,0:T(8,128)(2,1)} %mine_ref.9, bf16[768,2048]{1,0:T(8,128)(2,1)} %collective-permute-done.1.other_ref, bf16[2048,256]{1,0:T(8,128)(2,1)} %copy-done.21, ...), custom_call_target="tpu_custom_call" | custom-call | flops 103079215104 | bytes 8126464 | tf_op jit(solution)/shard_map/pallas_call | solution.py:75
  107.9 1.9 %collective-permute-start.17 = (bf16[384,256]{1,0:T(8,128)(2,1)}, bf16[384,256]{1,0:T(8,128)(2,1)S(1)}, u32[]{:S(2)}, u32[]{:S(2)}) collective-permute-start(bf16[384,256]{1,0:T(8,128)(2,1)} %get-tuple-element.53), channel_id=1, source_target_pairs={{0,3},{1,2},{2,1},{3,0},{4,7},{5,6},{6,5},{7,4},{8,11},{9,10},{10,... | collective-permute-start | bytes 589832 | tf_op jit(solution)/shard_map/ppermute | solution.py:390
  111.0 4.3 %shard_map.61.delta_ref = bf16[4,384,256]{2,1,0:T(8,128)(2,1)} custom-call(s32[384,1]{1,0:T(8,128)} %bitcast.20, f32[4,96,128]{2,1,0:T(8,128)} %copy-done.2, f32[4,96,128]{2,1,0:T(8,128)} %copy-done.12, bf16[4,1024,128]{2,1,0:T(8,128)(2,1)} %copy-done), custom_call_target="tpu_custom_call" | custom-call | flops 402653184 | bytes 1048576 | tf_op jit(solution)/shard_map/pallas_call | solution.py:265
  116.6 3.6 %shard_map.63 = (bf16[192,2048]{1,0:T(8,128)(2,1)}, bf16[192,256]{1,0:T(8,128)(2,1)}, bf16[192,256]{1,0:T(8,128)(2,1)}, bf16[192,256]{1,0:T(8,128)(2,1)}) custom-call(s32[6]{0:T(128)} %stack.94.info_ref, bf16[4,384,256]{2,1,0:T(8,128)(2,1)} %shard_map.61.delta_ref, f32[384,256]{1,0:T(8,128)} %get-tuple-element.54.rest_0_, bf16[384,256]{1,0:T(8,128)(2,1)} %copy-done.4, ...), custom_call_target="tpu_custom_call" | custom-call | flops 1179648 | bytes 3538944 | tf_op jit(solution)/shard_map/pallas_call | solution.py:307
  121.6 2.8 %shard_map.64 = (bf16[192,2048]{1,0:T(8,128)(2,1)}, bf16[192,256]{1,0:T(8,128)(2,1)}) custom-call(s32[2]{0:T(128)} %pad_add_fusion.info_ref, bf16[4,384,256]{2,1,0:T(8,128)(2,1)} %shard_map.61.delta_ref, f32[384,256]{1,0:T(8,128)} %get-tuple-element.50.rest_0_, bf16[384,256]{1,0:T(8,128)(2,1)} %copy-done.13, ...), custom_call_target="tpu_custom_call", output_to_operand_aliasing={{0}: (6, {})} | custom-call | flops 393216 | bytes 1179648 | tf_op jit(solution)/shard_map/pallas_call | solution.py:307
  126.2 1.7 %shard_map.65.rest_1_ = bf16[192,2048]{1,0:T(8,128)(2,1)} custom-call(s32[3]{0:T(128)} %pad_add_fusion.5.info_ref, bf16[192,256]{1,0:T(8,128)(2,1)} %copy-done.16, bf16[192,256]{1,0:T(8,128)(2,1)} %copy-done.17, bf16[192,256]{1,0:T(8,128)(2,1)} %copy-done.18, bf16[192,2048]{1,0:T(8,128)(2,1)} %get-tuple-element.64.rest_3_), custom_call_target="tpu_custom_call", output_to_operand_aliasing={{}: (4, {})} | custom-call | bytes 589824 | tf_op jit(solution)/shard_map/pallas_call | solution.py:339
  (104 shorter events, 29.4 us)
Async XLA Ops:
  0.0 19.5 %collective-permute-start.1 = (bf16[768,2048]{1,0:T(8,128)(2,1)}, bf16[768,2048]{1,0:T(8,128)(2,1)}, u32[]{:S(2)}, u32[]{:S(2)}) collective-permute-start(bf16[768,2048]{1,0:T(8,128)(2,1)} %mine_ref.9), channel_id=1, source_target_pairs={{0,4},{4,0},{8,12},{12,8},{16,20},{20,16},{24,28},{28,24},{1,5},{5... | collective-permute-start | bytes 9437192 | tf_op jit(solution)/shard_map/ppermute | solution.py:383
  0.5 28.6 %collective-permute-start.2 = (bf16[2048,256]{1,0:T(8,128)(2,1)}, bf16[2048,256]{1,0:T(8,128)(2,1)}, u32[]{:S(2)}, u32[]{:S(2)}) collective-permute-start(bf16[2048,256]{1,0:T(8,128)(2,1)} %rest_0_.1), channel_id=1, source_target_pairs={{8,0},{12,4},{16,8},{20,12},{24,16},{28,20},{9,1},{13,5},{17,9},{2... | collective-permute-start | bytes 3145736 | tf_op jit(solution)/shard_map/ppermute | solution.py:395
  1.7 28.5 %collective-permute-start.3 = (bf16[2048,256]{1,0:T(8,128)(2,1)}, bf16[2048,256]{1,0:T(8,128)(2,1)}, u32[]{:S(2)}, u32[]{:S(2)}) collective-permute-start(bf16[2048,256]{1,0:T(8,128)(2,1)} %rest_0_.1), channel_id=1, source_target_pairs={{0,8},{4,12},{8,16},{12,20},{16,24},{20,28},{1,9},{5,13},{9,17},{1... | collective-permute-start | bytes 3145736 | tf_op jit(solution)/shard_map/ppermute | solution.py:395
  7.9 10.7 %collective-permute-start = (s32[768]{0:T(1024)}, s32[768]{0:T(1024)S(1)}, u32[]{:S(2)}, u32[]{:S(2)}) collective-permute-start(s32[768]{0:T(1024)} %param.9), channel_id=1, source_target_pairs={{0,4},{4,0},{8,12},{12,8},{16,20},{20,16},{24,28},{28,24},{1,5},{5... | collective-permute-start | bytes 9224 | tf_op jit(solution)/shard_map/ppermute | solution.py:383
  10.5 30.2 %all-to-all-start = ((bf16[4,2048,128]{2,1,0:T(8,128)(2,1)}), bf16[4,2048,128]{2,1,0:T(8,128)(2,1)S(1)}, u32[]{:S(2)}, u32[]{:S(2)}) async-start(bf16[4,2048,128]{2,1,0:T(8,128)(2,1)} %shard_map.55), calls=%async_computation | async-start | bytes 4194304 | tf_op jit(solution)/shard_map/all_to_all | solution.py:386
  30.3 35.2 %collective-permute-start.6 = (bf16[384,256]{1,0:T(8,128)(2,1)}, bf16[384,256]{1,0:T(8,128)(2,1)S(1)}, u32[]{:S(2)}, u32[]{:S(2)}) collective-permute-start(bf16[384,256]{1,0:T(8,128)(2,1)} %get-tuple-element.42), channel_id=1, source_target_pairs={{0,1},{1,0},{2,3},{3,2},{4,5},{5,4},{6,7},{7,6},{8,9},{9,8},{10,11... | collective-permute-start | bytes 589832 | tf_op jit(solution)/shard_map/ppermute | solution.py:390
  31.9 35.0 %collective-permute-start.7 = (bf16[384,256]{1,0:T(8,128)(2,1)}, bf16[384,256]{1,0:T(8,128)(2,1)S(1)}, u32[]{:S(2)}, u32[]{:S(2)}) collective-permute-start(bf16[384,256]{1,0:T(8,128)(2,1)} %get-tuple-element.43), channel_id=1, source_target_pairs={{0,2},{1,3},{2,0},{3,1},{4,6},{5,7},{6,4},{7,5},{8,10},{9,11},{10,... | collective-permute-start | bytes 589832 | tf_op jit(solution)/shard_map/ppermute | solution.py:390
  33.4 35.1 %collective-permute-start.8 = (bf16[384,256]{1,0:T(8,128)(2,1)}, bf16[384,256]{1,0:T(8,128)(2,1)}, u32[]{:S(2)}, u32[]{:S(2)}) collective-permute-start(bf16[384,256]{1,0:T(8,128)(2,1)} %get-tuple-element.44), channel_id=1, source_target_pairs={{0,3},{1,2},{2,1},{3,0},{4,7},{5,6},{6,5},{7,4},{8,11},{9,10},{10,... | collective-permute-start | bytes 589832 | tf_op jit(solution)/shard_map/ppermute | solution.py:390
  33.7 19.3 %collective-permute-start.5 = (bf16[2048,256]{1,0:T(8,128)(2,1)}, bf16[2048,256]{1,0:T(8,128)(2,1)S(1)}, u32[]{:S(2)}, u32[]{:S(2)}) collective-permute-start(bf16[2048,256]{1,0:T(8,128)(2,1)} %collective-permute-done.3.rest_0_), channel_id=1, source_target_pairs={{8,16},{12,20},{16,24},{20,28},{9,17},{13,21},{17,25},{21,29},{10,... | collective-permute-start | bytes 3145736 | tf_op jit(solution)/shard_map/ppermute | solution.py:395
  34.5 29.4 %collective-permute-start.4 = (bf16[2048,256]{1,0:T(8,128)(2,1)}, bf16[2048,256]{1,0:T(8,128)(2,1)}, u32[]{:S(2)}, u32[]{:S(2)}) collective-permute-start(bf16[2048,256]{1,0:T(8,128)(2,1)} %collective-permute-done.2.rest_1_.rest_2_), channel_id=1, source_target_pairs={{8,0},{12,4},{16,8},{20,12},{9,1},{13,5},{17,9},{21,13},{10,2},{14... | collective-permute-start | bytes 3145736 | tf_op jit(solution)/shard_map/ppermute | solution.py:395
  49.5 28.0 %all-to-all-start.1 = ((bf16[4,1024,128]{2,1,0:T(8,128)(2,1)}), bf16[4,1024,128]{2,1,0:T(8,128)(2,1)S(1)}, u32[]{:S(2)}, u32[]{:S(2)}) async-start(bf16[4,1024,128]{2,1,0:T(8,128)(2,1)} %shard_map.56.rest_1_), calls=%async_computation.1 | async-start | bytes 2097152 | tf_op jit(solution)/shard_map/all_to_all | solution.py:386
  53.1 24.4 %collective-permute-start.9 = (bf16[384,256]{1,0:T(8,128)(2,1)}, bf16[384,256]{1,0:T(8,128)(2,1)S(1)}, u32[]{:S(2)}, u32[]{:S(2)}) collective-permute-start(bf16[384,256]{1,0:T(8,128)(2,1)} %get-tuple-element.47), channel_id=1, source_target_pairs={{0,1},{1,0},{2,3},{3,2},{4,5},{5,4},{6,7},{7,6},{8,9},{9,8},{10,11... | collective-permute-start | bytes 589832 | tf_op jit(solution)/shard_map/ppermute | solution.py:390
  63.9 13.6 %collective-permute-start.10 = (bf16[384,256]{1,0:T(8,128)(2,1)}, bf16[384,256]{1,0:T(8,128)(2,1)S(1)}, u32[]{:S(2)}, u32[]{:S(2)}) collective-permute-start(bf16[384,256]{1,0:T(8,128)(2,1)} %get-tuple-element.48), channel_id=1, source_target_pairs={{0,2},{1,3},{2,0},{3,1},{4,6},{5,7},{6,4},{7,5},{8,10},{9,11},{10,... | collective-permute-start | bytes 589832 | tf_op jit(solution)/shard_map/ppermute | solution.py:390
  65.4 12.0 %collective-permute-start.11 = (bf16[384,256]{1,0:T(8,128)(2,1)}, bf16[384,256]{1,0:T(8,128)(2,1)S(1)}, u32[]{:S(2)}, u32[]{:S(2)}) collective-permute-start(bf16[384,256]{1,0:T(8,128)(2,1)} %get-tuple-element.49), channel_id=1, source_target_pairs={{0,3},{1,2},{2,1},{3,0},{4,7},{5,6},{6,5},{7,4},{8,11},{9,10},{10,... | collective-permute-start | bytes 589832 | tf_op jit(solution)/shard_map/ppermute | solution.py:390
  66.9 31.2 %collective-permute-start.13 = (bf16[2048,256]{1,0:T(8,128)(2,1)S(1)}, bf16[2048,256]{1,0:T(8,128)(2,1)}, u32[]{:S(2)}, u32[]{:S(2)}) collective-permute-start(bf16[2048,256]{1,0:T(8,128)(2,1)S(1)} %collective-permute-done.5.rest_1_.rest_0_), channel_id=1, source_target_pairs={{16,24},{20,28},{17,25},{21,29},{18,26},{22,30},{19,27},{23,31}} | collective-permute-start | bytes 3145736 | tf_op jit(solution)/shard_map/ppermute | solution.py:395
  68.5 29.6 %collective-permute-start.14 = (bf16[2048,256]{1,0:T(8,128)(2,1)}, bf16[2048,256]{1,0:T(8,128)(2,1)}, u32[]{:S(2)}, u32[]{:S(2)}) collective-permute-start(bf16[2048,256]{1,0:T(8,128)(2,1)} %collective-permute-done.4.rest_3_.rest_2_), channel_id=1, source_target_pairs={{8,0},{12,4},{9,1},{13,5},{10,2},{14,6},{11,3},{15,7}} | collective-permute-start | bytes 3145736 | tf_op jit(solution)/shard_map/ppermute | solution.py:395
  88.2 9.9 %all-to-all-start.2 = ((f32[4,96,128]{2,1,0:T(8,128)}), f32[4,96,128]{2,1,0:T(8,128)S(1)}, u32[]{:S(2)}, u32[]{:S(2)}) async-start(f32[4,96,128]{2,1,0:T(8,128)} %shard_map.60), calls=%async_computation.2 | async-start | bytes 393216 | tf_op jit(solution)/shard_map/all_to_all | solution.py:386
  92.2 15.0 %collective-permute-start.18 = (bf16[384,256]{1,0:T(8,128)(2,1)S(1)}, bf16[384,256]{1,0:T(8,128)(2,1)S(1)}, u32[]{:S(2)}, u32[]{:S(2)}) collective-permute-start(bf16[384,256]{1,0:T(8,128)(2,1)S(1)} %copy-done.24), channel_id=1, source_target_pairs={{0,1},{1,0},{2,3},{3,2},{4,5},{5,4},{6,7},{7,6},{8,9},{9,8},{10,11... | collective-permute-start | bytes 589832 | tf_op jit(solution)/shard_map/ppermute | solution.py:390
  94.1 21.1 %collective-permute-start.19 = (bf16[384,256]{1,0:T(8,128)(2,1)S(1)}, bf16[384,256]{1,0:T(8,128)(2,1)S(1)}, u32[]{:S(2)}, u32[]{:S(2)}) collective-permute-start(bf16[384,256]{1,0:T(8,128)(2,1)S(1)} %copy-done.23), channel_id=1, source_target_pairs={{0,2},{1,3},{2,0},{3,1},{4,6},{5,7},{6,4},{7,5},{8,10},{9,11},{10,... | collective-permute-start | bytes 589832 | tf_op jit(solution)/shard_map/ppermute | solution.py:390
  95.6 19.7 %collective-permute-start.20 = (bf16[384,256]{1,0:T(8,128)(2,1)S(1)}, bf16[384,256]{1,0:T(8,128)(2,1)S(1)}, u32[]{:S(2)}, u32[]{:S(2)}) collective-permute-start(bf16[384,256]{1,0:T(8,128)(2,1)S(1)} %copy-done.22), channel_id=1, source_target_pairs={{0,3},{1,2},{2,1},{3,0},{4,7},{5,6},{6,5},{7,4},{8,11},{9,10},{10,... | collective-permute-start | bytes 589832 | tf_op jit(solution)/shard_map/ppermute | solution.py:390
  98.1 9.8 %collective-permute-start.12 = (f32[4,96,128]{2,1,0:T(8,128)S(1)}, f32[4,96,128]{2,1,0:T(8,128)S(1)}, u32[]{:S(2)}, u32[]{:S(2)}) collective-permute-start(f32[4,96,128]{2,1,0:T(8,128)S(1)} %all-to-all-done.2.mine_ref.rest_4_), channel_id=1, source_target_pairs={{0,4},{4,0},{8,12},{12,8},{16,20},{20,16},{24,28},{28,24},{1,5},{5... | collective-permute-start | bytes 589832 | tf_op jit(solution)/shard_map/ppermute | solution.py:383
  106.2 14.6 %collective-permute-start.15 = (bf16[384,256]{1,0:T(8,128)(2,1)}, bf16[384,256]{1,0:T(8,128)(2,1)S(1)}, u32[]{:S(2)}, u32[]{:S(2)}) collective-permute-start(bf16[384,256]{1,0:T(8,128)(2,1)} %get-tuple-element.51), channel_id=1, source_target_pairs={{0,1},{1,0},{2,3},{3,2},{4,5},{5,4},{6,7},{7,6},{8,9},{9,8},{10,11... | collective-permute-start | bytes 589832 | tf_op jit(solution)/shard_map/ppermute | solution.py:390
  107.2 13.7 %collective-permute-start.16 = (bf16[384,256]{1,0:T(8,128)(2,1)}, bf16[384,256]{1,0:T(8,128)(2,1)S(1)}, u32[]{:S(2)}, u32[]{:S(2)}) collective-permute-start(bf16[384,256]{1,0:T(8,128)(2,1)} %get-tuple-element.52), channel_id=1, source_target_pairs={{0,2},{1,3},{2,0},{3,1},{4,6},{5,7},{6,4},{7,5},{8,10},{9,11},{10,... | collective-permute-start | bytes 589832 | tf_op jit(solution)/shard_map/ppermute | solution.py:390
  107.9 13.0 %collective-permute-start.17 = (bf16[384,256]{1,0:T(8,128)(2,1)}, bf16[384,256]{1,0:T(8,128)(2,1)S(1)}, u32[]{:S(2)}, u32[]{:S(2)}) collective-permute-start(bf16[384,256]{1,0:T(8,128)(2,1)} %get-tuple-element.53), channel_id=1, source_target_pairs={{0,3},{1,2},{2,1},{3,0},{4,7},{5,6},{6,5},{7,4},{8,11},{9,10},{10,... | collective-permute-start | bytes 589832 | tf_op jit(solution)/shard_map/ppermute | solution.py:390
  (29 other events, 118.1 us)

commit v4 on v3

v4 whole, which is shorter than its diff:
```python
import functools

import jax
import jax.numpy as jnp
from jax import lax
from jax.experimental import pallas as pl
from jax.experimental.pallas import tpu as pltpu
from jax.sharding import PartitionSpec as P

ADAPTER_SCALE = 2.0
CORES = 2
LANES = 128
COVER = 64
VMEM_BYTES = 60 * 1024 * 1024
ANYWHERE = pl.BlockSpec(memory_space=pl.ANY)
WHOLE = pl.BlockSpec(memory_space=pltpu.VMEM)
SCALARS = pl.BlockSpec(memory_space=pltpu.SMEM)


def params():
    return pltpu.CompilerParams(vmem_limit_bytes=VMEM_BYTES)


def cost(flops, bytes_accessed):
    return pl.CostEstimate(flops=flops, bytes_accessed=bytes_accessed, transcendentals=0)


def start_all(pairs, sems):
    copies = [pltpu.make_async_copy(src, dst, sems.at[n]) for n, (src, dst) in enumerate(pairs)]
    for copy in copies:
        copy.start()
    return copies


def load_all(pairs, sems):
    for copy in start_all(pairs, sems):
        copy.wait()


def base_kernel(mp_count, count, kept, at, info_ref, mine_ref, other_ref, *rest):
    choices = rest[:count]
    weight, done, own, sems = rest[-4:] if kept else [*rest[-5:-4], *rest[-3:]]
    outs = rest[-4 - mp_count : -4] if kept else rest[-5 - mp_count : -5]
    rows = own.shape[0] // CORES
    for number, choice in enumerate(choices):

        @pl.when(info_ref[at] == number)
        def _(choice=choice):
            pltpu.make_async_copy(choice, weight, sems.at[0]).start()

    order = [(number, part) for number in reversed(range(mp_count)) for part in range(CORES)]
    blocks, copies = {}, []
    for number, part in order:
        place = pl.ds(pl.multiple_of((info_ref[0] ^ number) * rows, rows), rows)
        source = (mine_ref, other_ref)[part].at[place, :]
        n = CORES * number + part
        blocks[n] = source if kept else rest[-4].at[n]
        if not kept:
            copies.append(pltpu.make_async_copy(source, blocks[n], sems.at[1 + n]))
            copies[-1].start()
    pltpu.make_async_copy(choices[0], weight, sems.at[0]).wait()
    stores = []
    for turn, (number, part) in enumerate(order):
        if not kept:
            copies[turn].wait()
        target = done.at[number] if number else own
        product = jnp.dot(blocks[CORES * number + part][...], weight[...], preferred_element_type=jnp.float32)
        target[part * rows : (part + 1) * rows, :] = product.astype(target.dtype)
        if part:
            stores.append(pltpu.make_async_copy(target, outs[number], sems.at[1 + CORES * mp_count + number]))
            stores[-1].start()
    for store in stores:
        store.wait()


def base_products(info, at, mine, other, choices, mp_count, kept, *before):
    group_rows, features = mine.shape
    rows, span = group_rows // mp_count, choices[0].shape[1]
    return pl.pallas_call(
        functools.partial(base_kernel, mp_count, len(choices), kept, at),
        in_specs=[SCALARS] + [WHOLE if kept else ANYWHERE] * 2 + [ANYWHERE] * (len(choices) + len(before)),
        out_specs=[ANYWHERE] * mp_count,
        scratch_shapes=[pltpu.VMEM((features, span), mine.dtype)]
        + ([] if kept else [pltpu.VMEM((CORES * mp_count, rows, features), mine.dtype)])
        + [
            pltpu.VMEM((mp_count, CORES * rows, span), jnp.bfloat16),
            pltpu.VMEM((CORES * rows, span), jnp.float32),
            pltpu.SemaphoreType.DMA((1 + (1 + CORES) * mp_count,)),
        ],
        out_shape=[
            jax.ShapeDtypeStruct((CORES * rows, span), jnp.bfloat16 if number else jnp.float32)
            for number in range(mp_count)
        ],
        compiler_params=pltpu.CompilerParams(vmem_limit_bytes=VMEM_BYTES // 4 if kept else VMEM_BYTES),
        cost_estimate=cost(
            COVER * 2 * CORES * group_rows * features * span,
            2 * (CORES * group_rows * (features + span) + features * span),
        ),
    )(info, mine, other, *choices, *before)


def cut_down_kernel(info_ref, down_ref, out, block, sems):
    mp_count, features, lanes = block.shape
    mine = pl.ds(pl.multiple_of(info_ref[1] * lanes, lanes), lanes)
    loads = start_all(
        [(down_ref.at[n * features : (n + 1) * features, mine], block.at[n]) for n in range(mp_count)], sems
    )
    stores = []
    for n, load in enumerate(loads):
        load.wait()
        stores.append(pltpu.make_async_copy(block.at[n], out.at[n], sems.at[mp_count + n]))
        stores[-1].start()
    for store in stores:
        store.wait()


def cut_down(info, down, mp_count):
    shape = mp_count, down.shape[0] // mp_count, down.shape[1] // CORES
    return pl.pallas_call(
        cut_down_kernel,
        in_specs=[SCALARS, ANYWHERE],
        out_specs=ANYWHERE,
        out_shape=jax.ShapeDtypeStruct(shape, down.dtype),
        scratch_shapes=[pltpu.VMEM(shape, down.dtype), pltpu.SemaphoreType.DMA((2 * mp_count,))],
        compiler_params=params(),
        cost_estimate=cost(0, 2 * down.size),
    )(info, down)


def cut_up_kernel(width, info_ref, up_ref, out, block, sems):
    parts, ranks, span = up_ref.shape
    lanes = block.shape[1]
    pairs = []
    for part in range(parts):
        for place in range(0, span, CORES * width):
            for first in range(place, place + width, lanes):
                columns = pl.ds(pl.multiple_of(first + info_ref[1] * width, lanes), lanes)
                row = len(pairs) * ranks
                pairs.append((up_ref.at[part, :, columns], block.at[row : row + ranks, :]))
    load_all(pairs, sems)
    load_all([(block, out.at[n]) for n in range(out.shape[0])], sems)


def cut_up(info, up, mp_count, width, lanes):
    parts, ranks, span = up.shape
    blocks = parts * span // CORES // lanes
    return pl.pallas_call(
        functools.partial(cut_up_kernel, width),
        in_specs=[SCALARS, ANYWHERE],
        out_specs=ANYWHERE,
        out_shape=jax.ShapeDtypeStruct((mp_count, blocks * ranks, lanes), up.dtype),
        scratch_shapes=[
            pltpu.VMEM((blocks * ranks, lanes), up.dtype),
            pltpu.SemaphoreType.DMA((max(blocks, mp_count),)),
        ],
        compiler_params=params(),
        cost_estimate=cost(0, 4 * mp_count * blocks * ranks * lanes),
    )(info, up)


def low_kernel(adapters, rank_pair, info_ref, mine_ref, other_ref, mine_ids, other_ids, maps_ref, out, maps, sems):
    mp_count, features, lanes = maps.shape
    rows = mine_ref.shape[0] // mp_count
    load_all([(maps_ref.at[number, :features, :], maps.at[number]) for number in range(mp_count)], sems)
    lane_adapter = lax.broadcasted_iota(jnp.int32, (rows, lanes), 1) // rank_pair
    groups = lanes // rank_pair
    depth = CORES * rows // groups
    lane_group = lax.broadcasted_iota(jnp.int32, (depth, lanes), 1) // rank_pair
    for number in range(mp_count):
        halves = []
        for part in range(CORES):
            place = slice(number * rows, (number + 1) * rows)
            ids = (mine_ids, other_ids)[part][place, :]
            values = (mine_ref, other_ref)[part][place, :]
            total = jnp.zeros((rows, lanes), jnp.float32)
            for owner in range(0, mp_count, CORES):
                both = jnp.concatenate([maps[owner], maps[owner + 1]], axis=1)
                product = jnp.dot(values, both, preferred_element_type=jnp.float32)
                for m in range(CORES):
                    wanted = ids - (owner + m) * adapters - info_ref[1] * groups
                    total += jnp.where(lane_adapter == wanted, product[:, m * lanes : (m + 1) * lanes], 0.0)
            shift = lanes // 2
            while shift >= rank_pair:
                total = total + pltpu.roll(total, shift, 1)
                shift //= 2
            halves.append(total)
        both = jnp.concatenate(halves, axis=0)
        packed = jnp.zeros((depth, lanes), jnp.float32)
        for group in range(groups):
            packed += jnp.where(lane_group == group, both[group * depth : (group + 1) * depth, :], 0.0)
        out[number] = packed


def low_sums(info, mine, other, ids, maps, adapters, rank):
    group_rows, features = mine.shape
    mp_count, _, lanes = maps.shape
    rows = group_rows // mp_count
    depth = CORES * rows * 2 * rank // lanes
    return pl.pallas_call(
        functools.partial(low_kernel, adapters, 2 * rank),
        in_specs=[SCALARS] + [WHOLE] * 4 + [ANYWHERE],
        out_specs=WHOLE,
        out_shape=jax.ShapeDtypeStruct((mp_count, depth, lanes), jnp.float32),
        scratch_shapes=[pltpu.VMEM((mp_count, features, lanes), maps.dtype), pltpu.SemaphoreType.DMA((mp_count,))],
        compiler_params=pltpu.CompilerParams(vmem_limit_bytes=VMEM_BYTES // 4),
        cost_estimate=cost(
            2 * CORES * group_rows * features * mp_count * lanes, 2 * features * (CORES * group_rows + mp_count * lanes)
        ),
    )(info, mine, other, *ids, maps)


def delta_kernel(adapters, rank, info_ref, mine_ids, other_ids, mine_ref, other_ref, maps_ref, out, maps, sem):
    copy = pltpu.make_async_copy(maps_ref.at[:, maps_ref.shape[1] - maps.shape[1] :, :], maps, sem)
    copy.start()
    mp_count = maps.shape[0]
    planes, rows, span = out.shape
    lanes = mine_ref.shape[2]
    rank_pair = 2 * rank
    groups = lanes // rank_pair
    depth = rows // groups
    packed = sum(mine_ref[n] for n in range(mp_count))
    packed = packed + pltpu.roll(sum(other_ref[n] for n in range(mp_count)), lanes // 2, 1)
    lane_group = lax.broadcasted_iota(jnp.int32, (depth, lanes), 1) // rank_pair
    spread = []
    for group in range(groups):
        values = jnp.where(lane_group == group, packed, 0.0)
        shift = lanes // 2
        while shift >= rank_pair:
            values = values + pltpu.roll(values, shift, 1)
            shift //= 2
        spread.append(values)
    low = jnp.concatenate(spread, axis=0)
    place = pl.ds(pl.multiple_of(info_ref[0] * (rows // CORES), rows // CORES), rows // CORES)
    ids = jnp.concatenate([mine_ids[place, :], other_ids[place, :]], axis=0)
    lane_block = lax.broadcasted_iota(jnp.int32, (rows, lanes), 1) // rank
    even = lane_block % 2 == 0
    lows = [jnp.where(even, low, pltpu.roll(low, rank, 1)), jnp.where(even, pltpu.roll(low, lanes - rank, 1), low)]
    copy.wait()
    ranks = adapters * rank
    for part in range(2):
        spreads = [
            jnp.where(lane_block == ids - owner * adapters, lows[part], 0.0).astype(jnp.bfloat16)
            for owner in range(mp_count)
        ]
        for plane in range(part * planes // 2, (part + 1) * planes // 2):
            for piece in range(span // lanes):
                first = (plane * (span // lanes) + piece) * ranks
                total = jnp.zeros((rows, lanes), jnp.float32)
                for owner in range(mp_count):
                    weights = maps[owner, first : first + ranks, :]
                    total += jnp.dot(spreads[owner], weights, preferred_element_type=jnp.float32)
                out[plane, :, piece * lanes : (piece + 1) * lanes] = (ADAPTER_SCALE * total).astype(out.dtype)


def deltas_of(info, ids, mine, other, maps, adapters, rank, planes, span):
    mp_count, _, lanes = maps.shape
    rows = CORES * ids[0].shape[0] // mp_count
    depth = planes * span // lanes * adapters * rank
    return pl.pallas_call(
        functools.partial(delta_kernel, adapters, rank),
        in_specs=[SCALARS] + [WHOLE] * 4 + [ANYWHERE],
        out_specs=WHOLE,
        out_shape=jax.ShapeDtypeStruct((planes, rows, span), jnp.bfloat16),
        scratch_shapes=[pltpu.VMEM((mp_count, depth, lanes), maps.dtype), pltpu.SemaphoreType.DMA],
        compiler_params=params(),
        cost_estimate=cost(2 * rows * mp_count * depth * lanes, 2 * mp_count * depth * lanes),
    )(info, *ids, mine, other, maps)


def finish_kernel(mp_count, places, info_ref, delta_ref, *rest):
    turns = len(places)
    parts, (delta, own, others, done, sems) = rest[: mp_count * turns], rest[-5:]
    out, *away = rest[-6 - turns : -5]
    rows, span = away[0].shape
    each = mp_count + 1
    loads = []
    for turn in range(turns):
        first, *peers = parts[mp_count * turn : mp_count * (turn + 1)]
        pairs = [(first, own.at[turn]), (delta_ref.at[info_ref[places[turn]]], delta.at[turn])]
        pairs += [(part, others.at[turn, n]) for n, part in enumerate(peers)]
        loads.append(start_all(pairs, sems.at[pl.ds(turn * each, each)]))
    stores = []
    for turn in range(turns):
        for load in loads[turn]:
            load.wait()
        total = own[turn]
        for n in range(mp_count - 1):
            total = total + others[turn, n].astype(jnp.float32)
        done[turn] = (total + delta[turn].astype(jnp.float32)).astype(done.dtype)
        place = pl.ds(pl.multiple_of(info_ref[places[turn] + 1] * span, span), span)
        pairs = [(done.at[turn, rows:, :], away[turn]), (done.at[turn, :rows, :], out.at[:, place])]
        stores += start_all(pairs, sems.at[pl.ds(turns * each + 2 * turn, 2)])
    for store in stores:
        store.wait()


def finish(info, places, delta, parts, held, width):
    turns, mp_count = len(parts), len(parts[0])
    rows, span = parts[0][0].shape
    operands = [info, delta, *sum(parts, [])] + ([] if held is None else [held])
    away = jax.ShapeDtypeStruct((rows // CORES, span), delta.dtype)
    return pl.pallas_call(
        functools.partial(finish_kernel, mp_count, places),
        in_specs=[SCALARS] + [ANYWHERE] * (len(operands) - 1),
        out_specs=[ANYWHERE] * (1 + turns),
        out_shape=[jax.ShapeDtypeStruct((rows // CORES, width), delta.dtype)] + [away] * turns,
        scratch_shapes=[
            pltpu.VMEM((turns, rows, span), delta.dtype),
            pltpu.VMEM((turns, rows, span), jnp.float32),
            pltpu.VMEM((turns, mp_count - 1, rows, span), delta.dtype),
            pltpu.VMEM((turns, rows, span), delta.dtype),
            pltpu.SemaphoreType.DMA((turns * (mp_count + 3),)),
        ],
        input_output_aliases={} if held is None else {len(operands) - 1: 0},
        compiler_params=params(),
        cost_estimate=cost(4 * rows * span * turns, 12 * rows * span * turns),
    )(*operands)


def settle_kernel(places, info_ref, *rest):
    pieces, (out, sems) = rest[:-3], rest[-2:]
    span = pieces[0].shape[1]
    load_all(
        [
            (piece, out.at[:, pl.ds(pl.multiple_of(info_ref[places[n]] * span, span), span)])
            for n, piece in enumerate(pieces)
        ],
        sems,
    )


def settle(info, places, pieces, held):
    operands = [info, *pieces, held]
    return pl.pallas_call(
        functools.partial(settle_kernel, places),
        in_specs=[SCALARS] + [WHOLE] * len(pieces) + [ANYWHERE],
        out_specs=ANYWHERE,
        out_shape=jax.ShapeDtypeStruct(held.shape, held.dtype),
        scratch_shapes=[pltpu.SemaphoreType.DMA((len(pieces),))],
        input_output_aliases={len(operands) - 1: 0},
        compiler_params=params(),
        cost_estimate=cost(0, 4 * len(pieces) * pieces[0].size),
    )(*operands)


def by_plane(plane, values):
    return sum(jnp.where(plane == n, value, 0) for n, value in enumerate(values)).astype(jnp.int32)


def arrival_order(plane, planes):
    sides = (1, -1) if 2 * plane < planes else (-1, 1)
    return [
        (side, distance)
        for distance in range(1, planes)
        for side in sides
        if 0 <= plane + side * distance < planes
    ]


def local(tokens, frozen_weight, adapter_down_weight, adapter_up_weight, token_adapter_index):
    mp_count, dp_count = lax.axis_size("mp"), lax.axis_size("dp")
    position, replica = lax.axis_index("mp"), lax.axis_index("dp")
    planes = dp_count // CORES
    plane, core = replica // CORES, replica % CORES
    group_rows, features = tokens.shape
    rows = group_rows // mp_count
    width = frozen_weight.shape[1]
    adapters, rank, up_span = adapter_up_weight.shape[1:]
    ranks = adapters * rank

    def after_all(*arrays):
        return lax.optimization_barrier(arrays)

    def swap(array):
        return lax.ppermute(array, "dp", [(n, n ^ 1) for n in range(dp_count)])

    def trade(array):
        return lax.all_to_all(array, "mp", 0, 0)

    def pass_round(blocks):
        return [
            lax.ppermute(block, "mp", [(m, m ^ n) for m in range(mp_count)]) for n, block in enumerate(blocks, 1)
        ]

    def hop(array, side, step):
        sources = range(1, planes - step + 1) if side > 0 else range(step - 1, planes - 1)
        return lax.ppermute(
            array, "dp", [(CORES * n + m, CORES * (n - side) + m) for n in sources for m in range(CORES)]
        )

    got = {(side, 1): hop(frozen_weight, side, 1) for side in (1, -1)}
    other = swap(tokens)
    ids = token_adapter_index.reshape(group_rows, 1)
    ids = [ids, swap(token_adapter_index).reshape(group_rows, 1)]

    orders = [[(0, 0)] + arrival_order(n, planes) for n in range(planes)]
    options = [sorted({order[turn] for order in orders}) for turn in range(planes)]
    scalars = [position, core]
    choice_at, group_at = [], []
    for turn in range(planes):
        wanted = [order[turn] for order in orders]
        choice_at.append(len(scalars))
        scalars.append(by_plane(plane, [options[turn].index(item) for item in wanted]))
        group = by_plane(plane, [n + side * distance for n, (side, distance) in enumerate(wanted)])
        group_at.append(len(scalars))
        scalars += [group, CORES * group + core, CORES * group + 1 - core]
    info = jnp.stack([jnp.asarray(value, jnp.int32) for value in scalars])

    down = trade(cut_down(info, adapter_down_weight, mp_count))
    up = cut_up(info, adapter_up_weight.reshape(2, ranks, up_span), mp_count, width, down.shape[2])
    own, *sent = base_products(info, choice_at[0], tokens, other, [frozen_weight], mp_count, False, up, *ids)
    finished, out, away = [], None, []

    def finish_some(turns, out):
        places = [group_at[turn] for turn in turns]
        return finish(info, places, delta, [finished[turn] for turn in turns], out, dp_count * width)

    for turn in range(1, planes):
        last = turn == planes - 1
        if not last:
            got[1, turn], got[-1, turn], own = after_all(got[1, turn], got[-1, turn], own)
            for side in (1, -1):
                got[side, turn + 1] = hop(got[side, turn], side, turn + 1)
        finished.append([own] + pass_round(sent))
        before = []
        if turn == 1:
            sums = low_sums(info, tokens, other, ids, down, adapters, rank)
            before = [sums, *finished[0][1:]]
        elif turn == 2:
            up = trade(up)
            before = [up]
        if last:
            sums, finished[-1][0], *finished[-2][1:] = after_all(sums, own, *finished[-2][1:])
            sums = trade(sums)
            delta = deltas_of(info, ids, sums, swap(sums), up, adapters, rank, planes, width)
            before = [delta]
        shards = [got[option] for option in options[turn]]
        kept = turn == 1 or last
        own, *sent = base_products(info, choice_at[turn], tokens, other, shards, mp_count, kept, *before)
    finished.append([own] + pass_round(sent))

    for turns in (range(planes - 2), [planes - 2], [planes - 1]):
        out, *pieces = finish_some(turns, out)
        away += pieces
    away = [swap(piece) for piece in away]
    places = [at + 2 for at in group_at]
    out = settle(info, places[:-1], away[:-1], out)
    return settle(info, places[-1:], away[-1:], out)


def solution(mesh):
    placed = (P("dp", "mp"), P("mp", "dp"), P(None, "mp"), P(None, "mp", None, None), P("dp"))
    return jax.shard_map(
        local, mesh=mesh, in_specs=placed, out_specs=P(("dp", "mp"), None), check_vma=False
    )
```

time: 132 us -> 123 us (0.932)
  waiting for transfers between devices: 19.5 us -> 10 us
  blocking collectives: 0 us -> 9.33 us
  starting transfers between devices: 40.6 us -> 36.8 us
  other arithmetic: 3.69 us -> 0 us
  Pallas kernels: 57.5 us -> 54.8 us
    all_to_all x0 -> x1, blocking collectives: none -> 9.33 us  [trade(): return lax.all_to_all(array, 'mp', 0, 0)]
    ppermute x6, waiting for transfers between devices: 12 us -> 3.47 us  [hop(): lax.ppermute(array, 'dp', [(CORES * n + m, CORES * (n - side) + m) for n...]
    pallas_call x1, Pallas kernels: 9.54 us -> 5.69 us  [low_sums(): pl.pallas_call(functools.partial(low_kernel, adapters, 2 * rank), in_spec...]
    another operation x6 -> x0, other arithmetic: 3.69 us -> none  [info_of(): return jnp.stack([jnp.asarray(value, jnp.int32) for value in values])]
    all_to_all x3 -> x2, starting transfers between devices: 10.8 us -> 8.17 us  [trade(): return lax.all_to_all(array, 'mp', 0, 0)]
    all_to_all x3 -> x2, waiting for transfers between devices: 7.4 us -> 5.26 us  [trade(): return lax.all_to_all(array, 'mp', 0, 0)]
    reshape x0 -> x2, local copies, waits for them, and re-layouts: none -> 1.86 us  [the longest x1 0.95 us: local(): ids = [ids, swap(token_adapter_index).reshape(group_rows, 1)]]
    ppermute x12, starting transfers between devices: 15.5 us -> 13.6 us  [pass_round(): lax.ppermute(block, 'mp', [(m, m ^ n) for m in range(mp_count)])]
  transfers between devices with their start and end apart: 28 -> 27, of which waited for: 5 -> 6; matrix products, arithmetic and copies ran while one was open for 4% -> 2% of each run, Pallas kernels for 43% -> 44%
where the time goes in v4:
time: 123 us; the launch traced here: 121 us
  Pallas kernels  54.8 us (45%)
  starting transfers between devices  36.8 us (30%)
  waiting for transfers between devices  10 us (8%)
  blocking collectives  9.33 us (8%)
  local copies, waits for them, and re-layouts  9.1 us (7%)
    pallas_call x4, Pallas kernels, base_products(): pl.pallas_call(functools.partial(base_kernel, mp_count, len(choices), kep...  27 us
    ppermute x12, starting transfers between devices, pass_round(): lax.ppermute(block, 'mp', [(m, m ^ n) for m in range(mp_count)])  13.6 us
    ppermute x6, starting transfers between devices, hop(): lax.ppermute(array, 'dp', [(CORES * n + m, CORES * (n - side) + m) for n...  13.5 us
    all_to_all x1, blocking collectives, trade(): return lax.all_to_all(array, 'mp', 0, 0)  9.33 us
    pallas_call x3, Pallas kernels, finish(): pl.pallas_call(functools.partial(finish_kernel, mp_count, places), in_spe...  8.71 us
    all_to_all x2, starting transfers between devices, trade(): return lax.all_to_all(array, 'mp', 0, 0)  8.17 us
    unnamed x50, local copies, waits for them, and re-layouts  6.66 us
    pallas_call x1, Pallas kernels, low_sums(): pl.pallas_call(functools.partial(low_kernel, adapters, 2 * rank), in_spec...  5.69 us
  transfers between devices with their start and end apart: 27, of which 6 were waited for; matrix products, arithmetic and copies ran while one was open for 2% of the time, Pallas kernels for 44%

profile of v4, /device:TPU:0, one launch (start us, length us, event | category | flops | bytes accessed | tf_op | source)
XLA Modules:
  0.0 120.7 jit_solution(16870206221692630573)
XLA Ops:
  1.7 6.1 %collective-permute-start.3 = (bf16[2048,256]{1,0:T(8,128)(2,1)}, bf16[2048,256]{1,0:T(8,128)(2,1)}, u32[]{:S(2)}, u32[]{:S(2)}) collective-permute-start(bf16[2048,256]{1,0:T(8,128)(2,1)} %rest_0_.1), channel_id=1, source_target_pairs={{0,8},{4,12},{8,16},{12,20},{16,24},{20,28},{1,9},{5,13},{9,17},{1... | collective-permute-start | bytes 3145736 | tf_op jit(solution)/shard_map/ppermute | solution.py:387
  8.7 3.1 %shard_map.55 = bf16[4,2048,128]{2,1,0:T(8,128)(2,1)} custom-call(s32[18]{0:T(128)} %stack.72.info_ref, bf16[8192,256]{1,0:T(8,128)(2,1)} %down_ref.1), custom_call_target="tpu_custom_call" | custom-call | bytes 4194304 | tf_op jit(solution)/shard_map/pallas_call | solution.py:119
  11.8 3.9 %all-to-all-start = ((bf16[4,2048,128]{2,1,0:T(8,128)(2,1)}), bf16[4,2048,128]{2,1,0:T(8,128)(2,1)S(1)}, u32[]{:S(2)}, u32[]{:S(2)}) async-start(bf16[4,2048,128]{2,1,0:T(8,128)(2,1)} %shard_map.55), calls=%async_computation | async-start | bytes 4194304 | tf_op jit(solution)/shard_map/all_to_all | solution.py:378
  16.7 2.6 %shard_map.57.rest_1_ = bf16[4,1024,128]{2,1,0:T(8,128)(2,1)} custom-call(s32[18]{0:T(128)} %stack.72.info_ref, bf16[2,128,1024]{2,1,0:T(8,128)(2,1)} %bitcast.18), custom_call_target="tpu_custom_call" | custom-call | bytes 2097152 | tf_op jit(solution)/shard_map/pallas_call | solution.py:147
  20.2 7.6 %shard_map.58 = (f32[384,256]{1,0:T(8,128)}, bf16[384,256]{1,0:T(8,128)(2,1)}, bf16[384,256]{1,0:T(8,128)(2,1)}, bf16[384,256]{1,0:T(8,128)(2,1)}) custom-call(s32[18]{0:T(128)} %stack.72.info_ref, bf16[768,2048]{1,0:T(8,128)(2,1)} %mine_ref.9, bf16[768,2048]{1,0:T(8,128)(2,1)} %collective-permute-done.1.other_ref, bf16[2048,256]{1,0:T(8,128)(2,1)} %rest_0_.1, ...), custom_call_target="tpu_custom_call" | custom-call | flops 103079215104 | bytes 8126464 | tf_op jit(solution)/shard_map/pallas_call | solution.py:79
  30.3 1.6 %collective-permute-start.6 = (bf16[384,256]{1,0:T(8,128)(2,1)}, bf16[384,256]{1,0:T(8,128)(2,1)S(1)}, u32[]{:S(2)}, u32[]{:S(2)}) collective-permute-start(bf16[384,256]{1,0:T(8,128)(2,1)} %get-tuple-element.42), channel_id=1, source_target_pairs={{0,1},{1,0},{2,3},{3,2},{4,5},{5,4},{6,7},{7,6},{8,9},{9,8},{10,11... | collective-permute-start | bytes 589832 | tf_op jit(solution)/shard_map/ppermute | solution.py:382
  33.7 1.7 %collective-permute-start.5 = (bf16[2048,256]{1,0:T(8,128)(2,1)}, bf16[2048,256]{1,0:T(8,128)(2,1)}, u32[]{:S(2)}, u32[]{:S(2)}) collective-permute-start(bf16[2048,256]{1,0:T(8,128)(2,1)} %collective-permute-done.3.rest_0_), channel_id=1, source_target_pairs={{8,16},{12,20},{16,24},{20,28},{9,17},{13,21},{17,25},{21,29},{10,... | collective-permute-start | bytes 3145736 | tf_op jit(solution)/shard_map/ppermute | solution.py:387
  36.7 5.3 %all-to-all-done.maps_ref = bf16[4,2048,128]{2,1,0:T(8,128)(2,1)S(1)} async-done(((bf16[4,2048,128]{2,1,0:T(8,128)(2,1)}), bf16[4,2048,128]{2,1,0:T(8,128)(2,1)S(1)}, u32[]{:S(2)}, u32[]{:S(2)}) %all-to-all-start) | async-done | bytes 2097184 | tf_op jit(solution)/shard_map/all_to_all | solution.py:378
  42.0 4.2 %all-to-all-start.1 = ((bf16[4,1024,128]{2,1,0:T(8,128)(2,1)}), bf16[4,1024,128]{2,1,0:T(8,128)(2,1)}, u32[]{:S(2)}, u32[]{:S(2)}) async-start(bf16[4,1024,128]{2,1,0:T(8,128)(2,1)} %shard_map.57.rest_1_), calls=%async_computation.1 | async-start | bytes 2097152 | tf_op jit(solution)/shard_map/all_to_all | solution.py:378
  46.3 1.9 %copy-done.12 = bf16[768,2048]{1,0:T(8,128)(2,1)S(1)} copy-done((bf16[768,2048]{1,0:T(8,128)(2,1)S(1)}, bf16[768,2048]{1,0:T(8,128)(2,1)}, u32[]{:S(2)}) %copy-start.12) | copy-done | bytes 3145752
  48.2 5.7 %shard_map.56.rest_2_ = f32[4,96,128]{2,1,0:T(8,128)S(1)} custom-call(s32[18]{0:T(128)S(1)} %copy-done.10, bf16[768,2048]{1,0:T(8,128)(2,1)S(1)} %copy-done.12, bf16[768,2048]{1,0:T(8,128)(2,1)} %collective-permute-done.1.other_ref, s32[768,1]{1,0:T(8,128)S(1)} %copy-done.1, s32[768,1]{1,0:T(8,128)S(1)} %copy-done.2, ...), custom_call_target="tpu_custom_call" | custom-call | flops 3221225472 | bytes 8388608 | tf_op jit(solution)/shard_map/pallas_call | solution.py:199
  53.9 5.5 %shard_map.59 = (f32[384,256]{1,0:T(8,128)S(1)}, bf16[384,256]{1,0:T(8,128)(2,1)}, bf16[384,256]{1,0:T(8,128)(2,1)}, bf16[384,256]{1,0:T(8,128)(2,1)}) custom-call(s32[18]{0:T(128)S(1)} %copy-done.10, bf16[768,2048]{1,0:T(8,128)(2,1)S(1)} %copy-done.12, bf16[768,2048]{1,0:T(8,128)(2,1)} %collective-permute-done.1.other_ref, ...), custom_call_target="tpu_custom_call" | custom-call | flops 103079215104 | bytes 8126464 | tf_op jit(solution)/shard_map/pallas_call | solution.py:79
  60.3 2.0 %collective-permute-start.9 = (bf16[384,256]{1,0:T(8,128)(2,1)}, bf16[384,256]{1,0:T(8,128)(2,1)}, u32[]{:S(2)}, u32[]{:S(2)}) collective-permute-start(bf16[384,256]{1,0:T(8,128)(2,1)} %get-tuple-element.49), channel_id=1, source_target_pairs={{0,1},{1,0},{2,3},{3,2},{4,5},{5,4},{6,7},{7,6},{8,9},{9,8},{10,11... | collective-permute-start | bytes 589832 | tf_op jit(solution)/shard_map/ppermute | solution.py:382
  64.8 1.8 %collective-permute-start.13 = (bf16[2048,256]{1,0:T(8,128)(2,1)}, bf16[2048,256]{1,0:T(8,128)(2,1)}, u32[]{:S(2)}, u32[]{:S(2)}) collective-permute-start(bf16[2048,256]{1,0:T(8,128)(2,1)} %collective-permute-done.5.rest_1_.rest_0_), channel_id=1, source_target_pairs={{16,24},{20,28},{17,25},{21,29},{18,26},{22,30},{19,27},{23,31}} | collective-permute-start | bytes 3145736 | tf_op jit(solution)/shard_map/ppermute | solution.py:387
  67.9 7.4 %shard_map.60 = (f32[384,256]{1,0:T(8,128)}, bf16[384,256]{1,0:T(8,128)(2,1)}, bf16[384,256]{1,0:T(8,128)(2,1)}, bf16[384,256]{1,0:T(8,128)(2,1)}) custom-call(s32[18]{0:T(128)} %stack.72.info_ref, bf16[768,2048]{1,0:T(8,128)(2,1)} %mine_ref.9, bf16[768,2048]{1,0:T(8,128)(2,1)} %collective-permute-done.1.other_ref, ...), custom_call_target="tpu_custom_call" | custom-call | flops 103079215104 | bytes 8126464 | tf_op jit(solution)/shard_map/pallas_call | solution.py:79
  75.4 9.3 %all_to_all.15.mine_ref = f32[4,96,128]{2,1,0:T(8,128)S(1)} all-to-all(f32[4,96,128]{2,1,0:T(8,128)S(1)} %copy-done.9), channel_id=1, replica_groups=mesh['dp'=8,'mp'=4] {'mp'}, dimensions={0} | all-to-all | bytes 393216 | tf_op jit(solution)/shard_map/all_to_all | solution.py:378
  86.2 2.1 %collective-permute-start.20 = (bf16[384,256]{1,0:T(8,128)(2,1)}, bf16[384,256]{1,0:T(8,128)(2,1)}, u32[]{:S(2)}, u32[]{:S(2)}) collective-permute-start(bf16[384,256]{1,0:T(8,128)(2,1)} %get-tuple-element.60), channel_id=1, source_target_pairs={{0,3},{1,2},{2,1},{3,0},{4,7},{5,6},{6,5},{7,4},{8,11},{9,10},{10,... | collective-permute-start | bytes 589832 | tf_op jit(solution)/shard_map/ppermute | solution.py:382
  88.2 4.4 %shard_map.61.rest_4_.delta_ref = bf16[4,384,256]{2,1,0:T(8,128)(2,1)} custom-call(s32[18]{0:T(128)} %stack.72.info_ref, s32[768,1]{1,0:T(8,128)} %reshape.12.mine_ids.rest_2_, s32[768,1]{1,0:T(8,128)} %reshape.13.other_ids.rest_3_, f32[4,96,128]{2,1,0:T(8,128)} %copy-done.14, f32[4,96,128]{2,1,0:T(8,128)} %copy-done.15, ...), custom_call_target="tpu_custom_call" | custom-call | flops 402653184 | bytes 1048576 | tf_op jit(solution)/shard_map/pallas_call | solution.py:259
  93.8 6.5 %shard_map.62 = (f32[384,256]{1,0:T(8,128)S(1)}, bf16[384,256]{1,0:T(8,128)(2,1)S(1)}, bf16[384,256]{1,0:T(8,128)(2,1)S(1)}, bf16[384,256]{1,0:T(8,128)(2,1)S(1)}) custom-call(s32[18]{0:T(128)S(1)} %copy-done.11, bf16[768,2048]{1,0:T(8,128)(2,1)S(1)} %copy-done.13, bf16[768,2048]{1,0:T(8,128)(2,1)} %collective-permute-done.1.other_ref, ...), custom_call_target="tpu_custom_call" | custom-call | flops 103079215104 | bytes 8126464 | tf_op jit(solution)/shard_map/pallas_call | solution.py:79
  102.9 1.6 %collective-permute-start.17 = (bf16[384,256]{1,0:T(8,128)(2,1)S(1)}, bf16[384,256]{1,0:T(8,128)(2,1)S(1)}, u32[]{:S(2)}, u32[]{:S(2)}) collective-permute-start(bf16[384,256]{1,0:T(8,128)(2,1)S(1)} %get-tuple-element.56), channel_id=1, source_target_pairs={{0,3},{1,2},{2,1},{3,0},{4,7},{5,6},{6,5},{7,4},{8,11},{9,10},{10,... | collective-permute-start | bytes 589832 | tf_op jit(solution)/shard_map/ppermute | solution.py:382
  104.6 3.2 %shard_map.63 = (bf16[192,2048]{1,0:T(8,128)(2,1)}, bf16[192,256]{1,0:T(8,128)(2,1)}, bf16[192,256]{1,0:T(8,128)(2,1)}) custom-call(s32[18]{0:T(128)} %stack.72.info_ref, bf16[4,384,256]{2,1,0:T(8,128)(2,1)} %shard_map.61.rest_4_.delta_ref, f32[384,256]{1,0:T(8,128)} %get-tuple-element.61.rest_0_, bf16[384,256]{1,0:T(8,128)(2,1)} %copy-done.5, ...), custom_call_target="tpu_custom_call" | custom-call | flops 786432 | bytes 2359296 | tf_op jit(solution)/shard_map/pallas_call | solution.py:302
  108.4 2.8 %shard_map.64 = (bf16[192,2048]{1,0:T(8,128)(2,1)}, bf16[192,256]{1,0:T(8,128)(2,1)}) custom-call(s32[18]{0:T(128)} %stack.72.info_ref, bf16[4,384,256]{2,1,0:T(8,128)(2,1)} %shard_map.61.rest_4_.delta_ref, f32[384,256]{1,0:T(8,128)} %get-tuple-element.57.rest_0_, bf16[384,256]{1,0:T(8,128)(2,1)} %copy-done.16, ...), custom_call_target="tpu_custom_call", output_to_operand_aliasing={{0}: (6, {})} | custom-call | flops 393216 | bytes 1179648 | tf_op jit(solution)/shard_map/pallas_call | solution.py:302
  113.0 2.8 %shard_map.65 = (bf16[192,2048]{1,0:T(8,128)(2,1)}, bf16[192,256]{1,0:T(8,128)(2,1)}) custom-call(s32[18]{0:T(128)} %stack.72.info_ref, bf16[4,384,256]{2,1,0:T(8,128)(2,1)} %shard_map.61.rest_4_.delta_ref, f32[384,256]{1,0:T(8,128)} %copy-done.4, bf16[384,256]{1,0:T(8,128)(2,1)} %copy-done.17, ...), custom_call_target="tpu_custom_call", output_to_operand_aliasing={{0}: (6, {})} | custom-call | flops 393216 | bytes 1179648 | tf_op jit(solution)/shard_map/pallas_call | solution.py:302
  116.6 1.7 %shard_map.66.rest_1_ = bf16[192,2048]{1,0:T(8,128)(2,1)} custom-call(s32[18]{0:T(128)} %stack.72.info_ref, bf16[192,256]{1,0:T(8,128)(2,1)} %copy-done.20, bf16[192,256]{1,0:T(8,128)(2,1)} %copy-done.21, bf16[192,256]{1,0:T(8,128)(2,1)} %copy-done.22, bf16[192,2048]{1,0:T(8,128)(2,1)} %get-tuple-element.72.rest_3_), custom_call_target="tpu_custom_call", output_to_operand_aliasing={{}: (4, {})} | custom-call | bytes 589824 | tf_op jit(solution)/shard_map/pallas_call | solution.py:334
  (97 shorter events, 25.2 us)
Async XLA Ops:
  0.0 20.2 %collective-permute-start.1 = (bf16[768,2048]{1,0:T(8,128)(2,1)}, bf16[768,2048]{1,0:T(8,128)(2,1)}, u32[]{:S(2)}, u32[]{:S(2)}) collective-permute-start(bf16[768,2048]{1,0:T(8,128)(2,1)} %mine_ref.9), channel_id=1, source_target_pairs={{0,4},{4,0},{8,12},{12,8},{16,20},{20,16},{24,28},{28,24},{1,5},{5... | collective-permute-start | bytes 9437192 | tf_op jit(solution)/shard_map/ppermute | solution.py:375
  0.5 28.6 %collective-permute-start.2 = (bf16[2048,256]{1,0:T(8,128)(2,1)}, bf16[2048,256]{1,0:T(8,128)(2,1)}, u32[]{:S(2)}, u32[]{:S(2)}) collective-permute-start(bf16[2048,256]{1,0:T(8,128)(2,1)} %rest_0_.1), channel_id=1, source_target_pairs={{8,0},{12,4},{16,8},{20,12},{24,16},{28,20},{9,1},{13,5},{17,9},{2... | collective-permute-start | bytes 3145736 | tf_op jit(solution)/shard_map/ppermute | solution.py:387
  1.7 28.5 %collective-permute-start.3 = (bf16[2048,256]{1,0:T(8,128)(2,1)}, bf16[2048,256]{1,0:T(8,128)(2,1)}, u32[]{:S(2)}, u32[]{:S(2)}) collective-permute-start(bf16[2048,256]{1,0:T(8,128)(2,1)} %rest_0_.1), channel_id=1, source_target_pairs={{0,8},{4,12},{8,16},{12,20},{16,24},{20,28},{1,9},{5,13},{9,17},{1... | collective-permute-start | bytes 3145736 | tf_op jit(solution)/shard_map/ppermute | solution.py:387
  7.9 11.4 %collective-permute-start = (s32[768]{0:T(1024)}, s32[768]{0:T(1024)S(1)}, u32[]{:S(2)}, u32[]{:S(2)}) collective-permute-start(s32[768]{0:T(1024)} %param.9), channel_id=1, source_target_pairs={{0,4},{4,0},{8,12},{12,8},{16,20},{20,16},{24,28},{28,24},{1,5},{5... | collective-permute-start | bytes 9224 | tf_op jit(solution)/shard_map/ppermute | solution.py:375
  11.8 30.2 %all-to-all-start = ((bf16[4,2048,128]{2,1,0:T(8,128)(2,1)}), bf16[4,2048,128]{2,1,0:T(8,128)(2,1)S(1)}, u32[]{:S(2)}, u32[]{:S(2)}) async-start(bf16[4,2048,128]{2,1,0:T(8,128)(2,1)} %shard_map.55), calls=%async_computation | async-start | bytes 4194304 | tf_op jit(solution)/shard_map/all_to_all | solution.py:378
  30.3 23.6 %collective-permute-start.6 = (bf16[384,256]{1,0:T(8,128)(2,1)}, bf16[384,256]{1,0:T(8,128)(2,1)S(1)}, u32[]{:S(2)}, u32[]{:S(2)}) collective-permute-start(bf16[384,256]{1,0:T(8,128)(2,1)} %get-tuple-element.42), channel_id=1, source_target_pairs={{0,1},{1,0},{2,3},{3,2},{4,5},{5,4},{6,7},{7,6},{8,9},{9,8},{10,11... | collective-permute-start | bytes 589832 | tf_op jit(solution)/shard_map/ppermute | solution.py:382
  31.9 22.0 %collective-permute-start.7 = (bf16[384,256]{1,0:T(8,128)(2,1)}, bf16[384,256]{1,0:T(8,128)(2,1)S(1)}, u32[]{:S(2)}, u32[]{:S(2)}) collective-permute-start(bf16[384,256]{1,0:T(8,128)(2,1)} %get-tuple-element.43), channel_id=1, source_target_pairs={{0,2},{1,3},{2,0},{3,1},{4,6},{5,7},{6,4},{7,5},{8,10},{9,11},{10,... | collective-permute-start | bytes 589832 | tf_op jit(solution)/shard_map/ppermute | solution.py:382
  33.4 20.5 %collective-permute-start.8 = (bf16[384,256]{1,0:T(8,128)(2,1)}, bf16[384,256]{1,0:T(8,128)(2,1)S(1)}, u32[]{:S(2)}, u32[]{:S(2)}) collective-permute-start(bf16[384,256]{1,0:T(8,128)(2,1)} %get-tuple-element.44), channel_id=1, source_target_pairs={{0,3},{1,2},{2,1},{3,0},{4,7},{5,6},{6,5},{7,4},{8,11},{9,10},{10,... | collective-permute-start | bytes 589832 | tf_op jit(solution)/shard_map/ppermute | solution.py:382
  33.7 30.0 %collective-permute-start.5 = (bf16[2048,256]{1,0:T(8,128)(2,1)}, bf16[2048,256]{1,0:T(8,128)(2,1)}, u32[]{:S(2)}, u32[]{:S(2)}) collective-permute-start(bf16[2048,256]{1,0:T(8,128)(2,1)} %collective-permute-done.3.rest_0_), channel_id=1, source_target_pairs={{8,16},{12,20},{16,24},{20,28},{9,17},{13,21},{17,25},{21,29},{10,... | collective-permute-start | bytes 3145736 | tf_op jit(solution)/shard_map/ppermute | solution.py:387
  35.4 29.3 %collective-permute-start.4 = (bf16[2048,256]{1,0:T(8,128)(2,1)}, bf16[2048,256]{1,0:T(8,128)(2,1)}, u32[]{:S(2)}, u32[]{:S(2)}) collective-permute-start(bf16[2048,256]{1,0:T(8,128)(2,1)} %collective-permute-done.2.rest_1_.rest_2_), channel_id=1, source_target_pairs={{8,0},{12,4},{16,8},{20,12},{9,1},{13,5},{17,9},{21,13},{10,2},{14... | collective-permute-start | bytes 3145736 | tf_op jit(solution)/shard_map/ppermute | solution.py:387
  42.0 25.9 %all-to-all-start.1 = ((bf16[4,1024,128]{2,1,0:T(8,128)(2,1)}), bf16[4,1024,128]{2,1,0:T(8,128)(2,1)}, u32[]{:S(2)}, u32[]{:S(2)}) async-start(bf16[4,1024,128]{2,1,0:T(8,128)(2,1)} %shard_map.57.rest_1_), calls=%async_computation.1 | async-start | bytes 2097152 | tf_op jit(solution)/shard_map/all_to_all | solution.py:378
  60.3 15.1 %collective-permute-start.9 = (bf16[384,256]{1,0:T(8,128)(2,1)}, bf16[384,256]{1,0:T(8,128)(2,1)}, u32[]{:S(2)}, u32[]{:S(2)}) collective-permute-start(bf16[384,256]{1,0:T(8,128)(2,1)} %get-tuple-element.49), channel_id=1, source_target_pairs={{0,1},{1,0},{2,3},{3,2},{4,5},{5,4},{6,7},{7,6},{8,9},{9,8},{10,11... | collective-permute-start | bytes 589832 | tf_op jit(solution)/shard_map/ppermute | solution.py:382
  62.2 13.1 %collective-permute-start.10 = (bf16[384,256]{1,0:T(8,128)(2,1)}, bf16[384,256]{1,0:T(8,128)(2,1)}, u32[]{:S(2)}, u32[]{:S(2)}) collective-permute-start(bf16[384,256]{1,0:T(8,128)(2,1)} %get-tuple-element.50), channel_id=1, source_target_pairs={{0,2},{1,3},{2,0},{3,1},{4,6},{5,7},{6,4},{7,5},{8,10},{9,11},{10,... | collective-permute-start | bytes 589832 | tf_op jit(solution)/shard_map/ppermute | solution.py:382
  63.7 11.7 %collective-permute-start.11 = (bf16[384,256]{1,0:T(8,128)(2,1)}, bf16[384,256]{1,0:T(8,128)(2,1)}, u32[]{:S(2)}, u32[]{:S(2)}) collective-permute-start(bf16[384,256]{1,0:T(8,128)(2,1)} %get-tuple-element.51), channel_id=1, source_target_pairs={{0,3},{1,2},{2,1},{3,0},{4,7},{5,6},{6,5},{7,4},{8,11},{9,10},{10,... | collective-permute-start | bytes 589832 | tf_op jit(solution)/shard_map/ppermute | solution.py:382
  64.8 27.8 %collective-permute-start.13 = (bf16[2048,256]{1,0:T(8,128)(2,1)}, bf16[2048,256]{1,0:T(8,128)(2,1)}, u32[]{:S(2)}, u32[]{:S(2)}) collective-permute-start(bf16[2048,256]{1,0:T(8,128)(2,1)} %collective-permute-done.5.rest_1_.rest_0_), channel_id=1, source_target_pairs={{16,24},{20,28},{17,25},{21,29},{18,26},{22,30},{19,27},{23,31}} | collective-permute-start | bytes 3145736 | tf_op jit(solution)/shard_map/ppermute | solution.py:387
  66.6 26.0 %collective-permute-start.14 = (bf16[2048,256]{1,0:T(8,128)(2,1)}, bf16[2048,256]{1,0:T(8,128)(2,1)}, u32[]{:S(2)}, u32[]{:S(2)}) collective-permute-start(bf16[2048,256]{1,0:T(8,128)(2,1)} %collective-permute-done.4.rest_3_.rest_2_), channel_id=1, source_target_pairs={{8,0},{12,4},{9,1},{13,5},{10,2},{14,6},{11,3},{15,7}} | collective-permute-start | bytes 3145736 | tf_op jit(solution)/shard_map/ppermute | solution.py:387
  84.7 18.2 %collective-permute-start.18 = (bf16[384,256]{1,0:T(8,128)(2,1)}, bf16[384,256]{1,0:T(8,128)(2,1)S(1)}, u32[]{:S(2)}, u32[]{:S(2)}) collective-permute-start(bf16[384,256]{1,0:T(8,128)(2,1)} %get-tuple-element.58), channel_id=1, source_target_pairs={{0,1},{1,0},{2,3},{3,2},{4,5},{5,4},{6,7},{7,6},{8,9},{9,8},{10,11... | collective-permute-start | bytes 589832 | tf_op jit(solution)/shard_map/ppermute | solution.py:382
  85.5 22.3 %collective-permute-start.19 = (bf16[384,256]{1,0:T(8,128)(2,1)}, bf16[384,256]{1,0:T(8,128)(2,1)}, u32[]{:S(2)}, u32[]{:S(2)}) collective-permute-start(bf16[384,256]{1,0:T(8,128)(2,1)} %get-tuple-element.59), channel_id=1, source_target_pairs={{0,2},{1,3},{2,0},{3,1},{4,6},{5,7},{6,4},{7,5},{8,10},{9,11},{10,... | collective-permute-start | bytes 589832 | tf_op jit(solution)/shard_map/ppermute | solution.py:382
  86.2 21.7 %collective-permute-start.20 = (bf16[384,256]{1,0:T(8,128)(2,1)}, bf16[384,256]{1,0:T(8,128)(2,1)}, u32[]{:S(2)}, u32[]{:S(2)}) collective-permute-start(bf16[384,256]{1,0:T(8,128)(2,1)} %get-tuple-element.60), channel_id=1, source_target_pairs={{0,3},{1,2},{2,1},{3,0},{4,7},{5,6},{6,5},{7,4},{8,11},{9,10},{10,... | collective-permute-start | bytes 589832 | tf_op jit(solution)/shard_map/ppermute | solution.py:382
  101.1 10.1 %collective-permute-start.15 = (bf16[384,256]{1,0:T(8,128)(2,1)S(1)}, bf16[384,256]{1,0:T(8,128)(2,1)S(1)}, u32[]{:S(2)}, u32[]{:S(2)}) collective-permute-start(bf16[384,256]{1,0:T(8,128)(2,1)S(1)} %get-tuple-element.54), channel_id=1, source_target_pairs={{0,1},{1,0},{2,3},{3,2},{4,5},{5,4},{6,7},{7,6},{8,9},{9,8},{10,11... | collective-permute-start | bytes 589832 | tf_op jit(solution)/shard_map/ppermute | solution.py:382
  101.8 10.4 %collective-permute-start.16 = (bf16[384,256]{1,0:T(8,128)(2,1)S(1)}, bf16[384,256]{1,0:T(8,128)(2,1)S(1)}, u32[]{:S(2)}, u32[]{:S(2)}) collective-permute-start(bf16[384,256]{1,0:T(8,128)(2,1)S(1)} %get-tuple-element.55), channel_id=1, source_target_pairs={{0,2},{1,3},{2,0},{3,1},{4,6},{5,7},{6,4},{7,5},{8,10},{9,11},{10,... | collective-permute-start | bytes 589832 | tf_op jit(solution)/shard_map/ppermute | solution.py:382
  102.9 9.3 %collective-permute-start.17 = (bf16[384,256]{1,0:T(8,128)(2,1)S(1)}, bf16[384,256]{1,0:T(8,128)(2,1)S(1)}, u32[]{:S(2)}, u32[]{:S(2)}) collective-permute-start(bf16[384,256]{1,0:T(8,128)(2,1)S(1)} %get-tuple-element.56), channel_id=1, source_target_pairs={{0,3},{1,2},{2,1},{3,0},{4,7},{5,6},{6,5},{7,4},{8,11},{9,10},{10,... | collective-permute-start | bytes 589832 | tf_op jit(solution)/shard_map/ppermute | solution.py:382
  107.8 8.1 %collective-permute-start.22 = (bf16[192,256]{1,0:T(8,128)(2,1)}, bf16[192,256]{1,0:T(8,128)(2,1)S(1)}, u32[]{:S(2)}, u32[]{:S(2)}) collective-permute-start(bf16[192,256]{1,0:T(8,128)(2,1)} %get-tuple-element.69), channel_id=1, source_target_pairs={{0,4},{4,0},{8,12},{12,8},{16,20},{20,16},{24,28},{28,24},{1,5},{5... | collective-permute-start | bytes 294920 | tf_op jit(solution)/shard_map/ppermute | solution.py:375
  107.9 8.0 %collective-permute-start.23 = (bf16[192,256]{1,0:T(8,128)(2,1)}, bf16[192,256]{1,0:T(8,128)(2,1)S(1)}, u32[]{:S(2)}, u32[]{:S(2)}) collective-permute-start(bf16[192,256]{1,0:T(8,128)(2,1)} %get-tuple-element.70), channel_id=1, source_target_pairs={{0,4},{4,0},{8,12},{12,8},{16,20},{20,16},{24,28},{28,24},{1,5},{5... | collective-permute-start | bytes 294920 | tf_op jit(solution)/shard_map/ppermute | solution.py:375
  (28 other events, 179.2 us)

commit v5 on v4

--- a/solution.py
+++ b/solution.py
@@ -37,16 +37,22 @@
         copy.wait()
 
 
-def base_kernel(mp_count, count, kept, at, info_ref, mine_ref, other_ref, *rest):
-    choices = rest[:count]
+def base_kernel(mp_count, counts, kept, places, info_ref, mine_ref, other_ref, *rest):
+    total = sum(counts)
+    choices = rest[:total]
     weight, done, own, sems = rest[-4:] if kept else [*rest[-5:-4], *rest[-3:]]
     outs = rest[-4 - mp_count : -4] if kept else rest[-5 - mp_count : -5]
     rows = own.shape[0] // CORES
-    for number, choice in enumerate(choices):
-
-        @pl.when(info_ref[at] == number)
-        def _(choice=choice):
-            pltpu.make_async_copy(choice, weight, sems.at[0]).start()
+    span = weight.shape[2]
+    first = 0
+    for group, count in enumerate(counts):
+        for number in range(count):
+
+            @pl.when(info_ref[places[group]] == number)
+            def _(group=group, choice=choices[first + number]):
+                pltpu.make_async_copy(choice, weight.at[group], sems.at[group]).start()
+
+        first += count
 
     order = [(number, part) for number in reversed(range(mp_count)) for part in range(CORES)]
     blocks, copies = {}, []
@@ -56,47 +62,55 @@
         n = CORES * number + part
         blocks[n] = source if kept else rest[-4].at[n]
         if not kept:
-            copies.append(pltpu.make_async_copy(source, blocks[n], sems.at[1 + n]))
+            copies.append(pltpu.make_async_copy(source, blocks[n], sems.at[len(counts) + n]))
             copies[-1].start()
-    pltpu.make_async_copy(choices[0], weight, sems.at[0]).wait()
+    for group in range(len(counts)):
+        pltpu.make_async_copy(choices[0], weight.at[group], sems.at[group]).wait()
     stores = []
     for turn, (number, part) in enumerate(order):
         if not kept:
             copies[turn].wait()
         target = done.at[number] if number else own
-        product = jnp.dot(blocks[CORES * number + part][...], weight[...], preferred_element_type=jnp.float32)
-        target[part * rows : (part + 1) * rows, :] = product.astype(target.dtype)
+        for group in range(len(counts)):
+            product = jnp.dot(
+                blocks[CORES * number + part][...], weight[group], preferred_element_type=jnp.float32
+            )
+            columns = slice(group * span, (group + 1) * span)
+            target[part * rows : (part + 1) * rows, columns] = product.astype(target.dtype)
         if part:
-            stores.append(pltpu.make_async_copy(target, outs[number], sems.at[1 + CORES * mp_count + number]))
+            sem = sems.at[len(counts) + CORES * mp_count + number]
+            stores.append(pltpu.make_async_copy(target, outs[number], sem))
             stores[-1].start()
     for store in stores:
         store.wait()
 
 
-def base_products(info, at, mine, other, choices, mp_count, kept, *before):
+def base_products(info, places, mine, other, groups, mp_count, kept, cover, *before):
     group_rows, features = mine.shape
-    rows, span = group_rows // mp_count, choices[0].shape[1]
-    return pl.pallas_call(
-        functools.partial(base_kernel, mp_count, len(choices), kept, at),
-        in_specs=[SCALARS] + [WHOLE if kept else ANYWHERE] * 2 + [ANYWHERE] * (len(choices) + len(before)),
+    rows, span = group_rows // mp_count, groups[0][0].shape[1]
+    wide = span * len(groups)
+    shards = [shard for group in groups for shard in group]
+    return pl.pallas_call(
+        functools.partial(base_kernel, mp_count, [len(group) for group in groups], kept, places),
+        in_specs=[SCALARS] + [WHOLE if kept else ANYWHERE] * 2 + [ANYWHERE] * (len(shards) + len(before)),
         out_specs=[ANYWHERE] * mp_count,
-        scratch_shapes=[pltpu.VMEM((features, span), mine.dtype)]
+        scratch_shapes=[pltpu.VMEM((len(groups), features, span), mine.dtype)]
         + ([] if kept else [pltpu.VMEM((CORES * mp_count, rows, features), mine.dtype)])
         + [
-            pltpu.VMEM((mp_count, CORES * rows, span), jnp.bfloat16),
-            pltpu.VMEM((CORES * rows, span), jnp.float32),
-            pltpu.SemaphoreType.DMA((1 + (1 + CORES) * mp_count,)),
+            pltpu.VMEM((mp_count, CORES * rows, wide), jnp.bfloat16),
+            pltpu.VMEM((CORES * rows, wide), jnp.float32),
+            pltpu.SemaphoreType.DMA((len(groups) + (1 + CORES) * mp_count,)),
         ],
         out_shape=[
-            jax.ShapeDtypeStruct((CORES * rows, span), jnp.bfloat16 if number else jnp.float32)
+            jax.ShapeDtypeStruct((CORES * rows, wide), jnp.bfloat16 if number else jnp.float32)
             for number in range(mp_count)
         ],
         compiler_params=pltpu.CompilerParams(vmem_limit_bytes=VMEM_BYTES // 4 if kept else VMEM_BYTES),
         cost_estimate=cost(
-            COVER * 2 * CORES * group_rows * features * span,
-            2 * (CORES * group_rows * (features + span) + features * span),
+            cover * 2 * CORES * group_rows * features * wide,
+            2 * (CORES * group_rows * (features + wide) + features * wide),
         ),
-    )(info, mine, other, *choices, *before)
+    )(info, mine, other, *shards, *before)
 
 
 def cut_down_kernel(info_ref, down_ref, out, block, sems):
@@ -154,11 +168,11 @@
             pltpu.SemaphoreType.DMA((max(blocks, mp_count),)),
         ],
         compiler_params=params(),
-        cost_estimate=cost(0, 4 * mp_count * blocks * ranks * lanes),
+        cost_estimate=cost(COVER * 2**32, 4 * mp_count * blocks * ranks * lanes),
     )(info, up)
 
 
-def low_kernel(adapters, rank_pair, info_ref, mine_ref, other_ref, mine_ids, other_ids, maps_ref, out, maps, sems):
+def low_kernel(adapters, rank_pair, info_ref, mine_ref, other_ref, mine_ids, other_ids, maps_ref, _, out, maps, sems):
     mp_count, features, lanes = maps.shape
     rows = mine_ref.shape[0] // mp_count
     load_all([(maps_ref.at[number, :features, :], maps.at[number]) for number in range(mp_count)], sems)
@@ -191,22 +205,23 @@
         out[number] = packed
 
 
-def low_sums(info, mine, other, ids, maps, adapters, rank):
+def low_sums(info, mine, other, ids, maps, adapters, rank, before):
     group_rows, features = mine.shape
     mp_count, _, lanes = maps.shape
     rows = group_rows // mp_count
     depth = CORES * rows * 2 * rank // lanes
     return pl.pallas_call(
         functools.partial(low_kernel, adapters, 2 * rank),
-        in_specs=[SCALARS] + [WHOLE] * 4 + [ANYWHERE],
+        in_specs=[SCALARS] + [WHOLE] * 4 + [ANYWHERE] * 2,
         out_specs=WHOLE,
         out_shape=jax.ShapeDtypeStruct((mp_count, depth, lanes), jnp.float32),
         scratch_shapes=[pltpu.VMEM((mp_count, features, lanes), maps.dtype), pltpu.SemaphoreType.DMA((mp_count,))],
         compiler_params=pltpu.CompilerParams(vmem_limit_bytes=VMEM_BYTES // 4),
         cost_estimate=cost(
-            2 * CORES * group_rows * features * mp_count * lanes, 2 * features * (CORES * group_rows + mp_count * lanes)
+            COVER * 2 * CORES * group_rows * features * mp_count * lanes,
+            2 * features * (CORES * group_rows + mp_count * lanes)
         ),
-    )(info, mine, other, *ids, maps)
+    )(info, mine, other, *ids, maps, before)
 
 
 def delta_kernel(adapters, rank, info_ref, mine_ids, other_ids, mine_ref, other_ref, maps_ref, out, maps, sem):
@@ -268,78 +283,70 @@
 
 
 def finish_kernel(mp_count, places, info_ref, delta_ref, *rest):
-    turns = len(places)
-    parts, (delta, own, others, done, sems) = rest[: mp_count * turns], rest[-5:]
-    out, *away = rest[-6 - turns : -5]
-    rows, span = away[0].shape
-    each = mp_count + 1
-    loads = []
-    for turn in range(turns):
-        first, *peers = parts[mp_count * turn : mp_count * (turn + 1)]
-        pairs = [(first, own.at[turn]), (delta_ref.at[info_ref[places[turn]]], delta.at[turn])]
-        pairs += [(part, others.at[turn, n]) for n, part in enumerate(peers)]
-        loads.append(start_all(pairs, sems.at[pl.ds(turn * each, each)]))
-    stores = []
-    for turn in range(turns):
-        for load in loads[turn]:
-            load.wait()
-        total = own[turn]
+    parts, (out, away, delta, own, others, done, sems) = rest[:mp_count], rest[-7:]
+    groups, rows, span = delta.shape
+    rows //= CORES
+    pairs = [(parts[0], own)] + [(part, others.at[n]) for n, part in enumerate(parts[1:])]
+    pairs += [(delta_ref.at[info_ref[place]], delta.at[group]) for group, place in enumerate(places)]
+    load_all(pairs, sems)
+    pairs = [(done.at[rows:, :], away)]
+    for group, place in enumerate(places):
+        columns = slice(group * span, (group + 1) * span)
+        total = own[:, columns]
         for n in range(mp_count - 1):
-            total = total + others[turn, n].astype(jnp.float32)
-        done[turn] = (total + delta[turn].astype(jnp.float32)).astype(done.dtype)
-        place = pl.ds(pl.multiple_of(info_ref[places[turn] + 1] * span, span), span)
-        pairs = [(done.at[turn, rows:, :], away[turn]), (done.at[turn, :rows, :], out.at[:, place])]
-        stores += start_all(pairs, sems.at[pl.ds(turns * each + 2 * turn, 2)])
-    for store in stores:
-        store.wait()
+            total = total + others[n, :, columns].astype(jnp.float32)
+        done[:, columns] = (total + delta[group].astype(jnp.float32)).astype(done.dtype)
+        target = pl.ds(pl.multiple_of(info_ref[place + 1] * span, span), span)
+        pairs.append((done.at[:rows, columns], out.at[:, target]))
+    load_all(pairs, sems)
 
 
 def finish(info, places, delta, parts, held, width):
-    turns, mp_count = len(parts), len(parts[0])
-    rows, span = parts[0][0].shape
-    operands = [info, delta, *sum(parts, [])] + ([] if held is None else [held])
-    away = jax.ShapeDtypeStruct((rows // CORES, span), delta.dtype)
+    mp_count, groups = len(parts), len(places)
+    rows, wide = parts[0].shape
+    operands = [info, delta, *parts] + ([] if held is None else [held])
     return pl.pallas_call(
         functools.partial(finish_kernel, mp_count, places),
         in_specs=[SCALARS] + [ANYWHERE] * (len(operands) - 1),
-        out_specs=[ANYWHERE] * (1 + turns),
-        out_shape=[jax.ShapeDtypeStruct((rows // CORES, width), delta.dtype)] + [away] * turns,
+        out_specs=[ANYWHERE] * 2,
+        out_shape=[
+            jax.ShapeDtypeStruct((rows // CORES, width), delta.dtype),
+            jax.ShapeDtypeStruct((rows // CORES, wide), delta.dtype),
+        ],
         scratch_shapes=[
-            pltpu.VMEM((turns, rows, span), delta.dtype),
-            pltpu.VMEM((turns, rows, span), jnp.float32),
-            pltpu.VMEM((turns, mp_count - 1, rows, span), delta.dtype),
-            pltpu.VMEM((turns, rows, span), delta.dtype),
-            pltpu.SemaphoreType.DMA((turns * (mp_count + 3),)),
+            pltpu.VMEM((groups, rows, wide // groups), delta.dtype),
+            pltpu.VMEM((rows, wide), jnp.float32),
+            pltpu.VMEM((mp_count - 1, rows, wide), delta.dtype),
+            pltpu.VMEM((rows, wide), delta.dtype),
+            pltpu.SemaphoreType.DMA((mp_count + groups,)),
         ],
         input_output_aliases={} if held is None else {len(operands) - 1: 0},
         compiler_params=params(),
-        cost_estimate=cost(4 * rows * span * turns, 12 * rows * span * turns),
+        cost_estimate=cost(4 * rows * wide, 12 * rows * wide),
     )(*operands)
 
 
-def settle_kernel(places, info_ref, *rest):
-    pieces, (out, sems) = rest[:-3], rest[-2:]
-    span = pieces[0].shape[1]
-    load_all(
-        [
-            (piece, out.at[:, pl.ds(pl.multiple_of(info_ref[places[n]] * span, span), span)])
-            for n, piece in enumerate(pieces)
-        ],
-        sems,
-    )
-
-
-def settle(info, places, pieces, held):
+def settle_kernel(places, span, info_ref, *rest):
+    pieces, (out, sems) = rest[: len(places)], rest[-2:]
+    pairs = []
+    for piece, some in zip(pieces, places):
+        for group, place in enumerate(some):
+            target = pl.ds(pl.multiple_of(info_ref[place] * span, span), span)
+            pairs.append((piece.at[:, group * span : (group + 1) * span], out.at[:, target]))
+    load_all(pairs, sems)
+
+
+def settle(info, places, span, pieces, held):
     operands = [info, *pieces, held]
     return pl.pallas_call(
-        functools.partial(settle_kernel, places),
+        functools.partial(settle_kernel, places, span),
         in_specs=[SCALARS] + [WHOLE] * len(pieces) + [ANYWHERE],
         out_specs=ANYWHERE,
         out_shape=jax.ShapeDtypeStruct(held.shape, held.dtype),
-        scratch_shapes=[pltpu.SemaphoreType.DMA((len(pieces),))],
+        scratch_shapes=[pltpu.SemaphoreType.DMA((sum(len(some) for some in places),))],
         input_output_aliases={len(operands) - 1: 0},
         compiler_params=params(),
-        cost_estimate=cost(0, 4 * len(pieces) * pieces[0].size),
+        cost_estimate=cost(0, 4 * sum(piece.size for piece in pieces)),
     )(*operands)
 
 
@@ -408,44 +415,46 @@
 
     down = trade(cut_down(info, adapter_down_weight, mp_count))
     up = cut_up(info, adapter_up_weight.reshape(2, ranks, up_span), mp_count, width, down.shape[2])
-    own, *sent = base_products(info, choice_at[0], tokens, other, [frozen_weight], mp_count, False, up, *ids)
-    finished, out, away = [], None, []
-
-    def finish_some(turns, out):
-        places = [group_at[turn] for turn in turns]
-        return finish(info, places, delta, [finished[turn] for turn in turns], out, dp_count * width)
+    got[1, 1], got[-1, 1], up = after_all(got[1, 1], got[-1, 1], up)
+    finished, places = [], []
 
     for turn in range(1, planes):
         last = turn == planes - 1
         if not last:
-            got[1, turn], got[-1, turn], own = after_all(got[1, turn], got[-1, turn], own)
+            if turn > 1:
+                got[1, turn], got[-1, turn], own, sums = after_all(got[1, turn], got[-1, turn], own, sums)
             for side in (1, -1):
                 got[side, turn + 1] = hop(got[side, turn], side, turn + 1)
-        finished.append([own] + pass_round(sent))
+        if turn > 1:
+            finished.append([own] + pass_round(sent))
         before = []
-        if turn == 1:
-            sums = low_sums(info, tokens, other, ids, down, adapters, rank)
-            before = [sums, *finished[0][1:]]
-        elif turn == 2:
-            up = trade(up)
-            before = [up]
         if last:
-            sums, finished[-1][0], *finished[-2][1:] = after_all(sums, own, *finished[-2][1:])
-            sums = trade(sums)
             delta = deltas_of(info, ids, sums, swap(sums), up, adapters, rank, planes, width)
             before = [delta]
-        shards = [got[option] for option in options[turn]]
+        elif turn == 2:
+            sums = trade(sums)
+            up, sums = after_all(up, sums)
+            up = trade(up)
+            before = finished[0][1:]
+        turns = [0, 1] if turn == 1 else [turn]
+        groups = [[frozen_weight] if n == 0 else [got[option] for option in options[n]] for n in turns]
         kept = turn == 1 or last
-        own, *sent = base_products(info, choice_at[turn], tokens, other, shards, mp_count, kept, *before)
+        cover = 1 if turn == 1 else COVER
+        own, *sent = base_products(
+            info, [choice_at[n] for n in turns], tokens, other, groups, mp_count, kept, cover, *before
+        )
+        places.append([group_at[n] for n in turns])
+        if turn == 1:
+            sums = low_sums(info, tokens, other, ids, down, adapters, rank, own)
     finished.append([own] + pass_round(sent))
 
-    for turns in (range(planes - 2), [planes - 2], [planes - 1]):
-        out, *pieces = finish_some(turns, out)
-        away += pieces
-    away = [swap(piece) for piece in away]
-    places = [at + 2 for at in group_at]
-    out = settle(info, places[:-1], away[:-1], out)
-    return settle(info, places[-1:], away[-1:], out)
+    out, away = None, []
+    for some, parts in zip(places, finished):
+        out, piece = finish(info, some, delta, parts, out, dp_count * width)
+        away.append(swap(piece))
+    places = [[place + 2 for place in some] for some in places]
+    out = settle(info, places[:-1], width, away[:-1], out)
+    return settle(info, places[-1:], width, away[-1:], out)
 
 
 def solution(mesh):

time: 123 us -> 119 us (0.967)
  blocking collectives: 9.33 us -> 0 us
  waiting for transfers between devices: 10 us -> 15.9 us
  Pallas kernels: 54.8 us -> 50.9 us
  local copies, waits for them, and re-layouts: 9.1 us -> 11.5 us
  starting transfers between devices: 36.8 us -> 38.1 us
    ppermute x6, waiting for transfers between devices: 3.47 us -> 13.6 us  [hop(): lax.ppermute(array, 'dp', [(CORES * n + m, CORES * (n - side) + m) for n...]
    all_to_all x1 -> x0, blocking collectives: 9.33 us -> none  [trade(): return lax.all_to_all(array, 'mp', 0, 0)]
    pallas_call x6 -> x5, Pallas kernels: 30.3 us -> 24.2 us  [the longest x3 20.9 us: base_products(): pl.pallas_call(functools.partial(base_kernel, mp_count, [len(group) for g...]
    all_to_all x2 -> x3, starting transfers between devices: 8.17 us -> 12.4 us  [trade(): return lax.all_to_all(array, 'mp', 0, 0)]
    ppermute x12 -> x9, starting transfers between devices: 13.6 us -> 10.6 us  [pass_round(): lax.ppermute(block, 'mp', [(m, m ^ n) for m in range(mp_count)])]
    all_to_all x2 -> x3, waiting for transfers between devices: 5.26 us -> 2.28 us  [trade(): return lax.all_to_all(array, 'mp', 0, 0)]
    unnamed x50 -> x40, local copies, waits for them, and re-layouts: 6.66 us -> 9.16 us
    pallas_call x1, Pallas kernels: 5.69 us -> 7.74 us  [low_sums(): pl.pallas_call(functools.partial(low_kernel, adapters, 2 * rank), in_spec...]
  transfers between devices with their start and end apart: 27 -> 24, of which waited for: 6 -> 5; matrix products, arithmetic and copies ran while one was open for 2% -> 2% of each run, Pallas kernels for 44% -> 42%
where the time goes in v5:
time: 119 us; the launch traced here: 117 us
  Pallas kernels  50.9 us (43%)
  starting transfers between devices  38.1 us (32%)
  waiting for transfers between devices  15.9 us (13%)
  local copies, waits for them, and re-layouts  11.5 us (10%)
    pallas_call x3, Pallas kernels, base_products(): pl.pallas_call(functools.partial(base_kernel, mp_count, [len(group) for g...  20.9 us
    ppermute x6, starting transfers between devices, hop(): lax.ppermute(array, 'dp', [(CORES * n + m, CORES * (n - side) + m) for n...  13.7 us
    ppermute x6, waiting for transfers between devices, hop(): lax.ppermute(array, 'dp', [(CORES * n + m, CORES * (n - side) + m) for n...  13.6 us
    all_to_all x3, starting transfers between devices, trade(): return lax.all_to_all(array, 'mp', 0, 0)  12.4 us
    ppermute x9, starting transfers between devices, pass_round(): lax.ppermute(block, 'mp', [(m, m ^ n) for m in range(mp_count)])  10.6 us
    unnamed x40, local copies, waits for them, and re-layouts  9.16 us
    pallas_call x3, Pallas kernels, finish(): pl.pallas_call(functools.partial(finish_kernel, mp_count, places), in_spe...  8.73 us
    pallas_call x1, Pallas kernels, low_sums(): pl.pallas_call(functools.partial(low_kernel, adapters, 2 * rank), in_spec...  7.74 us
  transfers between devices with their start and end apart: 24, of which 5 were waited for; matrix products, arithmetic and copies ran while one was open for 2% of the time, Pallas kernels for 42%

profile of v5, /device:TPU:0, one launch (start us, length us, event | category | flops | bytes accessed | tf_op | source)
XLA Modules:
  0.0 117.0 jit_solution(3622456980225969017)
XLA Ops:
  1.3 6.6 %collective-permute-start.2 = (bf16[2048,256]{1,0:T(8,128)(2,1)}, bf16[2048,256]{1,0:T(8,128)(2,1)}, u32[]{:S(2)}, u32[]{:S(2)}) collective-permute-start(bf16[2048,256]{1,0:T(8,128)(2,1)} %rest_0_.1), channel_id=1, source_target_pairs={{0,8},{4,12},{8,16},{12,20},{16,24},{20,28},{1,9},{5,13},{9,17},{1... | collective-permute-start | bytes 3145736 | tf_op jit(solution)/shard_map/ppermute | solution.py:394
  8.6 3.1 %shard_map.57 = bf16[4,2048,128]{2,1,0:T(8,128)(2,1)} custom-call(s32[18]{0:T(128)} %stack.72.info_ref, bf16[8192,256]{1,0:T(8,128)(2,1)} %down_ref.1), custom_call_target="tpu_custom_call" | custom-call | bytes 4194304 | tf_op jit(solution)/shard_map/pallas_call | solution.py:133
  11.7 4.5 %all-to-all-start = ((bf16[4,2048,128]{2,1,0:T(8,128)(2,1)}), bf16[4,2048,128]{2,1,0:T(8,128)(2,1)}, u32[]{:S(2)}, u32[]{:S(2)}) async-start(bf16[4,2048,128]{2,1,0:T(8,128)(2,1)} %shard_map.57), calls=%async_computation | async-start | bytes 4194304 | tf_op jit(solution)/shard_map/all_to_all | solution.py:385
  16.7 2.8 %shard_map.55 = bf16[4,1024,128]{2,1,0:T(8,128)(2,1)} custom-call(s32[18]{0:T(128)} %stack.72.info_ref, bf16[2,128,1024]{2,1,0:T(8,128)(2,1)} %bitcast.18), custom_call_target="tpu_custom_call" | custom-call | flops 274877906944 | bytes 2097152 | tf_op jit(solution)/shard_map/pallas_call | solution.py:161
  21.2 7.2 %collective-permute-done.1.rest_2_ = bf16[2048,256]{1,0:T(8,128)(2,1)} collective-permute-done((bf16[2048,256]{1,0:T(8,128)(2,1)}, bf16[2048,256]{1,0:T(8,128)(2,1)}, u32[]{:S(2)}, u32[]{:S(2)}) %collective-permute-start.1) | collective-permute-done | bytes 1048608 | tf_op jit(solution)/shard_map/ppermute | solution.py:394
  32.5 1.9 %copy-done.7 = bf16[768,2048]{1,0:T(8,128)(2,1)S(1)} copy-done((bf16[768,2048]{1,0:T(8,128)(2,1)S(1)}, bf16[768,2048]{1,0:T(8,128)(2,1)}, u32[]{:S(2)}) %copy-start.7) | copy-done | bytes 3145752
  34.4 6.8 %shard_map.56 = (f32[384,512]{1,0:T(8,128)S(1)}, bf16[384,512]{1,0:T(8,128)(2,1)}, bf16[384,512]{1,0:T(8,128)(2,1)}, bf16[384,512]{1,0:T(8,128)(2,1)}) custom-call(s32[18]{0:T(128)S(1)} %copy-done.5, bf16[768,2048]{1,0:T(8,128)(2,1)S(1)} %copy-done.7, bf16[768,2048]{1,0:T(8,128)(2,1)} %collective-permute-done.5.other_ref, bf16[2048,256]{1,0:T(8,128)(2,1)S(1)} %copy-done.10, ...), custom_call_target="tpu_custom_call" | custom-call | flops 3221225472 | bytes 9961472 | tf_op jit(solution)/shard_map/pallas_call | solution.py:93
  41.2 1.7 %collective-permute-start.12 = (bf16[384,512]{1,0:T(8,128)(2,1)}, bf16[384,512]{1,0:T(8,128)(2,1)}, u32[]{:S(2)}, u32[]{:S(2)}) collective-permute-start(bf16[384,512]{1,0:T(8,128)(2,1)} %get-tuple-element.45), channel_id=1, source_target_pairs={{0,1},{1,0},{2,3},{3,2},{4,5},{5,4},{6,7},{7,6},{8,9},{9,8},{10,11... | collective-permute-start | bytes 1179656 | tf_op jit(solution)/shard_map/ppermute | solution.py:389
  44.8 1.9 %copy-done.8 = bf16[768,2048]{1,0:T(8,128)(2,1)S(1)} copy-done((bf16[768,2048]{1,0:T(8,128)(2,1)S(1)}, bf16[768,2048]{1,0:T(8,128)(2,1)}, u32[]{:S(2)}) %copy-start.8) | copy-done | bytes 3145752
  46.7 7.7 %shard_map.58 = f32[4,96,128]{2,1,0:T(8,128)} custom-call(s32[18]{0:T(128)S(1)} %copy-done.5, bf16[768,2048]{1,0:T(8,128)(2,1)S(1)} %copy-done.8, bf16[768,2048]{1,0:T(8,128)(2,1)} %collective-permute-done.5.other_ref, s32[768,1]{1,0:T(8,128)S(1)} %reshape.12.mine_ids, s32[768,1]{1,0:T(8,128)S(1)} %reshape.13.other_ids, ...), custom_call_target="tpu_custom_call" | custom-call | flops 206158430208 | bytes 8388608 | tf_op jit(solution)/shard_map/pallas_call | solution.py:213
  54.4 2.1 %collective-permute-done.3.rest_2_.rest_3_ = bf16[2048,256]{1,0:T(8,128)(2,1)} collective-permute-done((bf16[2048,256]{1,0:T(8,128)(2,1)}, bf16[2048,256]{1,0:T(8,128)(2,1)}, u32[]{:S(2)}, u32[]{:S(2)}) %collective-permute-start.3) | collective-permute-done | bytes 1048608 | tf_op jit(solution)/shard_map/ppermute | solution.py:394
  56.6 3.6 %all-to-all-start.1 = ((f32[4,96,128]{2,1,0:T(8,128)}), f32[4,96,128]{2,1,0:T(8,128)S(1)}, u32[]{:S(2)}, u32[]{:S(2)}) async-start(f32[4,96,128]{2,1,0:T(8,128)} %shard_map.58), calls=%async_computation.1 | async-start | bytes 393216 | tf_op jit(solution)/shard_map/all_to_all | solution.py:385
  63.0 2.3 %all-to-all-done.1.mine_ref = f32[4,96,128]{2,1,0:T(8,128)S(1)} async-done(((f32[4,96,128]{2,1,0:T(8,128)}), f32[4,96,128]{2,1,0:T(8,128)S(1)}, u32[]{:S(2)}, u32[]{:S(2)}) %all-to-all-start.1) | async-done | bytes 196640 | tf_op jit(solution)/shard_map/all_to_all | solution.py:385
  65.3 4.4 %all-to-all-start.2 = ((bf16[4,1024,128]{2,1,0:T(8,128)(2,1)}), bf16[4,1024,128]{2,1,0:T(8,128)(2,1)}, u32[]{:S(2)}, u32[]{:S(2)}) async-start(bf16[4,1024,128]{2,1,0:T(8,128)(2,1)} %shard_map.55), calls=%async_computation.2 | async-start | bytes 2097152 | tf_op jit(solution)/shard_map/all_to_all | solution.py:385
  69.9 7.6 %shard_map.61 = (f32[384,256]{1,0:T(8,128)}, bf16[384,256]{1,0:T(8,128)(2,1)}, bf16[384,256]{1,0:T(8,128)(2,1)}, bf16[384,256]{1,0:T(8,128)(2,1)}) custom-call(s32[18]{0:T(128)} %stack.72.info_ref, bf16[768,2048]{1,0:T(8,128)(2,1)} %mine_ref.7, bf16[768,2048]{1,0:T(8,128)(2,1)} %collective-permute-done.5.other_ref, ...), custom_call_target="tpu_custom_call" | custom-call | flops 103079215104 | bytes 8126464 | tf_op jit(solution)/shard_map/pallas_call | solution.py:93
  77.5 1.8 %collective-permute-start.15 = (bf16[384,256]{1,0:T(8,128)(2,1)}, bf16[384,256]{1,0:T(8,128)(2,1)}, u32[]{:S(2)}, u32[]{:S(2)}) collective-permute-start(bf16[384,256]{1,0:T(8,128)(2,1)} %get-tuple-element.49), channel_id=1, source_target_pairs={{0,1},{1,0},{2,3},{3,2},{4,5},{5,4},{6,7},{7,6},{8,9},{9,8},{10,11... | collective-permute-start | bytes 589832 | tf_op jit(solution)/shard_map/ppermute | solution.py:389
  79.3 1.7 %collective-permute-start.16 = (bf16[384,256]{1,0:T(8,128)(2,1)}, bf16[384,256]{1,0:T(8,128)(2,1)}, u32[]{:S(2)}, u32[]{:S(2)}) collective-permute-start(bf16[384,256]{1,0:T(8,128)(2,1)} %get-tuple-element.50), channel_id=1, source_target_pairs={{0,2},{1,3},{2,0},{3,1},{4,6},{5,7},{6,4},{7,5},{8,10},{9,11},{10,... | collective-permute-start | bytes 589832 | tf_op jit(solution)/shard_map/ppermute | solution.py:389
  81.7 4.4 %shard_map.59.rest_4_.delta_ref = bf16[4,384,256]{2,1,0:T(8,128)(2,1)} custom-call(s32[18]{0:T(128)} %stack.72.info_ref, s32[768,1]{1,0:T(8,128)} %copy-done.1, s32[768,1]{1,0:T(8,128)} %copy-done.2, f32[4,96,128]{2,1,0:T(8,128)} %copy-done.11, f32[4,96,128]{2,1,0:T(8,128)} %copy-done.12, bf16[4,1024,128]{2,1,0:T(8,128)(2,1)} %all-to-all-done.2.maps_ref), custom_call_target="tpu_custom_call" | custom-call | flops 402653184 | bytes 1048576 | tf_op jit(solution)/shard_map/pallas_call | solution.py:274
  86.1 3.1 %collective-permute-done.8.rest_3_ = bf16[2048,256]{1,0:T(8,128)(2,1)} collective-permute-done((bf16[2048,256]{1,0:T(8,128)(2,1)}, bf16[2048,256]{1,0:T(8,128)(2,1)}, u32[]{:S(2)}, u32[]{:S(2)}) %collective-permute-start.8) | collective-permute-done | bytes 1048608 | tf_op jit(solution)/shard_map/ppermute | solution.py:394
  90.4 6.5 %shard_map.60 = (f32[384,256]{1,0:T(8,128)S(1)}, bf16[384,256]{1,0:T(8,128)(2,1)S(1)}, bf16[384,256]{1,0:T(8,128)(2,1)S(1)}, bf16[384,256]{1,0:T(8,128)(2,1)S(1)}) custom-call(s32[18]{0:T(128)S(1)} %copy-done.6, bf16[768,2048]{1,0:T(8,128)(2,1)S(1)} %copy-done.9, bf16[768,2048]{1,0:T(8,128)(2,1)} %collective-permute-done.5.other_ref, ...), custom_call_target="tpu_custom_call" | custom-call | flops 103079215104 | bytes 8126464 | tf_op jit(solution)/shard_map/pallas_call | solution.py:93
  101.1 3.2 %shard_map.62 = (bf16[192,2048]{1,0:T(8,128)(2,1)}, bf16[192,512]{1,0:T(8,128)(2,1)}) custom-call(s32[18]{0:T(128)} %stack.72.info_ref, bf16[4,384,256]{2,1,0:T(8,128)(2,1)} %shard_map.59.rest_4_.delta_ref, f32[384,512]{1,0:T(8,128)} %copy-done.3, bf16[384,512]{1,0:T(8,128)(2,1)} %collective-permute-done.12.rest_4_.rest_1_, ...), custom_call_target="tpu_custom_call" | custom-call | flops 786432 | bytes 2359296 | tf_op jit(solution)/shard_map/pallas_call | solution.py:308
  105.2 2.7 %shard_map.63 = (bf16[192,2048]{1,0:T(8,128)(2,1)}, bf16[192,256]{1,0:T(8,128)(2,1)}) custom-call(s32[18]{0:T(128)} %stack.72.info_ref, bf16[4,384,256]{2,1,0:T(8,128)(2,1)} %shard_map.59.rest_4_.delta_ref, f32[384,256]{1,0:T(8,128)} %get-tuple-element.48.rest_0_, bf16[384,256]{1,0:T(8,128)(2,1)} %collective-permute-done.15.rest_1_, ...), custom_call_target="tpu_custom_call", output_to_operand_aliasing={{0}: (6, {})} | custom-call | flops 393216 | bytes 1179648 | tf_op jit(solution)/shard_map/pallas_call | solution.py:308
  109.4 2.7 %shard_map.64 = (bf16[192,2048]{1,0:T(8,128)(2,1)}, bf16[192,256]{1,0:T(8,128)(2,1)}) custom-call(s32[18]{0:T(128)} %stack.72.info_ref, bf16[4,384,256]{2,1,0:T(8,128)(2,1)} %shard_map.59.rest_4_.delta_ref, f32[384,256]{1,0:T(8,128)} %copy-done.4, bf16[384,256]{1,0:T(8,128)(2,1)} %copy-done.17, ...), custom_call_target="tpu_custom_call", output_to_operand_aliasing={{0}: (6, {})} | custom-call | flops 393216 | bytes 1179648 | tf_op jit(solution)/shard_map/pallas_call | solution.py:308
  112.9 1.7 %shard_map.65.rest_1_ = bf16[192,2048]{1,0:T(8,128)(2,1)} custom-call(s32[18]{0:T(128)} %stack.72.info_ref, bf16[192,512]{1,0:T(8,128)(2,1)} %copy-done.13, bf16[192,256]{1,0:T(8,128)(2,1)} %copy-done.18, bf16[192,2048]{1,0:T(8,128)(2,1)} %get-tuple-element.58.rest_2_), custom_call_target="tpu_custom_call", output_to_operand_aliasing={{}: (3, {})} | custom-call | bytes 589824 | tf_op jit(solution)/shard_map/pallas_call | solution.py:341
  (79 shorter events, 24.4 us)
Async XLA Ops:
  0.0 28.4 %collective-permute-start.1 = (bf16[2048,256]{1,0:T(8,128)(2,1)}, bf16[2048,256]{1,0:T(8,128)(2,1)}, u32[]{:S(2)}, u32[]{:S(2)}) collective-permute-start(bf16[2048,256]{1,0:T(8,128)(2,1)} %rest_0_.1), channel_id=1, source_target_pairs={{8,0},{12,4},{16,8},{20,12},{24,16},{28,20},{9,1},{13,5},{17,9},{2... | collective-permute-start | bytes 3145736 | tf_op jit(solution)/shard_map/ppermute | solution.py:394
  1.3 28.3 %collective-permute-start.2 = (bf16[2048,256]{1,0:T(8,128)(2,1)}, bf16[2048,256]{1,0:T(8,128)(2,1)}, u32[]{:S(2)}, u32[]{:S(2)}) collective-permute-start(bf16[2048,256]{1,0:T(8,128)(2,1)} %rest_0_.1), channel_id=1, source_target_pairs={{0,8},{4,12},{8,16},{12,20},{16,24},{20,28},{1,9},{5,13},{9,17},{1... | collective-permute-start | bytes 3145736 | tf_op jit(solution)/shard_map/ppermute | solution.py:394
  7.9 24.6 %collective-permute-start.5 = (bf16[768,2048]{1,0:T(8,128)(2,1)}, bf16[768,2048]{1,0:T(8,128)(2,1)}, u32[]{:S(2)}, u32[]{:S(2)}) collective-permute-start(bf16[768,2048]{1,0:T(8,128)(2,1)} %mine_ref.7), channel_id=1, source_target_pairs={{0,4},{4,0},{8,12},{12,8},{16,20},{20,16},{24,28},{28,24},{1,5},{5... | collective-permute-start | bytes 9437192 | tf_op jit(solution)/shard_map/ppermute | solution.py:382
  11.7 33.1 %all-to-all-start = ((bf16[4,2048,128]{2,1,0:T(8,128)(2,1)}), bf16[4,2048,128]{2,1,0:T(8,128)(2,1)}, u32[]{:S(2)}, u32[]{:S(2)}) async-start(bf16[4,2048,128]{2,1,0:T(8,128)(2,1)} %shard_map.57), calls=%async_computation | async-start | bytes 4194304 | tf_op jit(solution)/shard_map/all_to_all | solution.py:385
  16.1 4.2 %collective-permute-start = (s32[768]{0:T(1024)}, s32[768]{0:T(1024)}, u32[]{:S(2)}, u32[]{:S(2)}) collective-permute-start(s32[768]{0:T(1024)} %param.9), channel_id=1, source_target_pairs={{0,4},{4,0},{8,12},{12,8},{16,20},{20,16},{24,28},{28,24},{1,5},{5... | collective-permute-start | bytes 9224 | tf_op jit(solution)/shard_map/ppermute | solution.py:382
  29.6 27.0 %collective-permute-start.3 = (bf16[2048,256]{1,0:T(8,128)(2,1)}, bf16[2048,256]{1,0:T(8,128)(2,1)}, u32[]{:S(2)}, u32[]{:S(2)}) collective-permute-start(bf16[2048,256]{1,0:T(8,128)(2,1)} %collective-permute-done.1.rest_2_), channel_id=1, source_target_pairs={{8,0},{12,4},{16,8},{20,12},{9,1},{13,5},{17,9},{21,13},{10,2},{14... | collective-permute-start | bytes 3145736 | tf_op jit(solution)/shard_map/ppermute | solution.py:394
  30.9 25.7 %collective-permute-start.4 = (bf16[2048,256]{1,0:T(8,128)(2,1)}, bf16[2048,256]{1,0:T(8,128)(2,1)}, u32[]{:S(2)}, u32[]{:S(2)}) collective-permute-start(bf16[2048,256]{1,0:T(8,128)(2,1)} %collective-permute-done.2.rest_1_.rest_0_), channel_id=1, source_target_pairs={{8,16},{12,20},{16,24},{20,28},{9,17},{13,21},{17,25},{21,29},{10,... | collective-permute-start | bytes 3145736 | tf_op jit(solution)/shard_map/ppermute | solution.py:394
  41.2 28.5 %collective-permute-start.12 = (bf16[384,512]{1,0:T(8,128)(2,1)}, bf16[384,512]{1,0:T(8,128)(2,1)}, u32[]{:S(2)}, u32[]{:S(2)}) collective-permute-start(bf16[384,512]{1,0:T(8,128)(2,1)} %get-tuple-element.45), channel_id=1, source_target_pairs={{0,1},{1,0},{2,3},{3,2},{4,5},{5,4},{6,7},{7,6},{8,9},{9,8},{10,11... | collective-permute-start | bytes 1179656 | tf_op jit(solution)/shard_map/ppermute | solution.py:389
  42.9 26.9 %collective-permute-start.13 = (bf16[384,512]{1,0:T(8,128)(2,1)}, bf16[384,512]{1,0:T(8,128)(2,1)}, u32[]{:S(2)}, u32[]{:S(2)}) collective-permute-start(bf16[384,512]{1,0:T(8,128)(2,1)} %get-tuple-element.46), channel_id=1, source_target_pairs={{0,2},{1,3},{2,0},{3,1},{4,6},{5,7},{6,4},{7,5},{8,10},{9,11},{10,... | collective-permute-start | bytes 1179656 | tf_op jit(solution)/shard_map/ppermute | solution.py:389
  44.5 25.4 %collective-permute-start.14 = (bf16[384,512]{1,0:T(8,128)(2,1)}, bf16[384,512]{1,0:T(8,128)(2,1)}, u32[]{:S(2)}, u32[]{:S(2)}) collective-permute-start(bf16[384,512]{1,0:T(8,128)(2,1)} %get-tuple-element.47), channel_id=1, source_target_pairs={{0,3},{1,2},{2,1},{3,0},{4,7},{5,6},{6,5},{7,4},{8,11},{9,10},{10,... | collective-permute-start | bytes 1179656 | tf_op jit(solution)/shard_map/ppermute | solution.py:389
  56.6 8.8 %all-to-all-start.1 = ((f32[4,96,128]{2,1,0:T(8,128)}), f32[4,96,128]{2,1,0:T(8,128)S(1)}, u32[]{:S(2)}, u32[]{:S(2)}) async-start(f32[4,96,128]{2,1,0:T(8,128)} %shard_map.58), calls=%async_computation.1 | async-start | bytes 393216 | tf_op jit(solution)/shard_map/all_to_all | solution.py:385
  60.1 26.0 %collective-permute-start.7 = (bf16[2048,256]{1,0:T(8,128)(2,1)}, bf16[2048,256]{1,0:T(8,128)(2,1)}, u32[]{:S(2)}, u32[]{:S(2)}) collective-permute-start(bf16[2048,256]{1,0:T(8,128)(2,1)} %collective-permute-done.4.rest_0_.rest_1_), channel_id=1, source_target_pairs={{16,24},{20,28},{17,25},{21,29},{18,26},{22,30},{19,27},{23,31}} | collective-permute-start | bytes 3145736 | tf_op jit(solution)/shard_map/ppermute | solution.py:394
  61.7 27.5 %collective-permute-start.8 = (bf16[2048,256]{1,0:T(8,128)(2,1)}, bf16[2048,256]{1,0:T(8,128)(2,1)}, u32[]{:S(2)}, u32[]{:S(2)}) collective-permute-start(bf16[2048,256]{1,0:T(8,128)(2,1)} %collective-permute-done.3.rest_2_.rest_3_), channel_id=1, source_target_pairs={{8,0},{12,4},{9,1},{13,5},{10,2},{14,6},{11,3},{15,7}} | collective-permute-start | bytes 3145736 | tf_op jit(solution)/shard_map/ppermute | solution.py:394
  65.3 16.4 %all-to-all-start.2 = ((bf16[4,1024,128]{2,1,0:T(8,128)(2,1)}), bf16[4,1024,128]{2,1,0:T(8,128)(2,1)}, u32[]{:S(2)}, u32[]{:S(2)}) async-start(bf16[4,1024,128]{2,1,0:T(8,128)(2,1)} %shard_map.55), calls=%async_computation.2 | async-start | bytes 2097152 | tf_op jit(solution)/shard_map/all_to_all | solution.py:385
  69.8 11.2 %collective-permute-start.6 = (f32[4,96,128]{2,1,0:T(8,128)S(1)}, f32[4,96,128]{2,1,0:T(8,128)S(1)}, u32[]{:S(2)}, u32[]{:S(2)}) collective-permute-start(f32[4,96,128]{2,1,0:T(8,128)S(1)} %all-to-all-done.1.mine_ref), channel_id=1, source_target_pairs={{0,4},{4,0},{8,12},{12,8},{16,20},{20,16},{24,28},{28,24},{1,5},{5... | collective-permute-start | bytes 589832 | tf_op jit(solution)/shard_map/ppermute | solution.py:382
  77.5 23.3 %collective-permute-start.15 = (bf16[384,256]{1,0:T(8,128)(2,1)}, bf16[384,256]{1,0:T(8,128)(2,1)}, u32[]{:S(2)}, u32[]{:S(2)}) collective-permute-start(bf16[384,256]{1,0:T(8,128)(2,1)} %get-tuple-element.49), channel_id=1, source_target_pairs={{0,1},{1,0},{2,3},{3,2},{4,5},{5,4},{6,7},{7,6},{8,9},{9,8},{10,11... | collective-permute-start | bytes 589832 | tf_op jit(solution)/shard_map/ppermute | solution.py:389
  79.3 25.1 %collective-permute-start.16 = (bf16[384,256]{1,0:T(8,128)(2,1)}, bf16[384,256]{1,0:T(8,128)(2,1)}, u32[]{:S(2)}, u32[]{:S(2)}) collective-permute-start(bf16[384,256]{1,0:T(8,128)(2,1)} %get-tuple-element.50), channel_id=1, source_target_pairs={{0,2},{1,3},{2,0},{3,1},{4,6},{5,7},{6,4},{7,5},{8,10},{9,11},{10,... | collective-permute-start | bytes 589832 | tf_op jit(solution)/shard_map/ppermute | solution.py:389
  81.7 22.8 %collective-permute-start.17 = (bf16[384,256]{1,0:T(8,128)(2,1)}, bf16[384,256]{1,0:T(8,128)(2,1)S(1)}, u32[]{:S(2)}, u32[]{:S(2)}) collective-permute-start(bf16[384,256]{1,0:T(8,128)(2,1)} %get-tuple-element.51), channel_id=1, source_target_pairs={{0,3},{1,2},{2,1},{3,0},{4,7},{5,6},{6,5},{7,4},{8,11},{9,10},{10,... | collective-permute-start | bytes 589832 | tf_op jit(solution)/shard_map/ppermute | solution.py:389
  97.7 10.8 %collective-permute-start.10 = (bf16[384,256]{1,0:T(8,128)(2,1)S(1)}, bf16[384,256]{1,0:T(8,128)(2,1)S(1)}, u32[]{:S(2)}, u32[]{:S(2)}) collective-permute-start(bf16[384,256]{1,0:T(8,128)(2,1)S(1)} %get-tuple-element.43), channel_id=1, source_target_pairs={{0,2},{1,3},{2,0},{3,1},{4,6},{5,7},{6,4},{7,5},{8,10},{9,11},{10,... | collective-permute-start | bytes 589832 | tf_op jit(solution)/shard_map/ppermute | solution.py:389
  99.3 9.2 %collective-permute-start.11 = (bf16[384,256]{1,0:T(8,128)(2,1)S(1)}, bf16[384,256]{1,0:T(8,128)(2,1)S(1)}, u32[]{:S(2)}, u32[]{:S(2)}) collective-permute-start(bf16[384,256]{1,0:T(8,128)(2,1)S(1)} %get-tuple-element.44), channel_id=1, source_target_pairs={{0,3},{1,2},{2,1},{3,0},{4,7},{5,6},{6,5},{7,4},{8,11},{9,10},{10,... | collective-permute-start | bytes 589832 | tf_op jit(solution)/shard_map/ppermute | solution.py:389
  100.8 7.7 %collective-permute-start.9 = (bf16[384,256]{1,0:T(8,128)(2,1)S(1)}, bf16[384,256]{1,0:T(8,128)(2,1)S(1)}, u32[]{:S(2)}, u32[]{:S(2)}) collective-permute-start(bf16[384,256]{1,0:T(8,128)(2,1)S(1)} %get-tuple-element.42), channel_id=1, source_target_pairs={{0,1},{1,0},{2,3},{3,2},{4,5},{5,4},{6,7},{7,6},{8,9},{9,8},{10,11... | collective-permute-start | bytes 589832 | tf_op jit(solution)/shard_map/ppermute | solution.py:389
  104.4 7.8 %collective-permute-start.19 = (bf16[192,512]{1,0:T(8,128)(2,1)}, bf16[192,512]{1,0:T(8,128)(2,1)S(1)}, u32[]{:S(2)}, u32[]{:S(2)}) collective-permute-start(bf16[192,512]{1,0:T(8,128)(2,1)} %get-tuple-element.56), channel_id=1, source_target_pairs={{0,4},{4,0},{8,12},{12,8},{16,20},{20,16},{24,28},{28,24},{1,5},{5... | collective-permute-start | bytes 589832 | tf_op jit(solution)/shard_map/ppermute | solution.py:382
  107.9 4.3 %collective-permute-start.20 = (bf16[192,256]{1,0:T(8,128)(2,1)}, bf16[192,256]{1,0:T(8,128)(2,1)S(1)}, u32[]{:S(2)}, u32[]{:S(2)}) collective-permute-start(bf16[192,256]{1,0:T(8,128)(2,1)} %get-tuple-element.57), channel_id=1, source_target_pairs={{0,4},{4,0},{8,12},{12,8},{16,20},{20,16},{24,28},{28,24},{1,5},{5... | collective-permute-start | bytes 294920 | tf_op jit(solution)/shard_map/ppermute | solution.py:382
  112.1 2.6 %collective-permute-start.18 = (bf16[192,256]{1,0:T(8,128)(2,1)}, bf16[192,256]{1,0:T(8,128)(2,1)S(1)}, u32[]{:S(2)}, u32[]{:S(2)}) collective-permute-start(bf16[192,256]{1,0:T(8,128)(2,1)} %get-tuple-element.55), channel_id=1, source_target_pairs={{0,4},{4,0},{8,12},{12,8},{16,20},{20,16},{24,28},{28,24},{1,5},{5... | collective-permute-start | bytes 294920 | tf_op jit(solution)/shard_map/ppermute | solution.py:382
  (20 other events, 155.3 us)

commit v6 on v5

--- a/solution.py
+++ b/solution.py
@@ -136,7 +136,7 @@
         out_specs=ANYWHERE,
         out_shape=jax.ShapeDtypeStruct(shape, down.dtype),
         scratch_shapes=[pltpu.VMEM(shape, down.dtype), pltpu.SemaphoreType.DMA((2 * mp_count,))],
-        compiler_params=params(),
+        compiler_params=pltpu.CompilerParams(vmem_limit_bytes=VMEM_BYTES // 6),
         cost_estimate=cost(0, 2 * down.size),
     )(info, down)
 
@@ -167,7 +167,7 @@
             pltpu.VMEM((blocks * ranks, lanes), up.dtype),
             pltpu.SemaphoreType.DMA((max(blocks, mp_count),)),
         ],
-        compiler_params=params(),
+        compiler_params=pltpu.CompilerParams(vmem_limit_bytes=VMEM_BYTES // 6),
         cost_estimate=cost(COVER * 2**32, 4 * mp_count * blocks * ranks * lanes),
     )(info, up)
 
@@ -277,7 +277,7 @@
         out_specs=WHOLE,
         out_shape=jax.ShapeDtypeStruct((planes, rows, span), jnp.bfloat16),
         scratch_shapes=[pltpu.VMEM((mp_count, depth, lanes), maps.dtype), pltpu.SemaphoreType.DMA],
-        compiler_params=params(),
+        compiler_params=pltpu.CompilerParams(vmem_limit_bytes=VMEM_BYTES // 6),
         cost_estimate=cost(2 * rows * mp_count * depth * lanes, 2 * mp_count * depth * lanes),
     )(info, *ids, mine, other, maps)
 
@@ -321,7 +321,7 @@
             pltpu.SemaphoreType.DMA((mp_count + groups,)),
         ],
         input_output_aliases={} if held is None else {len(operands) - 1: 0},
-        compiler_params=params(),
+        compiler_params=pltpu.CompilerParams(vmem_limit_bytes=VMEM_BYTES // 6),
         cost_estimate=cost(4 * rows * wide, 12 * rows * wide),
     )(*operands)
 
@@ -345,7 +345,7 @@
         out_shape=jax.ShapeDtypeStruct(held.shape, held.dtype),
         scratch_shapes=[pltpu.SemaphoreType.DMA((sum(len(some) for some in places),))],
         input_output_aliases={len(operands) - 1: 0},
-        compiler_params=params(),
+        compiler_params=pltpu.CompilerParams(vmem_limit_bytes=VMEM_BYTES // 6),
         cost_estimate=cost(0, 4 * sum(piece.size for piece in pieces)),
     )(*operands)
 

time: 119 us -> 113 us (0.950)
  Pallas kernels: 50.9 us -> 45.3 us
  waiting for transfers between devices: 15.9 us -> 20.7 us
  local copies, waits for them, and re-layouts: 11.5 us -> 7.78 us
    ppermute x6, waiting for transfers between devices: 13.6 us -> 17.8 us  [hop(): lax.ppermute(array, 'dp', [(CORES * n + m, CORES * (n - side) + m) for n...]
    unnamed x40 -> x22, local copies, waits for them, and re-layouts: 9.16 us -> 6 us
    pallas_call x1, Pallas kernels: 4.4 us -> 2.02 us  [deltas_of(): pl.pallas_call(functools.partial(delta_kernel, adapters, rank), in_specs=...]
  transfers between devices with their start and end apart: 24 -> 24, of which waited for: 5 -> 6; matrix products, arithmetic and copies ran while one was open for 2% -> 2% of each run, Pallas kernels for 42% -> 39%
where the time goes in v6:
time: 113 us; the launch traced here: 112 us
  Pallas kernels  45.3 us (40%)
  starting transfers between devices  37.6 us (33%)
  waiting for transfers between devices  20.7 us (18%)
  local copies, waits for them, and re-layouts  7.78 us (7%)
    pallas_call x3, Pallas kernels, base_products(): pl.pallas_call(functools.partial(base_kernel, mp_count, [len(group) for g...  20.7 us
    ppermute x6, waiting for transfers between devices, hop(): lax.ppermute(array, 'dp', [(CORES * n + m, CORES * (n - side) + m) for n...  17.8 us
    ppermute x6, starting transfers between devices, hop(): lax.ppermute(array, 'dp', [(CORES * n + m, CORES * (n - side) + m) for n...  13.8 us
    all_to_all x3, starting transfers between devices, trade(): return lax.all_to_all(array, 'mp', 0, 0)  11.8 us
    ppermute x9, starting transfers between devices, pass_round(): lax.ppermute(block, 'mp', [(m, m ^ n) for m in range(mp_count)])  10.7 us
    pallas_call x3, Pallas kernels, finish(): pl.pallas_call(functools.partial(finish_kernel, mp_count, places), in_spe...  8.36 us
    pallas_call x1, Pallas kernels, low_sums(): pl.pallas_call(functools.partial(low_kernel, adapters, 2 * rank), in_spec...  7.69 us
    unnamed x22, local copies, waits for them, and re-layouts  6 us
  transfers between devices with their start and end apart: 24, of which 6 were waited for; matrix products, arithmetic and copies ran while one was open for 2% of the time, Pallas kernels for 39%

profile of v6, /device:TPU:0, one launch (start us, length us, event | category | flops | bytes accessed | tf_op | source)
XLA Modules:
  0.0 111.9 jit_solution(8182052849585020735)
XLA Ops:
  1.3 6.6 %collective-permute-start.2 = (bf16[2048,256]{1,0:T(8,128)(2,1)}, bf16[2048,256]{1,0:T(8,128)(2,1)}, u32[]{:S(2)}, u32[]{:S(2)}) collective-permute-start(bf16[2048,256]{1,0:T(8,128)(2,1)} %rest_0_.1), channel_id=1, source_target_pairs={{0,8},{4,12},{8,16},{12,20},{16,24},{20,28},{1,9},{5,13},{9,17},{1... | collective-permute-start | bytes 3145736 | tf_op jit(solution)/shard_map/ppermute | solution.py:394
  8.0 2.2 %copy-done = bf16[8192,256]{1,0:T(8,128)(2,1)S(1)} copy-done((bf16[8192,256]{1,0:T(8,128)(2,1)S(1)}, bf16[8192,256]{1,0:T(8,128)(2,1)}, u32[]{:S(2)}) %copy-start) | copy-done | bytes 4194328
  10.2 2.3 %shard_map.57 = bf16[4,2048,128]{2,1,0:T(8,128)(2,1)} custom-call(s32[18]{0:T(128)S(1)} %stack.72.info_ref, bf16[8192,256]{1,0:T(8,128)(2,1)S(1)} %copy-done), custom_call_target="tpu_custom_call" | custom-call | bytes 4194304 | tf_op jit(solution)/shard_map/pallas_call | solution.py:133
  12.6 4.6 %all-to-all-start = ((bf16[4,2048,128]{2,1,0:T(8,128)(2,1)}), bf16[4,2048,128]{2,1,0:T(8,128)(2,1)}, u32[]{:S(2)}, u32[]{:S(2)}) async-start(bf16[4,2048,128]{2,1,0:T(8,128)(2,1)} %shard_map.57), calls=%async_computation | async-start | bytes 4194304 | tf_op jit(solution)/shard_map/all_to_all | solution.py:385
  17.7 1.7 %shard_map.55 = bf16[4,1024,128]{2,1,0:T(8,128)(2,1)} custom-call(s32[18]{0:T(128)S(1)} %stack.72.info_ref, bf16[2,128,1024]{2,1,0:T(8,128)(2,1)S(1)} %bitcast.18), custom_call_target="tpu_custom_call" | custom-call | flops 274877906944 | bytes 2097152 | tf_op jit(solution)/shard_map/pallas_call | solution.py:161
  21.2 7.2 %collective-permute-done.1.rest_2_ = bf16[2048,256]{1,0:T(8,128)(2,1)} collective-permute-done((bf16[2048,256]{1,0:T(8,128)(2,1)}, bf16[2048,256]{1,0:T(8,128)(2,1)}, u32[]{:S(2)}, u32[]{:S(2)}) %collective-permute-start.1) | collective-permute-done | bytes 1048608 | tf_op jit(solution)/shard_map/ppermute | solution.py:394
  32.5 6.8 %shard_map.56 = (f32[384,512]{1,0:T(8,128)S(1)}, bf16[384,512]{1,0:T(8,128)(2,1)}, bf16[384,512]{1,0:T(8,128)(2,1)}, bf16[384,512]{1,0:T(8,128)(2,1)}) custom-call(s32[18]{0:T(128)S(1)} %stack.72.info_ref, bf16[768,2048]{1,0:T(8,128)(2,1)S(1)} %copy-done.6, bf16[768,2048]{1,0:T(8,128)(2,1)} %collective-permute-done.5.other_ref, ...), custom_call_target="tpu_custom_call" | custom-call | flops 3221225472 | bytes 9961472 | tf_op jit(solution)/shard_map/pallas_call | solution.py:93
  39.3 1.7 %collective-permute-start.12 = (bf16[384,512]{1,0:T(8,128)(2,1)}, bf16[384,512]{1,0:T(8,128)(2,1)}, u32[]{:S(2)}, u32[]{:S(2)}) collective-permute-start(bf16[384,512]{1,0:T(8,128)(2,1)} %get-tuple-element.45), channel_id=1, source_target_pairs={{0,1},{1,0},{2,3},{3,2},{4,5},{5,4},{6,7},{7,6},{8,9},{9,8},{10,11... | collective-permute-start | bytes 1179656 | tf_op jit(solution)/shard_map/ppermute | solution.py:389
  43.5 1.9 %copy-done.7 = bf16[768,2048]{1,0:T(8,128)(2,1)S(1)} copy-done((bf16[768,2048]{1,0:T(8,128)(2,1)S(1)}, bf16[768,2048]{1,0:T(8,128)(2,1)}, u32[]{:S(2)}) %copy-start.7) | copy-done | bytes 3145752
  45.4 7.7 %shard_map.58 = f32[4,96,128]{2,1,0:T(8,128)} custom-call(s32[18]{0:T(128)S(1)} %stack.72.info_ref, bf16[768,2048]{1,0:T(8,128)(2,1)S(1)} %copy-done.7, bf16[768,2048]{1,0:T(8,128)(2,1)} %collective-permute-done.5.other_ref, s32[768,1]{1,0:T(8,128)S(1)} %reshape.12.mine_ids, s32[768,1]{1,0:T(8,128)S(1)} %reshape.13.other_ids, ...), custom_call_target="tpu_custom_call" | custom-call | flops 206158430208 | bytes 8388608 | tf_op jit(solution)/shard_map/pallas_call | solution.py:213
  53.1 3.5 %collective-permute-done.3.rest_2_.rest_3_ = bf16[2048,256]{1,0:T(8,128)(2,1)} collective-permute-done((bf16[2048,256]{1,0:T(8,128)(2,1)}, bf16[2048,256]{1,0:T(8,128)(2,1)}, u32[]{:S(2)}, u32[]{:S(2)}) %collective-permute-start.3) | collective-permute-done | bytes 1048608 | tf_op jit(solution)/shard_map/ppermute | solution.py:394
  56.6 3.6 %all-to-all-start.1 = ((f32[4,96,128]{2,1,0:T(8,128)}), f32[4,96,128]{2,1,0:T(8,128)S(1)}, u32[]{:S(2)}, u32[]{:S(2)}) async-start(f32[4,96,128]{2,1,0:T(8,128)} %shard_map.58), calls=%async_computation.1 | async-start | bytes 393216 | tf_op jit(solution)/shard_map/all_to_all | solution.py:385
  63.0 2.3 %all-to-all-done.1.mine_ref = f32[4,96,128]{2,1,0:T(8,128)S(1)} async-done(((f32[4,96,128]{2,1,0:T(8,128)}), f32[4,96,128]{2,1,0:T(8,128)S(1)}, u32[]{:S(2)}, u32[]{:S(2)}) %all-to-all-start.1) | async-done | bytes 196640 | tf_op jit(solution)/shard_map/all_to_all | solution.py:385
  65.3 3.7 %all-to-all-start.2 = ((bf16[4,1024,128]{2,1,0:T(8,128)(2,1)}), bf16[4,1024,128]{2,1,0:T(8,128)(2,1)S(1)}, u32[]{:S(2)}, u32[]{:S(2)}) async-start(bf16[4,1024,128]{2,1,0:T(8,128)(2,1)} %shard_map.55), calls=%async_computation.2 | async-start | bytes 2097152 | tf_op jit(solution)/shard_map/all_to_all | solution.py:385
  69.1 7.4 %shard_map.61 = (f32[384,256]{1,0:T(8,128)}, bf16[384,256]{1,0:T(8,128)(2,1)}, bf16[384,256]{1,0:T(8,128)(2,1)}, bf16[384,256]{1,0:T(8,128)(2,1)}) custom-call(s32[18]{0:T(128)} %copy-done.4, bf16[768,2048]{1,0:T(8,128)(2,1)} %mine_ref.7, bf16[768,2048]{1,0:T(8,128)(2,1)} %collective-permute-done.5.other_ref, ...), custom_call_target="tpu_custom_call" | custom-call | flops 103079215104 | bytes 8126464 | tf_op jit(solution)/shard_map/pallas_call | solution.py:93
  76.6 1.8 %collective-permute-start.15 = (bf16[384,256]{1,0:T(8,128)(2,1)}, bf16[384,256]{1,0:T(8,128)(2,1)S(1)}, u32[]{:S(2)}, u32[]{:S(2)}) collective-permute-start(bf16[384,256]{1,0:T(8,128)(2,1)} %get-tuple-element.49), channel_id=1, source_target_pairs={{0,1},{1,0},{2,3},{3,2},{4,5},{5,4},{6,7},{7,6},{8,9},{9,8},{10,11... | collective-permute-start | bytes 589832 | tf_op jit(solution)/shard_map/ppermute | solution.py:389
  80.1 2.0 %shard_map.59.rest_4_.delta_ref = bf16[4,384,256]{2,1,0:T(8,128)(2,1)S(1)} custom-call(s32[18]{0:T(128)S(1)} %copy-done.5, s32[768,1]{1,0:T(8,128)S(1)} %reshape.12.mine_ids, s32[768,1]{1,0:T(8,128)S(1)} %reshape.13.other_ids, f32[4,96,128]{2,1,0:T(8,128)S(1)} %all-to-all-done.1.mine_ref, f32[4,96,128]{2,1,0:T(8,128)S(1)} %collective-permute-done.6.other_ref, ...), custom_call_target="tpu_custom_call" | custom-call | flops 402653184 | bytes 1048576 | tf_op jit(solution)/shard_map/pallas_call | solution.py:274
  82.2 5.9 %collective-permute-done.8.rest_3_ = bf16[2048,256]{1,0:T(8,128)(2,1)} collective-permute-done((bf16[2048,256]{1,0:T(8,128)(2,1)}, bf16[2048,256]{1,0:T(8,128)(2,1)}, u32[]{:S(2)}, u32[]{:S(2)}) %collective-permute-start.8) | collective-permute-done | bytes 1048608 | tf_op jit(solution)/shard_map/ppermute | solution.py:394
  88.1 1.9 %copy-done.8 = bf16[768,2048]{1,0:T(8,128)(2,1)S(1)} copy-done((bf16[768,2048]{1,0:T(8,128)(2,1)S(1)}, bf16[768,2048]{1,0:T(8,128)(2,1)}, u32[]{:S(2)}) %copy-start.8) | copy-done | bytes 3145752
  90.0 6.5 %shard_map.60 = (f32[384,256]{1,0:T(8,128)S(1)}, bf16[384,256]{1,0:T(8,128)(2,1)S(1)}, bf16[384,256]{1,0:T(8,128)(2,1)S(1)}, bf16[384,256]{1,0:T(8,128)(2,1)S(1)}) custom-call(s32[18]{0:T(128)S(1)} %copy-done.5, bf16[768,2048]{1,0:T(8,128)(2,1)S(1)} %copy-done.8, bf16[768,2048]{1,0:T(8,128)(2,1)} %collective-permute-done.5.other_ref, ...), custom_call_target="tpu_custom_call" | custom-call | flops 103079215104 | bytes 8126464 | tf_op jit(solution)/shard_map/pallas_call | solution.py:93
  96.5 1.8 %collective-permute-start.10 = (bf16[384,256]{1,0:T(8,128)(2,1)S(1)}, bf16[384,256]{1,0:T(8,128)(2,1)S(1)}, u32[]{:S(2)}, u32[]{:S(2)}) collective-permute-start(bf16[384,256]{1,0:T(8,128)(2,1)S(1)} %get-tuple-element.43), channel_id=1, source_target_pairs={{0,2},{1,3},{2,0},{3,1},{4,6},{5,7},{6,4},{7,5},{8,10},{9,11},{10,... | collective-permute-start | bytes 589832 | tf_op jit(solution)/shard_map/ppermute | solution.py:389
  100.1 3.0 %shard_map.62 = (bf16[192,2048]{1,0:T(8,128)(2,1)}, bf16[192,512]{1,0:T(8,128)(2,1)S(1)}) custom-call(s32[18]{0:T(128)S(1)} %copy-done.5, bf16[4,384,256]{2,1,0:T(8,128)(2,1)S(1)} %shard_map.59.rest_4_.delta_ref, f32[384,512]{1,0:T(8,128)S(1)} %copy-done.2, bf16[384,512]{1,0:T(8,128)(2,1)} %collective-permute-done.12.rest_4_.rest_1_, ...), custom_call_target="tpu_custom_call" | custom-call | flops 786432 | bytes 2359296 | tf_op jit(solution)/shard_map/pallas_call | solution.py:308
  103.2 2.7 %shard_map.63 = (bf16[192,2048]{1,0:T(8,128)(2,1)}, bf16[192,256]{1,0:T(8,128)(2,1)S(1)}) custom-call(s32[18]{0:T(128)S(1)} %copy-done.5, bf16[4,384,256]{2,1,0:T(8,128)(2,1)S(1)} %shard_map.59.rest_4_.delta_ref, f32[384,256]{1,0:T(8,128)S(1)} %copy-done.3, bf16[384,256]{1,0:T(8,128)(2,1)S(1)} %collective-permute-done.15.rest_1_, ...), custom_call_target="tpu_custom_call", output_to_operand_aliasing={{0}: (6, {})} | custom-call | flops 393216 | bytes 1179648 | tf_op jit(solution)/shard_map/pallas_call | solution.py:308
  106.5 2.7 %shard_map.64 = (bf16[192,2048]{1,0:T(8,128)(2,1)}, bf16[192,256]{1,0:T(8,128)(2,1)S(1)}) custom-call(s32[18]{0:T(128)S(1)} %copy-done.5, bf16[4,384,256]{2,1,0:T(8,128)(2,1)S(1)} %shard_map.59.rest_4_.delta_ref, f32[384,256]{1,0:T(8,128)S(1)} %get-tuple-element.41.rest_0_, ...), custom_call_target="tpu_custom_call", output_to_operand_aliasing={{0}: (6, {})} | custom-call | flops 393216 | bytes 1179648 | tf_op jit(solution)/shard_map/pallas_call | solution.py:308
  (61 shorter events, 20.0 us)
Async XLA Ops:
  0.0 28.4 %collective-permute-start.1 = (bf16[2048,256]{1,0:T(8,128)(2,1)}, bf16[2048,256]{1,0:T(8,128)(2,1)}, u32[]{:S(2)}, u32[]{:S(2)}) collective-permute-start(bf16[2048,256]{1,0:T(8,128)(2,1)} %rest_0_.1), channel_id=1, source_target_pairs={{8,0},{12,4},{16,8},{20,12},{24,16},{28,20},{9,1},{13,5},{17,9},{2... | collective-permute-start | bytes 3145736 | tf_op jit(solution)/shard_map/ppermute | solution.py:394
  1.3 28.3 %collective-permute-start.2 = (bf16[2048,256]{1,0:T(8,128)(2,1)}, bf16[2048,256]{1,0:T(8,128)(2,1)}, u32[]{:S(2)}, u32[]{:S(2)}) collective-permute-start(bf16[2048,256]{1,0:T(8,128)(2,1)} %rest_0_.1), channel_id=1, source_target_pairs={{0,8},{4,12},{8,16},{12,20},{16,24},{20,28},{1,9},{5,13},{9,17},{1... | collective-permute-start | bytes 3145736 | tf_op jit(solution)/shard_map/ppermute | solution.py:394
  7.9 24.6 %collective-permute-start.5 = (bf16[768,2048]{1,0:T(8,128)(2,1)}, bf16[768,2048]{1,0:T(8,128)(2,1)}, u32[]{:S(2)}, u32[]{:S(2)}) collective-permute-start(bf16[768,2048]{1,0:T(8,128)(2,1)} %mine_ref.7), channel_id=1, source_target_pairs={{0,4},{4,0},{8,12},{12,8},{16,20},{20,16},{24,28},{28,24},{1,5},{5... | collective-permute-start | bytes 9437192 | tf_op jit(solution)/shard_map/ppermute | solution.py:382
  12.6 30.9 %all-to-all-start = ((bf16[4,2048,128]{2,1,0:T(8,128)(2,1)}), bf16[4,2048,128]{2,1,0:T(8,128)(2,1)}, u32[]{:S(2)}, u32[]{:S(2)}) async-start(bf16[4,2048,128]{2,1,0:T(8,128)(2,1)} %shard_map.57), calls=%async_computation | async-start | bytes 4194304 | tf_op jit(solution)/shard_map/all_to_all | solution.py:385
  17.1 3.2 %collective-permute-start = (s32[768]{0:T(1024)}, s32[768]{0:T(1024)}, u32[]{:S(2)}, u32[]{:S(2)}) collective-permute-start(s32[768]{0:T(1024)} %param.9), channel_id=1, source_target_pairs={{0,4},{4,0},{8,12},{12,8},{16,20},{20,16},{24,28},{28,24},{1,5},{5... | collective-permute-start | bytes 9224 | tf_op jit(solution)/shard_map/ppermute | solution.py:382
  29.6 27.0 %collective-permute-start.3 = (bf16[2048,256]{1,0:T(8,128)(2,1)}, bf16[2048,256]{1,0:T(8,128)(2,1)}, u32[]{:S(2)}, u32[]{:S(2)}) collective-permute-start(bf16[2048,256]{1,0:T(8,128)(2,1)} %collective-permute-done.1.rest_2_), channel_id=1, source_target_pairs={{8,0},{12,4},{16,8},{20,12},{9,1},{13,5},{17,9},{21,13},{10,2},{14... | collective-permute-start | bytes 3145736 | tf_op jit(solution)/shard_map/ppermute | solution.py:394
  30.9 25.7 %collective-permute-start.4 = (bf16[2048,256]{1,0:T(8,128)(2,1)}, bf16[2048,256]{1,0:T(8,128)(2,1)}, u32[]{:S(2)}, u32[]{:S(2)}) collective-permute-start(bf16[2048,256]{1,0:T(8,128)(2,1)} %collective-permute-done.2.rest_1_.rest_0_), channel_id=1, source_target_pairs={{8,16},{12,20},{16,24},{20,28},{9,17},{13,21},{17,25},{21,29},{10,... | collective-permute-start | bytes 3145736 | tf_op jit(solution)/shard_map/ppermute | solution.py:394
  39.3 29.7 %collective-permute-start.12 = (bf16[384,512]{1,0:T(8,128)(2,1)}, bf16[384,512]{1,0:T(8,128)(2,1)}, u32[]{:S(2)}, u32[]{:S(2)}) collective-permute-start(bf16[384,512]{1,0:T(8,128)(2,1)} %get-tuple-element.45), channel_id=1, source_target_pairs={{0,1},{1,0},{2,3},{3,2},{4,5},{5,4},{6,7},{7,6},{8,9},{9,8},{10,11... | collective-permute-start | bytes 1179656 | tf_op jit(solution)/shard_map/ppermute | solution.py:389
  41.1 28.1 %collective-permute-start.13 = (bf16[384,512]{1,0:T(8,128)(2,1)}, bf16[384,512]{1,0:T(8,128)(2,1)}, u32[]{:S(2)}, u32[]{:S(2)}) collective-permute-start(bf16[384,512]{1,0:T(8,128)(2,1)} %get-tuple-element.46), channel_id=1, source_target_pairs={{0,2},{1,3},{2,0},{3,1},{4,6},{5,7},{6,4},{7,5},{8,10},{9,11},{10,... | collective-permute-start | bytes 1179656 | tf_op jit(solution)/shard_map/ppermute | solution.py:389
  42.6 26.5 %collective-permute-start.14 = (bf16[384,512]{1,0:T(8,128)(2,1)}, bf16[384,512]{1,0:T(8,128)(2,1)}, u32[]{:S(2)}, u32[]{:S(2)}) collective-permute-start(bf16[384,512]{1,0:T(8,128)(2,1)} %get-tuple-element.47), channel_id=1, source_target_pairs={{0,3},{1,2},{2,1},{3,0},{4,7},{5,6},{6,5},{7,4},{8,11},{9,10},{10,... | collective-permute-start | bytes 1179656 | tf_op jit(solution)/shard_map/ppermute | solution.py:389
  56.6 8.8 %all-to-all-start.1 = ((f32[4,96,128]{2,1,0:T(8,128)}), f32[4,96,128]{2,1,0:T(8,128)S(1)}, u32[]{:S(2)}, u32[]{:S(2)}) async-start(f32[4,96,128]{2,1,0:T(8,128)} %shard_map.58), calls=%async_computation.1 | async-start | bytes 393216 | tf_op jit(solution)/shard_map/all_to_all | solution.py:385
  60.1 22.1 %collective-permute-start.7 = (bf16[2048,256]{1,0:T(8,128)(2,1)}, bf16[2048,256]{1,0:T(8,128)(2,1)}, u32[]{:S(2)}, u32[]{:S(2)}) collective-permute-start(bf16[2048,256]{1,0:T(8,128)(2,1)} %collective-permute-done.4.rest_0_.rest_1_), channel_id=1, source_target_pairs={{16,24},{20,28},{17,25},{21,29},{18,26},{22,30},{19,27},{23,31}} | collective-permute-start | bytes 3145736 | tf_op jit(solution)/shard_map/ppermute | solution.py:394
  61.8 26.4 %collective-permute-start.8 = (bf16[2048,256]{1,0:T(8,128)(2,1)}, bf16[2048,256]{1,0:T(8,128)(2,1)}, u32[]{:S(2)}, u32[]{:S(2)}) collective-permute-start(bf16[2048,256]{1,0:T(8,128)(2,1)} %collective-permute-done.3.rest_2_.rest_3_), channel_id=1, source_target_pairs={{8,0},{12,4},{9,1},{13,5},{10,2},{14,6},{11,3},{15,7}} | collective-permute-start | bytes 3145736 | tf_op jit(solution)/shard_map/ppermute | solution.py:394
  65.3 14.8 %all-to-all-start.2 = ((bf16[4,1024,128]{2,1,0:T(8,128)(2,1)}), bf16[4,1024,128]{2,1,0:T(8,128)(2,1)S(1)}, u32[]{:S(2)}, u32[]{:S(2)}) async-start(bf16[4,1024,128]{2,1,0:T(8,128)(2,1)} %shard_map.55), calls=%async_computation.2 | async-start | bytes 2097152 | tf_op jit(solution)/shard_map/all_to_all | solution.py:385
  69.0 10.8 %collective-permute-start.6 = (f32[4,96,128]{2,1,0:T(8,128)S(1)}, f32[4,96,128]{2,1,0:T(8,128)S(1)}, u32[]{:S(2)}, u32[]{:S(2)}) collective-permute-start(f32[4,96,128]{2,1,0:T(8,128)S(1)} %all-to-all-done.1.mine_ref), channel_id=1, source_target_pairs={{0,4},{4,0},{8,12},{12,8},{16,20},{20,16},{24,28},{28,24},{1,5},{5... | collective-permute-start | bytes 589832 | tf_op jit(solution)/shard_map/ppermute | solution.py:382
  76.6 23.2 %collective-permute-start.15 = (bf16[384,256]{1,0:T(8,128)(2,1)}, bf16[384,256]{1,0:T(8,128)(2,1)S(1)}, u32[]{:S(2)}, u32[]{:S(2)}) collective-permute-start(bf16[384,256]{1,0:T(8,128)(2,1)} %get-tuple-element.49), channel_id=1, source_target_pairs={{0,1},{1,0},{2,3},{3,2},{4,5},{5,4},{6,7},{7,6},{8,9},{9,8},{10,11... | collective-permute-start | bytes 589832 | tf_op jit(solution)/shard_map/ppermute | solution.py:389
  78.4 24.7 %collective-permute-start.16 = (bf16[384,256]{1,0:T(8,128)(2,1)}, bf16[384,256]{1,0:T(8,128)(2,1)S(1)}, u32[]{:S(2)}, u32[]{:S(2)}) collective-permute-start(bf16[384,256]{1,0:T(8,128)(2,1)} %get-tuple-element.50), channel_id=1, source_target_pairs={{0,2},{1,3},{2,0},{3,1},{4,6},{5,7},{6,4},{7,5},{8,10},{9,11},{10,... | collective-permute-start | bytes 589832 | tf_op jit(solution)/shard_map/ppermute | solution.py:389
  79.8 23.3 %collective-permute-start.17 = (bf16[384,256]{1,0:T(8,128)(2,1)}, bf16[384,256]{1,0:T(8,128)(2,1)S(1)}, u32[]{:S(2)}, u32[]{:S(2)}) collective-permute-start(bf16[384,256]{1,0:T(8,128)(2,1)} %get-tuple-element.51), channel_id=1, source_target_pairs={{0,3},{1,2},{2,1},{3,0},{4,7},{5,6},{6,5},{7,4},{8,11},{9,10},{10,... | collective-permute-start | bytes 589832 | tf_op jit(solution)/shard_map/ppermute | solution.py:389
  96.5 9.9 %collective-permute-start.10 = (bf16[384,256]{1,0:T(8,128)(2,1)S(1)}, bf16[384,256]{1,0:T(8,128)(2,1)S(1)}, u32[]{:S(2)}, u32[]{:S(2)}) collective-permute-start(bf16[384,256]{1,0:T(8,128)(2,1)S(1)} %get-tuple-element.43), channel_id=1, source_target_pairs={{0,2},{1,3},{2,0},{3,1},{4,6},{5,7},{6,4},{7,5},{8,10},{9,11},{10,... | collective-permute-start | bytes 589832 | tf_op jit(solution)/shard_map/ppermute | solution.py:389
  98.3 8.2 %collective-permute-start.11 = (bf16[384,256]{1,0:T(8,128)(2,1)S(1)}, bf16[384,256]{1,0:T(8,128)(2,1)S(1)}, u32[]{:S(2)}, u32[]{:S(2)}) collective-permute-start(bf16[384,256]{1,0:T(8,128)(2,1)S(1)} %get-tuple-element.44), channel_id=1, source_target_pairs={{0,3},{1,2},{2,1},{3,0},{4,7},{5,6},{6,5},{7,4},{8,11},{9,10},{10,... | collective-permute-start | bytes 589832 | tf_op jit(solution)/shard_map/ppermute | solution.py:389
  99.7 6.7 %collective-permute-start.9 = (bf16[384,256]{1,0:T(8,128)(2,1)S(1)}, bf16[384,256]{1,0:T(8,128)(2,1)S(1)}, u32[]{:S(2)}, u32[]{:S(2)}) collective-permute-start(bf16[384,256]{1,0:T(8,128)(2,1)S(1)} %get-tuple-element.42), channel_id=1, source_target_pairs={{0,1},{1,0},{2,3},{3,2},{4,5},{5,4},{6,7},{7,6},{8,9},{9,8},{10,11... | collective-permute-start | bytes 589832 | tf_op jit(solution)/shard_map/ppermute | solution.py:389
  103.1 6.1 %collective-permute-start.19 = (bf16[192,512]{1,0:T(8,128)(2,1)S(1)}, bf16[192,512]{1,0:T(8,128)(2,1)S(1)}, u32[]{:S(2)}, u32[]{:S(2)}) collective-permute-start(bf16[192,512]{1,0:T(8,128)(2,1)S(1)} %get-tuple-element.56), channel_id=1, source_target_pairs={{0,4},{4,0},{8,12},{12,8},{16,20},{20,16},{24,28},{28,24},{1,5},{5... | collective-permute-start | bytes 589832 | tf_op jit(solution)/shard_map/ppermute | solution.py:382
  105.9 3.3 %collective-permute-start.20 = (bf16[192,256]{1,0:T(8,128)(2,1)S(1)}, bf16[192,256]{1,0:T(8,128)(2,1)S(1)}, u32[]{:S(2)}, u32[]{:S(2)}) collective-permute-start(bf16[192,256]{1,0:T(8,128)(2,1)S(1)} %get-tuple-element.57), channel_id=1, source_target_pairs={{0,4},{4,0},{8,12},{12,8},{16,20},{20,16},{24,28},{28,24},{1,5},{5... | collective-permute-start | bytes 294920 | tf_op jit(solution)/shard_map/ppermute | solution.py:382
  109.1 1.4 %collective-permute-start.18 = (bf16[192,256]{1,0:T(8,128)(2,1)S(1)}, bf16[192,256]{1,0:T(8,128)(2,1)S(1)}, u32[]{:S(2)}, u32[]{:S(2)}) collective-permute-start(bf16[192,256]{1,0:T(8,128)(2,1)S(1)} %get-tuple-element.55), channel_id=1, source_target_pairs={{0,4},{4,0},{8,12},{12,8},{16,20},{20,16},{24,28},{28,24},{1,5},{5... | collective-permute-start | bytes 294920 | tf_op jit(solution)/shard_map/ppermute | solution.py:382
  (11 other events, 137.8 us)

commit v7 on v6

--- a/solution.py
+++ b/solution.py
@@ -225,11 +225,17 @@
 
 
 def delta_kernel(adapters, rank, info_ref, mine_ids, other_ids, mine_ref, other_ref, maps_ref, out, maps, sem):
-    copy = pltpu.make_async_copy(maps_ref.at[:, maps_ref.shape[1] - maps.shape[1] :, :], maps, sem)
-    copy.start()
-    mp_count = maps.shape[0]
+    mp_count, _, lanes = maps_ref.shape
     planes, rows, span = out.shape
-    lanes = mine_ref.shape[2]
+    ranks = adapters * rank
+    copies = []
+    for plane in range(planes):
+        for first in range(0, span, lanes):
+            row = (plane * span + first) // lanes * ranks
+            for owner in range(mp_count):
+                target = maps.at[plane, owner * ranks : (owner + 1) * ranks, first : first + lanes]
+                copies.append(pltpu.make_async_copy(maps_ref.at[owner, row : row + ranks, :], target, sem))
+                copies[-1].start()
     rank_pair = 2 * rank
     groups = lanes // rank_pair
     depth = rows // groups
@@ -250,79 +256,93 @@
     lane_block = lax.broadcasted_iota(jnp.int32, (rows, lanes), 1) // rank
     even = lane_block % 2 == 0
     lows = [jnp.where(even, low, pltpu.roll(low, rank, 1)), jnp.where(even, pltpu.roll(low, lanes - rank, 1), low)]
-    copy.wait()
-    ranks = adapters * rank
+    for copy in copies:
+        copy.wait()
     for part in range(2):
-        spreads = [
-            jnp.where(lane_block == ids - owner * adapters, lows[part], 0.0).astype(jnp.bfloat16)
-            for owner in range(mp_count)
-        ]
+        spread = jnp.concatenate(
+            [
+                jnp.where(lane_block == ids - owner * adapters, lows[part], 0.0).astype(jnp.bfloat16)
+                for owner in range(mp_count)
+            ],
+            axis=1,
+        )
         for plane in range(part * planes // 2, (part + 1) * planes // 2):
-            for piece in range(span // lanes):
-                first = (plane * (span // lanes) + piece) * ranks
-                total = jnp.zeros((rows, lanes), jnp.float32)
-                for owner in range(mp_count):
-                    weights = maps[owner, first : first + ranks, :]
-                    total += jnp.dot(spreads[owner], weights, preferred_element_type=jnp.float32)
-                out[plane, :, piece * lanes : (piece + 1) * lanes] = (ADAPTER_SCALE * total).astype(out.dtype)
+            total = jnp.dot(spread, maps[plane], preferred_element_type=jnp.float32)
+            out[plane] = (ADAPTER_SCALE * total).astype(out.dtype)
 
 
 def deltas_of(info, ids, mine, other, maps, adapters, rank, planes, span):
     mp_count, _, lanes = maps.shape
     rows = CORES * ids[0].shape[0] // mp_count
-    depth = planes * span // lanes * adapters * rank
+    depth = mp_count * adapters * rank
     return pl.pallas_call(
         functools.partial(delta_kernel, adapters, rank),
         in_specs=[SCALARS] + [WHOLE] * 4 + [ANYWHERE],
         out_specs=WHOLE,
         out_shape=jax.ShapeDtypeStruct((planes, rows, span), jnp.bfloat16),
-        scratch_shapes=[pltpu.VMEM((mp_count, depth, lanes), maps.dtype), pltpu.SemaphoreType.DMA],
+        scratch_shapes=[pltpu.VMEM((planes, depth, span), maps.dtype), pltpu.SemaphoreType.DMA],
         compiler_params=pltpu.CompilerParams(vmem_limit_bytes=VMEM_BYTES // 6),
-        cost_estimate=cost(2 * rows * mp_count * depth * lanes, 2 * mp_count * depth * lanes),
+        cost_estimate=cost(2 * rows * planes * depth * span, 2 * planes * depth * span),
     )(info, *ids, mine, other, maps)
 
 
 def finish_kernel(mp_count, places, info_ref, delta_ref, *rest):
-    parts, (out, away, delta, own, others, done, sems) = rest[:mp_count], rest[-7:]
-    groups, rows, span = delta.shape
-    rows //= CORES
-    pairs = [(parts[0], own)] + [(part, others.at[n]) for n, part in enumerate(parts[1:])]
-    pairs += [(delta_ref.at[info_ref[place]], delta.at[group]) for group, place in enumerate(places)]
+    turns = len(places)
+    parts, scratch = rest[: mp_count * turns], rest[-1 - 4 * turns :]
+    out, away = rest[-3 - 4 * turns : -1 - 4 * turns]
+    sems = scratch[-1]
+    rows = away.shape[0]
+    pairs = []
+    for turn, some in enumerate(places):
+        delta, own, others, _ = scratch[4 * turn : 4 * turn + 4]
+        first, *peers = parts[mp_count * turn : mp_count * (turn + 1)]
+        pairs += [(first, own)] + [(part, others.at[n]) for n, part in enumerate(peers)]
+        pairs += [(delta_ref.at[info_ref[place]], delta.at[group]) for group, place in enumerate(some)]
     load_all(pairs, sems)
-    pairs = [(done.at[rows:, :], away)]
-    for group, place in enumerate(places):
-        columns = slice(group * span, (group + 1) * span)
-        total = own[:, columns]
-        for n in range(mp_count - 1):
-            total = total + others[n, :, columns].astype(jnp.float32)
-        done[:, columns] = (total + delta[group].astype(jnp.float32)).astype(done.dtype)
-        target = pl.ds(pl.multiple_of(info_ref[place + 1] * span, span), span)
-        pairs.append((done.at[:rows, columns], out.at[:, target]))
+    pairs, at = [], 0
+    for turn, some in enumerate(places):
+        delta, own, others, done = scratch[4 * turn : 4 * turn + 4]
+        span = delta.shape[2]
+        for group, place in enumerate(some):
+            columns = slice(group * span, (group + 1) * span)
+            total = own[:, columns]
+            for n in range(mp_count - 1):
+                total = total + others[n, :, columns].astype(jnp.float32)
+            done[:, columns] = (total + delta[group].astype(jnp.float32)).astype(done.dtype)
+            target = pl.ds(pl.multiple_of(info_ref[place + 1] * span, span), span)
+            pairs.append((done.at[rows:, columns], away.at[:, at : at + span]))
+            pairs.append((done.at[:rows, columns], out.at[:, target]))
+            at += span
     load_all(pairs, sems)
 
 
-def finish(info, places, delta, parts, held, width):
-    mp_count, groups = len(parts), len(places)
-    rows, wide = parts[0].shape
-    operands = [info, delta, *parts] + ([] if held is None else [held])
+def finish(info, places, delta, parts, held, width, *before):
+    mp_count, rows = len(parts[0]), parts[0][0].shape[0]
+    span = delta.shape[2]
+    count = sum(len(some) for some in places)
+    operands = [info, delta, *sum(parts, []), *before] + ([] if held is None else [held])
+    scratch = []
+    for some in places:
+        wide = span * len(some)
+        scratch += [
+            pltpu.VMEM((len(some), rows, span), delta.dtype),
+            pltpu.VMEM((rows, wide), jnp.float32),
+            pltpu.VMEM((mp_count - 1, rows, wide), delta.dtype),
+            pltpu.VMEM((rows, wide), delta.dtype),
+        ]
+    held_bytes = rows * span * count * (2 * mp_count + 6)
     return pl.pallas_call(
         functools.partial(finish_kernel, mp_count, places),
         in_specs=[SCALARS] + [ANYWHERE] * (len(operands) - 1),
         out_specs=[ANYWHERE] * 2,
         out_shape=[
             jax.ShapeDtypeStruct((rows // CORES, width), delta.dtype),
-            jax.ShapeDtypeStruct((rows // CORES, wide), delta.dtype),
+            jax.ShapeDtypeStruct((rows // CORES, span * count), delta.dtype),
         ],
-        scratch_shapes=[
-            pltpu.VMEM((groups, rows, wide // groups), delta.dtype),
-            pltpu.VMEM((rows, wide), jnp.float32),
-            pltpu.VMEM((mp_count - 1, rows, wide), delta.dtype),
-            pltpu.VMEM((rows, wide), delta.dtype),
-            pltpu.SemaphoreType.DMA((mp_count + groups,)),
-        ],
+        scratch_shapes=scratch + [pltpu.SemaphoreType.DMA((mp_count * len(places) + 2 * count,))],
         input_output_aliases={} if held is None else {len(operands) - 1: 0},
-        compiler_params=pltpu.CompilerParams(vmem_limit_bytes=VMEM_BYTES // 6),
-        cost_estimate=cost(4 * rows * wide, 12 * rows * wide),
+        compiler_params=pltpu.CompilerParams(vmem_limit_bytes=VMEM_BYTES // 10 + held_bytes + held_bytes // 4),
+        cost_estimate=cost(4 * rows * span * count, 12 * rows * span * count),
     )(*operands)
 
 
@@ -448,13 +468,13 @@
             sums = low_sums(info, tokens, other, ids, down, adapters, rank, own)
     finished.append([own] + pass_round(sent))
 
-    out, away = None, []
-    for some, parts in zip(places, finished):
-        out, piece = finish(info, some, delta, parts, out, dp_count * width)
-        away.append(swap(piece))
-    places = [[place + 2 for place in some] for some in places]
-    out = settle(info, places[:-1], width, away[:-1], out)
-    return settle(info, places[-1:], width, away[-1:], out)
+    out, first = finish(info, places[:-1], delta, finished[:-1], None, dp_count * width, own)
+    first = swap(first)
+    out, second = finish(info, places[-1:], delta, finished[-1:], out, dp_count * width)
+    second = swap(second)
+    places = [place + 2 for some in places for place in some]
+    out = settle(info, [places[:-1]], width, [first], out)
+    return settle(info, [places[-1:]], width, [second], out)
 
 
 def solution(mesh):

time: 113 us -> 111 us (0.982)
  local copies, waits for them, and re-layouts: 7.78 us -> 3.3 us
  waiting for transfers between devices: 20.7 us -> 24.2 us
    unnamed x22 -> x18, local copies, waits for them, and re-layouts: 6 us -> 2.22 us
    ppermute x9, waiting for transfers between devices: 0.02 us -> 2.64 us  [pass_round(): lax.ppermute(block, 'mp', [(m, m ^ n) for m in range(mp_count)])]
    pallas_call x3 -> x2, Pallas kernels: 8.36 us -> 6.16 us  [finish(): pl.pallas_call(functools.partial(finish_kernel, mp_count, places), in_spe...]
    pallas_call x3, Pallas kernels: 20.7 us -> 22.7 us  [base_products(): pl.pallas_call(functools.partial(base_kernel, mp_count, [len(group) for g...]
    ppermute x6, waiting for transfers between devices: 17.8 us -> 19.3 us  [hop(): lax.ppermute(array, 'dp', [(CORES * n + m, CORES * (n - side) + m) for n...]
  transfers between devices with their start and end apart: 24 -> 23, of which waited for: 6 -> 7; matrix products, arithmetic and copies ran while one was open for 2% -> 1% of each run, Pallas kernels for 39% -> 40%
where the time goes in v7:
time: 111 us
  Pallas kernels  45.7 us (41%)
  starting transfers between devices  37.1 us (33%)
  waiting for transfers between devices  24.2 us (22%)
  local copies, waits for them, and re-layouts  3.3 us (3%)
    pallas_call x3, Pallas kernels, base_products(): pl.pallas_call(functools.partial(base_kernel, mp_count, [len(group) for g...  22.7 us
    ppermute x6, waiting for transfers between devices, hop(): lax.ppermute(array, 'dp', [(CORES * n + m, CORES * (n - side) + m) for n...  19.3 us
    ppermute x6, starting transfers between devices, hop(): lax.ppermute(array, 'dp', [(CORES * n + m, CORES * (n - side) + m) for n...  13.8 us
    all_to_all x3, starting transfers between devices, trade(): return lax.all_to_all(array, 'mp', 0, 0)  11.8 us
    ppermute x9, starting transfers between devices, pass_round(): lax.ppermute(block, 'mp', [(m, m ^ n) for m in range(mp_count)])  10.7 us
    pallas_call x1, Pallas kernels, low_sums(): pl.pallas_call(functools.partial(low_kernel, adapters, 2 * rank), in_spec...  8.68 us
    pallas_call x2, Pallas kernels, finish(): pl.pallas_call(functools.partial(finish_kernel, mp_count, places), in_spe...  6.16 us
    ppermute x9, waiting for transfers between devices, pass_round(): lax.ppermute(block, 'mp', [(m, m ^ n) for m in range(mp_count)])  2.64 us
  transfers between devices with their start and end apart: 23, of which 7 were waited for; matrix products, arithmetic and copies ran while one was open for 1% of the time, Pallas kernels for 40%

profile of v7, /device:TPU:0, one launch (start us, length us, event | category | flops | bytes accessed | tf_op | source)
XLA Modules:
  0.0 110.8 jit_solution(8125673163374453209)
XLA Ops:
  1.3 6.7 %collective-permute-start.2 = (bf16[2048,256]{1,0:T(8,128)(2,1)}, bf16[2048,256]{1,0:T(8,128)(2,1)}, u32[]{:S(2)}, u32[]{:S(2)}) collective-permute-start(bf16[2048,256]{1,0:T(8,128)(2,1)} %rest_0_.1), channel_id=1, source_target_pairs={{0,8},{4,12},{8,16},{12,20},{16,24},{20,28},{1,9},{5,13},{9,17},{1... | collective-permute-start | bytes 3145736 | tf_op jit(solution)/shard_map/ppermute | solution.py:414
  8.1 2.2 %copy-done = bf16[8192,256]{1,0:T(8,128)(2,1)S(1)} copy-done((bf16[8192,256]{1,0:T(8,128)(2,1)S(1)}, bf16[8192,256]{1,0:T(8,128)(2,1)}, u32[]{:S(2)}) %copy-start) | copy-done | bytes 4194328
  10.2 2.3 %shard_map.57 = bf16[4,2048,128]{2,1,0:T(8,128)(2,1)} custom-call(s32[18]{0:T(128)S(1)} %stack.72.info_ref, bf16[8192,256]{1,0:T(8,128)(2,1)S(1)} %copy-done), custom_call_target="tpu_custom_call" | custom-call | bytes 4194304 | tf_op jit(solution)/shard_map/pallas_call | solution.py:133
  12.5 4.6 %all-to-all-start = ((bf16[4,2048,128]{2,1,0:T(8,128)(2,1)}), bf16[4,2048,128]{2,1,0:T(8,128)(2,1)}, u32[]{:S(2)}, u32[]{:S(2)}) async-start(bf16[4,2048,128]{2,1,0:T(8,128)(2,1)} %shard_map.57), calls=%async_computation | async-start | bytes 4194304 | tf_op jit(solution)/shard_map/all_to_all | solution.py:405
  17.7 1.7 %shard_map.55 = bf16[4,1024,128]{2,1,0:T(8,128)(2,1)} custom-call(s32[18]{0:T(128)S(1)} %stack.72.info_ref, bf16[2,128,1024]{2,1,0:T(8,128)(2,1)S(1)} %bitcast.18), custom_call_target="tpu_custom_call" | custom-call | flops 274877906944 | bytes 2097152 | tf_op jit(solution)/shard_map/pallas_call | solution.py:161
  20.5 7.9 %collective-permute-done.1.rest_2_ = bf16[2048,256]{1,0:T(8,128)(2,1)} collective-permute-done((bf16[2048,256]{1,0:T(8,128)(2,1)}, bf16[2048,256]{1,0:T(8,128)(2,1)}, u32[]{:S(2)}, u32[]{:S(2)}) %collective-permute-start.1) | collective-permute-done | bytes 1048608 | tf_op jit(solution)/shard_map/ppermute | solution.py:414
  30.9 1.7 %collective-permute-start.4 = (bf16[2048,256]{1,0:T(8,128)(2,1)}, bf16[2048,256]{1,0:T(8,128)(2,1)}, u32[]{:S(2)}, u32[]{:S(2)}) collective-permute-start(bf16[2048,256]{1,0:T(8,128)(2,1)} %collective-permute-done.2.rest_1_.rest_0_), channel_id=1, source_target_pairs={{8,16},{12,20},{16,24},{20,28},{9,17},{13,21},{17,25},{21,29},{10,... | collective-permute-start | bytes 3145736 | tf_op jit(solution)/shard_map/ppermute | solution.py:414
  32.5 7.8 %shard_map.56 = (f32[384,512]{1,0:T(8,128)S(1)}, bf16[384,512]{1,0:T(8,128)(2,1)}, bf16[384,512]{1,0:T(8,128)(2,1)}, bf16[384,512]{1,0:T(8,128)(2,1)}) custom-call(s32[18]{0:T(128)S(1)} %stack.72.info_ref, bf16[768,2048]{1,0:T(8,128)(2,1)} %mine_ref.7, bf16[768,2048]{1,0:T(8,128)(2,1)} %collective-permute-done.5.other_ref, bf16[2048,256]{1,0:T(8,128)(2,1)S(1)} %copy-done.6, ...), custom_call_target="tpu_custom_call" | custom-call | flops 3221225472 | bytes 9961472 | tf_op jit(solution)/shard_map/pallas_call | solution.py:93
  40.3 1.7 %collective-permute-start.12 = (bf16[384,512]{1,0:T(8,128)(2,1)}, bf16[384,512]{1,0:T(8,128)(2,1)}, u32[]{:S(2)}, u32[]{:S(2)}) collective-permute-start(bf16[384,512]{1,0:T(8,128)(2,1)} %get-tuple-element.44), channel_id=1, source_target_pairs={{0,1},{1,0},{2,3},{3,2},{4,5},{5,4},{6,7},{7,6},{8,9},{9,8},{10,11... | collective-permute-start | bytes 1179656 | tf_op jit(solution)/shard_map/ppermute | solution.py:409
  42.0 1.5 %collective-permute-start.13 = (bf16[384,512]{1,0:T(8,128)(2,1)}, bf16[384,512]{1,0:T(8,128)(2,1)}, u32[]{:S(2)}, u32[]{:S(2)}) collective-permute-start(bf16[384,512]{1,0:T(8,128)(2,1)} %get-tuple-element.45), channel_id=1, source_target_pairs={{0,2},{1,3},{2,0},{3,1},{4,6},{5,7},{6,4},{7,5},{8,10},{9,11},{10,... | collective-permute-start | bytes 1179656 | tf_op jit(solution)/shard_map/ppermute | solution.py:409
  43.9 8.7 %shard_map.58 = f32[4,96,128]{2,1,0:T(8,128)} custom-call(s32[18]{0:T(128)S(1)} %stack.72.info_ref, bf16[768,2048]{1,0:T(8,128)(2,1)} %mine_ref.7, bf16[768,2048]{1,0:T(8,128)(2,1)} %collective-permute-done.5.other_ref, s32[768,1]{1,0:T(8,128)S(1)} %reshape.12.mine_ids, s32[768,1]{1,0:T(8,128)S(1)} %reshape.13.other_ids, ...), custom_call_target="tpu_custom_call" | custom-call | flops 206158430208 | bytes 8388608 | tf_op jit(solution)/shard_map/pallas_call | solution.py:213
  52.6 4.0 %collective-permute-done.3.rest_2_.rest_3_ = bf16[2048,256]{1,0:T(8,128)(2,1)} collective-permute-done((bf16[2048,256]{1,0:T(8,128)(2,1)}, bf16[2048,256]{1,0:T(8,128)(2,1)}, u32[]{:S(2)}, u32[]{:S(2)}) %collective-permute-start.3) | collective-permute-done | bytes 1048608 | tf_op jit(solution)/shard_map/ppermute | solution.py:414
  56.6 3.6 %all-to-all-start.1 = ((f32[4,96,128]{2,1,0:T(8,128)}), f32[4,96,128]{2,1,0:T(8,128)S(1)}, u32[]{:S(2)}, u32[]{:S(2)}) async-start(f32[4,96,128]{2,1,0:T(8,128)} %shard_map.58), calls=%async_computation.1 | async-start | bytes 393216 | tf_op jit(solution)/shard_map/all_to_all | solution.py:405
  60.1 1.7 %collective-permute-start.7 = (bf16[2048,256]{1,0:T(8,128)(2,1)}, bf16[2048,256]{1,0:T(8,128)(2,1)}, u32[]{:S(2)}, u32[]{:S(2)}) collective-permute-start(bf16[2048,256]{1,0:T(8,128)(2,1)} %collective-permute-done.4.rest_0_.rest_1_), channel_id=1, source_target_pairs={{16,24},{20,28},{17,25},{21,29},{18,26},{22,30},{19,27},{23,31}} | collective-permute-start | bytes 3145736 | tf_op jit(solution)/shard_map/ppermute | solution.py:414
  63.0 2.3 %all-to-all-done.1.mine_ref = f32[4,96,128]{2,1,0:T(8,128)S(1)} async-done(((f32[4,96,128]{2,1,0:T(8,128)}), f32[4,96,128]{2,1,0:T(8,128)S(1)}, u32[]{:S(2)}, u32[]{:S(2)}) %all-to-all-start.1) | async-done | bytes 196640 | tf_op jit(solution)/shard_map/all_to_all | solution.py:405
  65.3 3.7 %all-to-all-start.2 = ((bf16[4,1024,128]{2,1,0:T(8,128)(2,1)}), bf16[4,1024,128]{2,1,0:T(8,128)(2,1)S(1)}, u32[]{:S(2)}, u32[]{:S(2)}) async-start(bf16[4,1024,128]{2,1,0:T(8,128)(2,1)} %shard_map.55), calls=%async_computation.2 | async-start | bytes 2097152 | tf_op jit(solution)/shard_map/all_to_all | solution.py:405
  69.1 7.4 %shard_map.61 = (f32[384,256]{1,0:T(8,128)}, bf16[384,256]{1,0:T(8,128)(2,1)}, bf16[384,256]{1,0:T(8,128)(2,1)}, bf16[384,256]{1,0:T(8,128)(2,1)}) custom-call(s32[18]{0:T(128)} %copy-done.4, bf16[768,2048]{1,0:T(8,128)(2,1)} %mine_ref.7, bf16[768,2048]{1,0:T(8,128)(2,1)} %collective-permute-done.5.other_ref, ...), custom_call_target="tpu_custom_call" | custom-call | flops 103079215104 | bytes 8126464 | tf_op jit(solution)/shard_map/pallas_call | solution.py:93
  76.6 1.8 %collective-permute-start.15 = (bf16[384,256]{1,0:T(8,128)(2,1)}, bf16[384,256]{1,0:T(8,128)(2,1)S(1)}, u32[]{:S(2)}, u32[]{:S(2)}) collective-permute-start(bf16[384,256]{1,0:T(8,128)(2,1)} %get-tuple-element.48), channel_id=1, source_target_pairs={{0,1},{1,0},{2,3},{3,2},{4,5},{5,4},{6,7},{7,6},{8,9},{9,8},{10,11... | collective-permute-start | bytes 589832 | tf_op jit(solution)/shard_map/ppermute | solution.py:409
  80.1 1.7 %shard_map.59.rest_4_.delta_ref = bf16[4,384,256]{2,1,0:T(8,128)(2,1)S(1)} custom-call(s32[18]{0:T(128)S(1)} %copy-done.5, s32[768,1]{1,0:T(8,128)S(1)} %reshape.12.mine_ids, s32[768,1]{1,0:T(8,128)S(1)} %reshape.13.other_ids, f32[4,96,128]{2,1,0:T(8,128)S(1)} %all-to-all-done.1.mine_ref, f32[4,96,128]{2,1,0:T(8,128)S(1)} %collective-permute-done.6.other_ref, ...), custom_call_target="tpu_custom_call" | custom-call | flops 402653184 | bytes 1048576 | tf_op jit(solution)/shard_map/pallas_call | solution.py:278
  81.9 6.2 %collective-permute-done.8.rest_3_ = bf16[2048,256]{1,0:T(8,128)(2,1)} collective-permute-done((bf16[2048,256]{1,0:T(8,128)(2,1)}, bf16[2048,256]{1,0:T(8,128)(2,1)}, u32[]{:S(2)}, u32[]{:S(2)}) %collective-permute-start.8) | collective-permute-done | bytes 1048608 | tf_op jit(solution)/shard_map/ppermute | solution.py:414
  88.1 7.5 %shard_map.60 = (f32[384,256]{1,0:T(8,128)S(1)}, bf16[384,256]{1,0:T(8,128)(2,1)S(1)}, bf16[384,256]{1,0:T(8,128)(2,1)S(1)}, bf16[384,256]{1,0:T(8,128)(2,1)S(1)}) custom-call(s32[18]{0:T(128)S(1)} %copy-done.5, bf16[768,2048]{1,0:T(8,128)(2,1)} %mine_ref.7, bf16[768,2048]{1,0:T(8,128)(2,1)} %collective-permute-done.5.other_ref, ...), custom_call_target="tpu_custom_call" | custom-call | flops 103079215104 | bytes 8126464 | tf_op jit(solution)/shard_map/pallas_call | solution.py:93
  95.6 1.7 %collective-permute-start.9 = (bf16[384,256]{1,0:T(8,128)(2,1)S(1)}, bf16[384,256]{1,0:T(8,128)(2,1)S(1)}, u32[]{:S(2)}, u32[]{:S(2)}) collective-permute-start(bf16[384,256]{1,0:T(8,128)(2,1)S(1)} %get-tuple-element.40), channel_id=1, source_target_pairs={{0,1},{1,0},{2,3},{3,2},{4,5},{5,4},{6,7},{7,6},{8,9},{9,8},{10,11... | collective-permute-start | bytes 589832 | tf_op jit(solution)/shard_map/ppermute | solution.py:409
  99.2 3.5 %shard_map.62 = (bf16[192,2048]{1,0:T(8,128)(2,1)}, bf16[192,768]{1,0:T(8,128)(2,1)S(1)}) custom-call(s32[18]{0:T(128)S(1)} %copy-done.5, bf16[4,384,256]{2,1,0:T(8,128)(2,1)S(1)} %shard_map.59.rest_4_.delta_ref, f32[384,512]{1,0:T(8,128)S(1)} %copy-done.2, bf16[384,512]{1,0:T(8,128)(2,1)} %collective-permute-done.12.rest_4_.rest_1_, ...), custom_call_target="tpu_custom_call" | custom-call | flops 1179648 | bytes 3538944 | tf_op jit(solution)/shard_map/pallas_call | solution.py:334
  105.4 2.7 %shard_map.63 = (bf16[192,2048]{1,0:T(8,128)(2,1)}, bf16[192,256]{1,0:T(8,128)(2,1)S(1)}) custom-call(s32[18]{0:T(128)S(1)} %copy-done.5, bf16[4,384,256]{2,1,0:T(8,128)(2,1)S(1)} %shard_map.59.rest_4_.delta_ref, f32[384,256]{1,0:T(8,128)S(1)} %get-tuple-element.39.rest_8_.rest_0_, ...), custom_call_target="tpu_custom_call", output_to_operand_aliasing={{0}: (6, {})} | custom-call | flops 393216 | bytes 1179648 | tf_op jit(solution)/shard_map/pallas_call | solution.py:334
  (54 shorter events, 15.9 us)
Async XLA Ops:
  0.0 28.4 %collective-permute-start.1 = (bf16[2048,256]{1,0:T(8,128)(2,1)}, bf16[2048,256]{1,0:T(8,128)(2,1)}, u32[]{:S(2)}, u32[]{:S(2)}) collective-permute-start(bf16[2048,256]{1,0:T(8,128)(2,1)} %rest_0_.1), channel_id=1, source_target_pairs={{8,0},{12,4},{16,8},{20,12},{24,16},{28,20},{9,1},{13,5},{17,9},{2... | collective-permute-start | bytes 3145736 | tf_op jit(solution)/shard_map/ppermute | solution.py:414
  1.3 28.3 %collective-permute-start.2 = (bf16[2048,256]{1,0:T(8,128)(2,1)}, bf16[2048,256]{1,0:T(8,128)(2,1)}, u32[]{:S(2)}, u32[]{:S(2)}) collective-permute-start(bf16[2048,256]{1,0:T(8,128)(2,1)} %rest_0_.1), channel_id=1, source_target_pairs={{0,8},{4,12},{8,16},{12,20},{16,24},{20,28},{1,9},{5,13},{9,17},{1... | collective-permute-start | bytes 3145736 | tf_op jit(solution)/shard_map/ppermute | solution.py:414
  7.9 11.7 %collective-permute-start = (s32[768]{0:T(1024)}, s32[768]{0:T(1024)}, u32[]{:S(2)}, u32[]{:S(2)}) collective-permute-start(s32[768]{0:T(1024)} %param.9), channel_id=1, source_target_pairs={{0,4},{4,0},{8,12},{12,8},{16,20},{20,16},{24,28},{28,24},{1,5},{5... | collective-permute-start | bytes 9224 | tf_op jit(solution)/shard_map/ppermute | solution.py:402
  10.2 33.6 %copy-start.4 = (s32[18]{0:T(128)}, s32[18]{0:T(128)S(1)}, u32[]{:S(2)}) copy-start(s32[18]{0:T(128)S(1)} %stack.72.info_ref) | copy-start | bytes 220
  12.5 31.3 %all-to-all-start = ((bf16[4,2048,128]{2,1,0:T(8,128)(2,1)}), bf16[4,2048,128]{2,1,0:T(8,128)(2,1)}, u32[]{:S(2)}, u32[]{:S(2)}) async-start(bf16[4,2048,128]{2,1,0:T(8,128)(2,1)} %shard_map.57), calls=%async_computation | async-start | bytes 4194304 | tf_op jit(solution)/shard_map/all_to_all | solution.py:405
  17.1 15.4 %collective-permute-start.5 = (bf16[768,2048]{1,0:T(8,128)(2,1)}, bf16[768,2048]{1,0:T(8,128)(2,1)}, u32[]{:S(2)}, u32[]{:S(2)}) collective-permute-start(bf16[768,2048]{1,0:T(8,128)(2,1)} %mine_ref.7), channel_id=1, source_target_pairs={{0,4},{4,0},{8,12},{12,8},{16,20},{20,16},{24,28},{28,24},{1,5},{5... | collective-permute-start | bytes 9437192 | tf_op jit(solution)/shard_map/ppermute | solution.py:402
  29.6 27.0 %collective-permute-start.3 = (bf16[2048,256]{1,0:T(8,128)(2,1)}, bf16[2048,256]{1,0:T(8,128)(2,1)}, u32[]{:S(2)}, u32[]{:S(2)}) collective-permute-start(bf16[2048,256]{1,0:T(8,128)(2,1)} %collective-permute-done.1.rest_2_), channel_id=1, source_target_pairs={{8,0},{12,4},{16,8},{20,12},{9,1},{13,5},{17,9},{21,13},{10,2},{14... | collective-permute-start | bytes 3145736 | tf_op jit(solution)/shard_map/ppermute | solution.py:414
  30.9 25.7 %collective-permute-start.4 = (bf16[2048,256]{1,0:T(8,128)(2,1)}, bf16[2048,256]{1,0:T(8,128)(2,1)}, u32[]{:S(2)}, u32[]{:S(2)}) collective-permute-start(bf16[2048,256]{1,0:T(8,128)(2,1)} %collective-permute-done.2.rest_1_.rest_0_), channel_id=1, source_target_pairs={{8,16},{12,20},{16,24},{20,28},{9,17},{13,21},{17,25},{21,29},{10,... | collective-permute-start | bytes 3145736 | tf_op jit(solution)/shard_map/ppermute | solution.py:414
  40.3 28.7 %collective-permute-start.12 = (bf16[384,512]{1,0:T(8,128)(2,1)}, bf16[384,512]{1,0:T(8,128)(2,1)}, u32[]{:S(2)}, u32[]{:S(2)}) collective-permute-start(bf16[384,512]{1,0:T(8,128)(2,1)} %get-tuple-element.44), channel_id=1, source_target_pairs={{0,1},{1,0},{2,3},{3,2},{4,5},{5,4},{6,7},{7,6},{8,9},{9,8},{10,11... | collective-permute-start | bytes 1179656 | tf_op jit(solution)/shard_map/ppermute | solution.py:409
  42.0 27.1 %collective-permute-start.13 = (bf16[384,512]{1,0:T(8,128)(2,1)}, bf16[384,512]{1,0:T(8,128)(2,1)}, u32[]{:S(2)}, u32[]{:S(2)}) collective-permute-start(bf16[384,512]{1,0:T(8,128)(2,1)} %get-tuple-element.45), channel_id=1, source_target_pairs={{0,2},{1,3},{2,0},{3,1},{4,6},{5,7},{6,4},{7,5},{8,10},{9,11},{10,... | collective-permute-start | bytes 1179656 | tf_op jit(solution)/shard_map/ppermute | solution.py:409
  43.6 25.6 %collective-permute-start.14 = (bf16[384,512]{1,0:T(8,128)(2,1)}, bf16[384,512]{1,0:T(8,128)(2,1)}, u32[]{:S(2)}, u32[]{:S(2)}) collective-permute-start(bf16[384,512]{1,0:T(8,128)(2,1)} %get-tuple-element.46), channel_id=1, source_target_pairs={{0,3},{1,2},{2,1},{3,0},{4,7},{5,6},{6,5},{7,4},{8,11},{9,10},{10,... | collective-permute-start | bytes 1179656 | tf_op jit(solution)/shard_map/ppermute | solution.py:409
  56.6 8.8 %all-to-all-start.1 = ((f32[4,96,128]{2,1,0:T(8,128)}), f32[4,96,128]{2,1,0:T(8,128)S(1)}, u32[]{:S(2)}, u32[]{:S(2)}) async-start(f32[4,96,128]{2,1,0:T(8,128)} %shard_map.58), calls=%async_computation.1 | async-start | bytes 393216 | tf_op jit(solution)/shard_map/all_to_all | solution.py:405
  60.1 21.8 %collective-permute-start.7 = (bf16[2048,256]{1,0:T(8,128)(2,1)}, bf16[2048,256]{1,0:T(8,128)(2,1)}, u32[]{:S(2)}, u32[]{:S(2)}) collective-permute-start(bf16[2048,256]{1,0:T(8,128)(2,1)} %collective-permute-done.4.rest_0_.rest_1_), channel_id=1, source_target_pairs={{16,24},{20,28},{17,25},{21,29},{18,26},{22,30},{19,27},{23,31}} | collective-permute-start | bytes 3145736 | tf_op jit(solution)/shard_map/ppermute | solution.py:414
  61.8 26.4 %collective-permute-start.8 = (bf16[2048,256]{1,0:T(8,128)(2,1)}, bf16[2048,256]{1,0:T(8,128)(2,1)}, u32[]{:S(2)}, u32[]{:S(2)}) collective-permute-start(bf16[2048,256]{1,0:T(8,128)(2,1)} %collective-permute-done.3.rest_2_.rest_3_), channel_id=1, source_target_pairs={{8,0},{12,4},{9,1},{13,5},{10,2},{14,6},{11,3},{15,7}} | collective-permute-start | bytes 3145736 | tf_op jit(solution)/shard_map/ppermute | solution.py:414
  65.3 14.8 %all-to-all-start.2 = ((bf16[4,1024,128]{2,1,0:T(8,128)(2,1)}), bf16[4,1024,128]{2,1,0:T(8,128)(2,1)S(1)}, u32[]{:S(2)}, u32[]{:S(2)}) async-start(bf16[4,1024,128]{2,1,0:T(8,128)(2,1)} %shard_map.55), calls=%async_computation.2 | async-start | bytes 2097152 | tf_op jit(solution)/shard_map/all_to_all | solution.py:405
  69.0 10.8 %collective-permute-start.6 = (f32[4,96,128]{2,1,0:T(8,128)S(1)}, f32[4,96,128]{2,1,0:T(8,128)S(1)}, u32[]{:S(2)}, u32[]{:S(2)}) collective-permute-start(f32[4,96,128]{2,1,0:T(8,128)S(1)} %all-to-all-done.1.mine_ref), channel_id=1, source_target_pairs={{0,4},{4,0},{8,12},{12,8},{16,20},{20,16},{24,28},{28,24},{1,5},{5... | collective-permute-start | bytes 589832 | tf_op jit(solution)/shard_map/ppermute | solution.py:402
  76.6 22.2 %collective-permute-start.15 = (bf16[384,256]{1,0:T(8,128)(2,1)}, bf16[384,256]{1,0:T(8,128)(2,1)S(1)}, u32[]{:S(2)}, u32[]{:S(2)}) collective-permute-start(bf16[384,256]{1,0:T(8,128)(2,1)} %get-tuple-element.48), channel_id=1, source_target_pairs={{0,1},{1,0},{2,3},{3,2},{4,5},{5,4},{6,7},{7,6},{8,9},{9,8},{10,11... | collective-permute-start | bytes 589832 | tf_op jit(solution)/shard_map/ppermute | solution.py:409
  78.4 20.8 %collective-permute-start.16 = (bf16[384,256]{1,0:T(8,128)(2,1)}, bf16[384,256]{1,0:T(8,128)(2,1)S(1)}, u32[]{:S(2)}, u32[]{:S(2)}) collective-permute-start(bf16[384,256]{1,0:T(8,128)(2,1)} %get-tuple-element.49), channel_id=1, source_target_pairs={{0,2},{1,3},{2,0},{3,1},{4,6},{5,7},{6,4},{7,5},{8,10},{9,11},{10,... | collective-permute-start | bytes 589832 | tf_op jit(solution)/shard_map/ppermute | solution.py:409
  79.9 19.3 %collective-permute-start.17 = (bf16[384,256]{1,0:T(8,128)(2,1)}, bf16[384,256]{1,0:T(8,128)(2,1)S(1)}, u32[]{:S(2)}, u32[]{:S(2)}) collective-permute-start(bf16[384,256]{1,0:T(8,128)(2,1)} %get-tuple-element.50), channel_id=1, source_target_pairs={{0,3},{1,2},{2,1},{3,0},{4,7},{5,6},{6,5},{7,4},{8,11},{9,10},{10,... | collective-permute-start | bytes 589832 | tf_op jit(solution)/shard_map/ppermute | solution.py:409
  95.6 7.2 %collective-permute-start.9 = (bf16[384,256]{1,0:T(8,128)(2,1)S(1)}, bf16[384,256]{1,0:T(8,128)(2,1)S(1)}, u32[]{:S(2)}, u32[]{:S(2)}) collective-permute-start(bf16[384,256]{1,0:T(8,128)(2,1)S(1)} %get-tuple-element.40), channel_id=1, source_target_pairs={{0,1},{1,0},{2,3},{3,2},{4,5},{5,4},{6,7},{7,6},{8,9},{9,8},{10,11... | collective-permute-start | bytes 589832 | tf_op jit(solution)/shard_map/ppermute | solution.py:409
  97.3 6.8 %collective-permute-start.10 = (bf16[384,256]{1,0:T(8,128)(2,1)S(1)}, bf16[384,256]{1,0:T(8,128)(2,1)S(1)}, u32[]{:S(2)}, u32[]{:S(2)}) collective-permute-start(bf16[384,256]{1,0:T(8,128)(2,1)S(1)} %get-tuple-element.41), channel_id=1, source_target_pairs={{0,2},{1,3},{2,0},{3,1},{4,6},{5,7},{6,4},{7,5},{8,10},{9,11},{10,... | collective-permute-start | bytes 589832 | tf_op jit(solution)/shard_map/ppermute | solution.py:409
  98.8 6.6 %collective-permute-start.11 = (bf16[384,256]{1,0:T(8,128)(2,1)S(1)}, bf16[384,256]{1,0:T(8,128)(2,1)S(1)}, u32[]{:S(2)}, u32[]{:S(2)}) collective-permute-start(bf16[384,256]{1,0:T(8,128)(2,1)S(1)} %get-tuple-element.42), channel_id=1, source_target_pairs={{0,3},{1,2},{2,1},{3,0},{4,7},{5,6},{6,5},{7,4},{8,11},{9,10},{10,... | collective-permute-start | bytes 589832 | tf_op jit(solution)/shard_map/ppermute | solution.py:409
  102.7 5.5 %collective-permute-start.19 = (bf16[192,768]{1,0:T(8,128)(2,1)S(1)}, bf16[192,768]{1,0:T(8,128)(2,1)S(1)}, u32[]{:S(2)}, u32[]{:S(2)}) collective-permute-start(bf16[192,768]{1,0:T(8,128)(2,1)S(1)} %get-tuple-element.53), channel_id=1, source_target_pairs={{0,4},{4,0},{8,12},{12,8},{16,20},{20,16},{24,28},{28,24},{1,5},{5... | collective-permute-start | bytes 884744 | tf_op jit(solution)/shard_map/ppermute | solution.py:402
  108.1 1.4 %collective-permute-start.18 = (bf16[192,256]{1,0:T(8,128)(2,1)S(1)}, bf16[192,256]{1,0:T(8,128)(2,1)S(1)}, u32[]{:S(2)}, u32[]{:S(2)}) collective-permute-start(bf16[192,256]{1,0:T(8,128)(2,1)S(1)} %get-tuple-element.52), channel_id=1, source_target_pairs={{0,4},{4,0},{8,12},{12,8},{16,20},{20,16},{24,28},{28,24},{1,5},{5... | collective-permute-start | bytes 294920 | tf_op jit(solution)/shard_map/ppermute | solution.py:402
  (8 other events, 81.9 us)

commit v8 on v7

--- a/solution.py
+++ b/solution.py
@@ -458,7 +458,7 @@
             before = finished[0][1:]
         turns = [0, 1] if turn == 1 else [turn]
         groups = [[frozen_weight] if n == 0 else [got[option] for option in options[n]] for n in turns]
-        kept = turn == 1 or last
+        kept = True
         cover = 1 if turn == 1 else COVER
         own, *sent = base_products(
             info, [choice_at[n] for n in turns], tokens, other, groups, mp_count, kept, cover, *before

time: 111 us -> 112 us (level)
  transfers between devices with their start and end apart: 23 -> 23, of which waited for: 7 -> 8; matrix products, arithmetic and copies ran while one was open for 1% -> 1% of each run, Pallas kernels for 40% -> 40%
where the time goes in v8:
time: 112 us; the launch traced here: 111 us
  Pallas kernels  45 us (40%)
  starting transfers between devices  37.1 us (33%)
  waiting for transfers between devices  25 us (22%)
  local copies, waits for them, and re-layouts  3.3 us (3%)
    pallas_call x3, Pallas kernels, base_products(): pl.pallas_call(functools.partial(base_kernel, mp_count, [len(group) for g...  21.9 us
    ppermute x6, waiting for transfers between devices, hop(): lax.ppermute(array, 'dp', [(CORES * n + m, CORES * (n - side) + m) for n...  19 us
    ppermute x6, starting transfers between devices, hop(): lax.ppermute(array, 'dp', [(CORES * n + m, CORES * (n - side) + m) for n...  13.8 us
    all_to_all x3, starting transfers between devices, trade(): return lax.all_to_all(array, 'mp', 0, 0)  11.8 us
    ppermute x9, starting transfers between devices, pass_round(): lax.ppermute(block, 'mp', [(m, m ^ n) for m in range(mp_count)])  10.7 us
    pallas_call x1, Pallas kernels, low_sums(): pl.pallas_call(functools.partial(low_kernel, adapters, 2 * rank), in_spec...  8.67 us
    pallas_call x2, Pallas kernels, finish(): pl.pallas_call(functools.partial(finish_kernel, mp_count, places), in_spe...  6.16 us
    all_to_all x3, waiting for transfers between devices, trade(): return lax.all_to_all(array, 'mp', 0, 0)  3.37 us
  transfers between devices with their start and end apart: 23, of which 8 were waited for; matrix products, arithmetic and copies ran while one was open for 1% of the time, Pallas kernels for 40%

profile of v8, /device:TPU:0, one launch (start us, length us, event | category | flops | bytes accessed | tf_op | source)
XLA Modules:
  0.0 110.8 jit_solution(11168150549295230648)
XLA Ops:
  1.3 6.7 %collective-permute-start.2 = (bf16[2048,256]{1,0:T(8,128)(2,1)}, bf16[2048,256]{1,0:T(8,128)(2,1)}, u32[]{:S(2)}, u32[]{:S(2)}) collective-permute-start(bf16[2048,256]{1,0:T(8,128)(2,1)} %rest_0_.1), channel_id=1, source_target_pairs={{0,8},{4,12},{8,16},{12,20},{16,24},{20,28},{1,9},{5,13},{9,17},{1... | collective-permute-start | bytes 3145736 | tf_op jit(solution)/shard_map/ppermute | solution.py:414
  8.1 2.2 %copy-done = bf16[8192,256]{1,0:T(8,128)(2,1)S(1)} copy-done((bf16[8192,256]{1,0:T(8,128)(2,1)S(1)}, bf16[8192,256]{1,0:T(8,128)(2,1)}, u32[]{:S(2)}) %copy-start) | copy-done | bytes 4194328
  10.2 2.3 %shard_map.57 = bf16[4,2048,128]{2,1,0:T(8,128)(2,1)} custom-call(s32[18]{0:T(128)S(1)} %stack.72.info_ref, bf16[8192,256]{1,0:T(8,128)(2,1)S(1)} %copy-done), custom_call_target="tpu_custom_call" | custom-call | bytes 4194304 | tf_op jit(solution)/shard_map/pallas_call | solution.py:133
  12.6 4.6 %all-to-all-start = ((bf16[4,2048,128]{2,1,0:T(8,128)(2,1)}), bf16[4,2048,128]{2,1,0:T(8,128)(2,1)}, u32[]{:S(2)}, u32[]{:S(2)}) async-start(bf16[4,2048,128]{2,1,0:T(8,128)(2,1)} %shard_map.57), calls=%async_computation | async-start | bytes 4194304 | tf_op jit(solution)/shard_map/all_to_all | solution.py:405
  17.7 1.7 %shard_map.55 = bf16[4,1024,128]{2,1,0:T(8,128)(2,1)} custom-call(s32[18]{0:T(128)S(1)} %stack.72.info_ref, bf16[2,128,1024]{2,1,0:T(8,128)(2,1)S(1)} %bitcast.18), custom_call_target="tpu_custom_call" | custom-call | flops 274877906944 | bytes 2097152 | tf_op jit(solution)/shard_map/pallas_call | solution.py:161
  20.5 7.9 %collective-permute-done.1.rest_2_ = bf16[2048,256]{1,0:T(8,128)(2,1)} collective-permute-done((bf16[2048,256]{1,0:T(8,128)(2,1)}, bf16[2048,256]{1,0:T(8,128)(2,1)}, u32[]{:S(2)}, u32[]{:S(2)}) %collective-permute-start.1) | collective-permute-done | bytes 1048608 | tf_op jit(solution)/shard_map/ppermute | solution.py:414
  30.9 1.7 %collective-permute-start.4 = (bf16[2048,256]{1,0:T(8,128)(2,1)}, bf16[2048,256]{1,0:T(8,128)(2,1)}, u32[]{:S(2)}, u32[]{:S(2)}) collective-permute-start(bf16[2048,256]{1,0:T(8,128)(2,1)} %collective-permute-done.2.rest_1_.rest_0_), channel_id=1, source_target_pairs={{8,16},{12,20},{16,24},{20,28},{9,17},{13,21},{17,25},{21,29},{10,... | collective-permute-start | bytes 3145736 | tf_op jit(solution)/shard_map/ppermute | solution.py:414
  32.5 7.8 %shard_map.56 = (f32[384,512]{1,0:T(8,128)S(1)}, bf16[384,512]{1,0:T(8,128)(2,1)}, bf16[384,512]{1,0:T(8,128)(2,1)}, bf16[384,512]{1,0:T(8,128)(2,1)}) custom-call(s32[18]{0:T(128)S(1)} %stack.72.info_ref, bf16[768,2048]{1,0:T(8,128)(2,1)} %mine_ref.7, bf16[768,2048]{1,0:T(8,128)(2,1)} %collective-permute-done.5.other_ref, bf16[2048,256]{1,0:T(8,128)(2,1)S(1)} %copy-done.3, ...), custom_call_target="tpu_custom_call" | custom-call | flops 3221225472 | bytes 9961472 | tf_op jit(solution)/shard_map/pallas_call | solution.py:93
  40.3 1.7 %collective-permute-start.12 = (bf16[384,512]{1,0:T(8,128)(2,1)}, bf16[384,512]{1,0:T(8,128)(2,1)}, u32[]{:S(2)}, u32[]{:S(2)}) collective-permute-start(bf16[384,512]{1,0:T(8,128)(2,1)} %get-tuple-element.44), channel_id=1, source_target_pairs={{0,1},{1,0},{2,3},{3,2},{4,5},{5,4},{6,7},{7,6},{8,9},{9,8},{10,11... | collective-permute-start | bytes 1179656 | tf_op jit(solution)/shard_map/ppermute | solution.py:409
  42.0 1.5 %collective-permute-start.13 = (bf16[384,512]{1,0:T(8,128)(2,1)}, bf16[384,512]{1,0:T(8,128)(2,1)}, u32[]{:S(2)}, u32[]{:S(2)}) collective-permute-start(bf16[384,512]{1,0:T(8,128)(2,1)} %get-tuple-element.45), channel_id=1, source_target_pairs={{0,2},{1,3},{2,0},{3,1},{4,6},{5,7},{6,4},{7,5},{8,10},{9,11},{10,... | collective-permute-start | bytes 1179656 | tf_op jit(solution)/shard_map/ppermute | solution.py:409
  43.9 8.7 %shard_map.58 = f32[4,96,128]{2,1,0:T(8,128)} custom-call(s32[18]{0:T(128)S(1)} %stack.72.info_ref, bf16[768,2048]{1,0:T(8,128)(2,1)} %mine_ref.7, bf16[768,2048]{1,0:T(8,128)(2,1)} %collective-permute-done.5.other_ref, s32[768,1]{1,0:T(8,128)S(1)} %reshape.12.mine_ids, s32[768,1]{1,0:T(8,128)S(1)} %reshape.13.other_ids, ...), custom_call_target="tpu_custom_call" | custom-call | flops 206158430208 | bytes 8388608 | tf_op jit(solution)/shard_map/pallas_call | solution.py:213
  52.5 4.0 %collective-permute-done.3.rest_2_.rest_3_ = bf16[2048,256]{1,0:T(8,128)(2,1)} collective-permute-done((bf16[2048,256]{1,0:T(8,128)(2,1)}, bf16[2048,256]{1,0:T(8,128)(2,1)}, u32[]{:S(2)}, u32[]{:S(2)}) %collective-permute-start.3) | collective-permute-done | bytes 1048608 | tf_op jit(solution)/shard_map/ppermute | solution.py:414
  56.6 3.6 %all-to-all-start.1 = ((f32[4,96,128]{2,1,0:T(8,128)}), f32[4,96,128]{2,1,0:T(8,128)S(1)}, u32[]{:S(2)}, u32[]{:S(2)}) async-start(f32[4,96,128]{2,1,0:T(8,128)} %shard_map.58), calls=%async_computation.1 | async-start | bytes 393216 | tf_op jit(solution)/shard_map/all_to_all | solution.py:405
  60.1 1.6 %collective-permute-start.7 = (bf16[2048,256]{1,0:T(8,128)(2,1)}, bf16[2048,256]{1,0:T(8,128)(2,1)}, u32[]{:S(2)}, u32[]{:S(2)}) collective-permute-start(bf16[2048,256]{1,0:T(8,128)(2,1)} %collective-permute-done.4.rest_0_.rest_1_), channel_id=1, source_target_pairs={{16,24},{20,28},{17,25},{21,29},{18,26},{22,30},{19,27},{23,31}} | collective-permute-start | bytes 3145736 | tf_op jit(solution)/shard_map/ppermute | solution.py:414
  63.0 2.3 %all-to-all-done.1.mine_ref = f32[4,96,128]{2,1,0:T(8,128)S(1)} async-done(((f32[4,96,128]{2,1,0:T(8,128)}), f32[4,96,128]{2,1,0:T(8,128)S(1)}, u32[]{:S(2)}, u32[]{:S(2)}) %all-to-all-start.1) | async-done | bytes 196640 | tf_op jit(solution)/shard_map/all_to_all | solution.py:405
  65.3 3.7 %all-to-all-start.2 = ((bf16[4,1024,128]{2,1,0:T(8,128)(2,1)}), bf16[4,1024,128]{2,1,0:T(8,128)(2,1)S(1)}, u32[]{:S(2)}, u32[]{:S(2)}) async-start(bf16[4,1024,128]{2,1,0:T(8,128)(2,1)} %shard_map.55), calls=%async_computation.2 | async-start | bytes 2097152 | tf_op jit(solution)/shard_map/all_to_all | solution.py:405
  69.1 6.7 %shard_map.61 = (f32[384,256]{1,0:T(8,128)S(1)}, bf16[384,256]{1,0:T(8,128)(2,1)}, bf16[384,256]{1,0:T(8,128)(2,1)}, bf16[384,256]{1,0:T(8,128)(2,1)S(1)}) custom-call(s32[18]{0:T(128)S(1)} %stack.72.info_ref, bf16[768,2048]{1,0:T(8,128)(2,1)} %mine_ref.7, bf16[768,2048]{1,0:T(8,128)(2,1)} %collective-permute-done.5.other_ref, ...), custom_call_target="tpu_custom_call" | custom-call | flops 103079215104 | bytes 8126464 | tf_op jit(solution)/shard_map/pallas_call | solution.py:93
  75.9 1.8 %collective-permute-start.15 = (bf16[384,256]{1,0:T(8,128)(2,1)}, bf16[384,256]{1,0:T(8,128)(2,1)S(1)}, u32[]{:S(2)}, u32[]{:S(2)}) collective-permute-start(bf16[384,256]{1,0:T(8,128)(2,1)} %get-tuple-element.48), channel_id=1, source_target_pairs={{0,1},{1,0},{2,3},{3,2},{4,5},{5,4},{6,7},{7,6},{8,9},{9,8},{10,11... | collective-permute-start | bytes 589832 | tf_op jit(solution)/shard_map/ppermute | solution.py:409
  80.5 1.7 %shard_map.59.rest_4_.delta_ref = bf16[4,384,256]{2,1,0:T(8,128)(2,1)S(1)} custom-call(s32[18]{0:T(128)S(1)} %stack.72.info_ref, s32[768,1]{1,0:T(8,128)S(1)} %reshape.12.mine_ids, s32[768,1]{1,0:T(8,128)S(1)} %reshape.13.other_ids, f32[4,96,128]{2,1,0:T(8,128)S(1)} %all-to-all-done.1.mine_ref, f32[4,96,128]{2,1,0:T(8,128)S(1)} %collective-permute-done.6.other_ref, ...), custom_call_target="tpu_custom_call" | custom-call | flops 402653184 | bytes 1048576 | tf_op jit(solution)/shard_map/pallas_call | solution.py:278
  82.3 5.9 %collective-permute-done.8.rest_3_ = bf16[2048,256]{1,0:T(8,128)(2,1)} collective-permute-done((bf16[2048,256]{1,0:T(8,128)(2,1)}, bf16[2048,256]{1,0:T(8,128)(2,1)}, u32[]{:S(2)}, u32[]{:S(2)}) %collective-permute-start.8) | collective-permute-done | bytes 1048608 | tf_op jit(solution)/shard_map/ppermute | solution.py:414
  88.1 7.5 %shard_map.60 = (f32[384,256]{1,0:T(8,128)S(1)}, bf16[384,256]{1,0:T(8,128)(2,1)S(1)}, bf16[384,256]{1,0:T(8,128)(2,1)S(1)}, bf16[384,256]{1,0:T(8,128)(2,1)S(1)}) custom-call(s32[18]{0:T(128)S(1)} %stack.72.info_ref, bf16[768,2048]{1,0:T(8,128)(2,1)} %mine_ref.7, bf16[768,2048]{1,0:T(8,128)(2,1)} %collective-permute-done.5.other_ref, ...), custom_call_target="tpu_custom_call" | custom-call | flops 103079215104 | bytes 8126464 | tf_op jit(solution)/shard_map/pallas_call | solution.py:93
  95.6 1.8 %collective-permute-start.9 = (bf16[384,256]{1,0:T(8,128)(2,1)S(1)}, bf16[384,256]{1,0:T(8,128)(2,1)S(1)}, u32[]{:S(2)}, u32[]{:S(2)}) collective-permute-start(bf16[384,256]{1,0:T(8,128)(2,1)S(1)} %get-tuple-element.40), channel_id=1, source_target_pairs={{0,1},{1,0},{2,3},{3,2},{4,5},{5,4},{6,7},{7,6},{8,9},{9,8},{10,11... | collective-permute-start | bytes 589832 | tf_op jit(solution)/shard_map/ppermute | solution.py:409
  99.2 3.5 %shard_map.62 = (bf16[192,2048]{1,0:T(8,128)(2,1)}, bf16[192,768]{1,0:T(8,128)(2,1)S(1)}) custom-call(s32[18]{0:T(128)S(1)} %stack.72.info_ref, bf16[4,384,256]{2,1,0:T(8,128)(2,1)S(1)} %shard_map.59.rest_4_.delta_ref, f32[384,512]{1,0:T(8,128)S(1)} %copy-done.2, bf16[384,512]{1,0:T(8,128)(2,1)} %collective-permute-done.12.rest_4_.rest_1_, ...), custom_call_target="tpu_custom_call" | custom-call | flops 1179648 | bytes 3538944 | tf_op jit(solution)/shard_map/pallas_call | solution.py:334
  105.4 2.7 %shard_map.63 = (bf16[192,2048]{1,0:T(8,128)(2,1)}, bf16[192,256]{1,0:T(8,128)(2,1)S(1)}) custom-call(s32[18]{0:T(128)S(1)} %stack.72.info_ref, bf16[4,384,256]{2,1,0:T(8,128)(2,1)S(1)} %shard_map.59.rest_4_.delta_ref, f32[384,256]{1,0:T(8,128)S(1)} %get-tuple-element.39.rest_8_.rest_0_, ...), custom_call_target="tpu_custom_call", output_to_operand_aliasing={{0}: (6, {})} | custom-call | flops 393216 | bytes 1179648 | tf_op jit(solution)/shard_map/pallas_call | solution.py:334
  (48 shorter events, 17.1 us)
Async XLA Ops:
  0.0 28.4 %collective-permute-start.1 = (bf16[2048,256]{1,0:T(8,128)(2,1)}, bf16[2048,256]{1,0:T(8,128)(2,1)}, u32[]{:S(2)}, u32[]{:S(2)}) collective-permute-start(bf16[2048,256]{1,0:T(8,128)(2,1)} %rest_0_.1), channel_id=1, source_target_pairs={{8,0},{12,4},{16,8},{20,12},{24,16},{28,20},{9,1},{13,5},{17,9},{2... | collective-permute-start | bytes 3145736 | tf_op jit(solution)/shard_map/ppermute | solution.py:414
  1.3 28.3 %collective-permute-start.2 = (bf16[2048,256]{1,0:T(8,128)(2,1)}, bf16[2048,256]{1,0:T(8,128)(2,1)}, u32[]{:S(2)}, u32[]{:S(2)}) collective-permute-start(bf16[2048,256]{1,0:T(8,128)(2,1)} %rest_0_.1), channel_id=1, source_target_pairs={{0,8},{4,12},{8,16},{12,20},{16,24},{20,28},{1,9},{5,13},{9,17},{1... | collective-permute-start | bytes 3145736 | tf_op jit(solution)/shard_map/ppermute | solution.py:414
  7.9 11.7 %collective-permute-start = (s32[768]{0:T(1024)}, s32[768]{0:T(1024)}, u32[]{:S(2)}, u32[]{:S(2)}) collective-permute-start(s32[768]{0:T(1024)} %param.9), channel_id=1, source_target_pairs={{0,4},{4,0},{8,12},{12,8},{16,20},{20,16},{24,28},{28,24},{1,5},{5... | collective-permute-start | bytes 9224 | tf_op jit(solution)/shard_map/ppermute | solution.py:402
  12.6 31.3 %all-to-all-start = ((bf16[4,2048,128]{2,1,0:T(8,128)(2,1)}), bf16[4,2048,128]{2,1,0:T(8,128)(2,1)}, u32[]{:S(2)}, u32[]{:S(2)}) async-start(bf16[4,2048,128]{2,1,0:T(8,128)(2,1)} %shard_map.57), calls=%async_computation | async-start | bytes 4194304 | tf_op jit(solution)/shard_map/all_to_all | solution.py:405
  17.1 15.4 %collective-permute-start.5 = (bf16[768,2048]{1,0:T(8,128)(2,1)}, bf16[768,2048]{1,0:T(8,128)(2,1)}, u32[]{:S(2)}, u32[]{:S(2)}) collective-permute-start(bf16[768,2048]{1,0:T(8,128)(2,1)} %mine_ref.7), channel_id=1, source_target_pairs={{0,4},{4,0},{8,12},{12,8},{16,20},{20,16},{24,28},{28,24},{1,5},{5... | collective-permute-start | bytes 9437192 | tf_op jit(solution)/shard_map/ppermute | solution.py:402
  29.6 27.0 %collective-permute-start.3 = (bf16[2048,256]{1,0:T(8,128)(2,1)}, bf16[2048,256]{1,0:T(8,128)(2,1)}, u32[]{:S(2)}, u32[]{:S(2)}) collective-permute-start(bf16[2048,256]{1,0:T(8,128)(2,1)} %collective-permute-done.1.rest_2_), channel_id=1, source_target_pairs={{8,0},{12,4},{16,8},{20,12},{9,1},{13,5},{17,9},{21,13},{10,2},{14... | collective-permute-start | bytes 3145736 | tf_op jit(solution)/shard_map/ppermute | solution.py:414
  30.9 25.7 %collective-permute-start.4 = (bf16[2048,256]{1,0:T(8,128)(2,1)}, bf16[2048,256]{1,0:T(8,128)(2,1)}, u32[]{:S(2)}, u32[]{:S(2)}) collective-permute-start(bf16[2048,256]{1,0:T(8,128)(2,1)} %collective-permute-done.2.rest_1_.rest_0_), channel_id=1, source_target_pairs={{8,16},{12,20},{16,24},{20,28},{9,17},{13,21},{17,25},{21,29},{10,... | collective-permute-start | bytes 3145736 | tf_op jit(solution)/shard_map/ppermute | solution.py:414
  40.3 28.7 %collective-permute-start.12 = (bf16[384,512]{1,0:T(8,128)(2,1)}, bf16[384,512]{1,0:T(8,128)(2,1)}, u32[]{:S(2)}, u32[]{:S(2)}) collective-permute-start(bf16[384,512]{1,0:T(8,128)(2,1)} %get-tuple-element.44), channel_id=1, source_target_pairs={{0,1},{1,0},{2,3},{3,2},{4,5},{5,4},{6,7},{7,6},{8,9},{9,8},{10,11... | collective-permute-start | bytes 1179656 | tf_op jit(solution)/shard_map/ppermute | solution.py:409
  42.0 27.1 %collective-permute-start.13 = (bf16[384,512]{1,0:T(8,128)(2,1)}, bf16[384,512]{1,0:T(8,128)(2,1)}, u32[]{:S(2)}, u32[]{:S(2)}) collective-permute-start(bf16[384,512]{1,0:T(8,128)(2,1)} %get-tuple-element.45), channel_id=1, source_target_pairs={{0,2},{1,3},{2,0},{3,1},{4,6},{5,7},{6,4},{7,5},{8,10},{9,11},{10,... | collective-permute-start | bytes 1179656 | tf_op jit(solution)/shard_map/ppermute | solution.py:409
  43.5 25.6 %collective-permute-start.14 = (bf16[384,512]{1,0:T(8,128)(2,1)}, bf16[384,512]{1,0:T(8,128)(2,1)}, u32[]{:S(2)}, u32[]{:S(2)}) collective-permute-start(bf16[384,512]{1,0:T(8,128)(2,1)} %get-tuple-element.46), channel_id=1, source_target_pairs={{0,3},{1,2},{2,1},{3,0},{4,7},{5,6},{6,5},{7,4},{8,11},{9,10},{10,... | collective-permute-start | bytes 1179656 | tf_op jit(solution)/shard_map/ppermute | solution.py:409
  56.6 8.8 %all-to-all-start.1 = ((f32[4,96,128]{2,1,0:T(8,128)}), f32[4,96,128]{2,1,0:T(8,128)S(1)}, u32[]{:S(2)}, u32[]{:S(2)}) async-start(f32[4,96,128]{2,1,0:T(8,128)} %shard_map.58), calls=%async_computation.1 | async-start | bytes 393216 | tf_op jit(solution)/shard_map/all_to_all | solution.py:405
  60.1 22.1 %collective-permute-start.7 = (bf16[2048,256]{1,0:T(8,128)(2,1)}, bf16[2048,256]{1,0:T(8,128)(2,1)}, u32[]{:S(2)}, u32[]{:S(2)}) collective-permute-start(bf16[2048,256]{1,0:T(8,128)(2,1)} %collective-permute-done.4.rest_0_.rest_1_), channel_id=1, source_target_pairs={{16,24},{20,28},{17,25},{21,29},{18,26},{22,30},{19,27},{23,31}} | collective-permute-start | bytes 3145736 | tf_op jit(solution)/shard_map/ppermute | solution.py:414
  61.7 26.4 %collective-permute-start.8 = (bf16[2048,256]{1,0:T(8,128)(2,1)}, bf16[2048,256]{1,0:T(8,128)(2,1)}, u32[]{:S(2)}, u32[]{:S(2)}) collective-permute-start(bf16[2048,256]{1,0:T(8,128)(2,1)} %collective-permute-done.3.rest_2_.rest_3_), channel_id=1, source_target_pairs={{8,0},{12,4},{9,1},{13,5},{10,2},{14,6},{11,3},{15,7}} | collective-permute-start | bytes 3145736 | tf_op jit(solution)/shard_map/ppermute | solution.py:414
  65.3 15.2 %all-to-all-start.2 = ((bf16[4,1024,128]{2,1,0:T(8,128)(2,1)}), bf16[4,1024,128]{2,1,0:T(8,128)(2,1)S(1)}, u32[]{:S(2)}, u32[]{:S(2)}) async-start(bf16[4,1024,128]{2,1,0:T(8,128)(2,1)} %shard_map.55), calls=%async_computation.2 | async-start | bytes 2097152 | tf_op jit(solution)/shard_map/all_to_all | solution.py:405
  69.0 10.1 %collective-permute-start.6 = (f32[4,96,128]{2,1,0:T(8,128)S(1)}, f32[4,96,128]{2,1,0:T(8,128)S(1)}, u32[]{:S(2)}, u32[]{:S(2)}) collective-permute-start(f32[4,96,128]{2,1,0:T(8,128)S(1)} %all-to-all-done.1.mine_ref), channel_id=1, source_target_pairs={{0,4},{4,0},{8,12},{12,8},{16,20},{20,16},{24,28},{28,24},{1,5},{5... | collective-permute-start | bytes 589832 | tf_op jit(solution)/shard_map/ppermute | solution.py:402
  75.9 23.0 %collective-permute-start.15 = (bf16[384,256]{1,0:T(8,128)(2,1)}, bf16[384,256]{1,0:T(8,128)(2,1)S(1)}, u32[]{:S(2)}, u32[]{:S(2)}) collective-permute-start(bf16[384,256]{1,0:T(8,128)(2,1)} %get-tuple-element.48), channel_id=1, source_target_pairs={{0,1},{1,0},{2,3},{3,2},{4,5},{5,4},{6,7},{7,6},{8,9},{9,8},{10,11... | collective-permute-start | bytes 589832 | tf_op jit(solution)/shard_map/ppermute | solution.py:409
  77.6 21.5 %collective-permute-start.16 = (bf16[384,256]{1,0:T(8,128)(2,1)}, bf16[384,256]{1,0:T(8,128)(2,1)S(1)}, u32[]{:S(2)}, u32[]{:S(2)}) collective-permute-start(bf16[384,256]{1,0:T(8,128)(2,1)} %get-tuple-element.49), channel_id=1, source_target_pairs={{0,2},{1,3},{2,0},{3,1},{4,6},{5,7},{6,4},{7,5},{8,10},{9,11},{10,... | collective-permute-start | bytes 589832 | tf_op jit(solution)/shard_map/ppermute | solution.py:409
  79.1 20.1 %collective-permute-start.17 = (bf16[384,256]{1,0:T(8,128)(2,1)S(1)}, bf16[384,256]{1,0:T(8,128)(2,1)S(1)}, u32[]{:S(2)}, u32[]{:S(2)}) collective-permute-start(bf16[384,256]{1,0:T(8,128)(2,1)S(1)} %get-tuple-element.50), channel_id=1, source_target_pairs={{0,3},{1,2},{2,1},{3,0},{4,7},{5,6},{6,5},{7,4},{8,11},{9,10},{10,... | collective-permute-start | bytes 589832 | tf_op jit(solution)/shard_map/ppermute | solution.py:409
  82.2 16.9 %copy-start.2 = (f32[384,512]{1,0:T(8,128)S(1)}, f32[384,512]{1,0:T(8,128)}, u32[]{:S(2)}) copy-start(f32[384,512]{1,0:T(8,128)} %copy-done.1) | copy-start | bytes 2359300
  95.6 7.1 %collective-permute-start.9 = (bf16[384,256]{1,0:T(8,128)(2,1)S(1)}, bf16[384,256]{1,0:T(8,128)(2,1)S(1)}, u32[]{:S(2)}, u32[]{:S(2)}) collective-permute-start(bf16[384,256]{1,0:T(8,128)(2,1)S(1)} %get-tuple-element.40), channel_id=1, source_target_pairs={{0,1},{1,0},{2,3},{3,2},{4,5},{5,4},{6,7},{7,6},{8,9},{9,8},{10,11... | collective-permute-start | bytes 589832 | tf_op jit(solution)/shard_map/ppermute | solution.py:409
  97.4 6.8 %collective-permute-start.10 = (bf16[384,256]{1,0:T(8,128)(2,1)S(1)}, bf16[384,256]{1,0:T(8,128)(2,1)S(1)}, u32[]{:S(2)}, u32[]{:S(2)}) collective-permute-start(bf16[384,256]{1,0:T(8,128)(2,1)S(1)} %get-tuple-element.41), channel_id=1, source_target_pairs={{0,2},{1,3},{2,0},{3,1},{4,6},{5,7},{6,4},{7,5},{8,10},{9,11},{10,... | collective-permute-start | bytes 589832 | tf_op jit(solution)/shard_map/ppermute | solution.py:409
  98.8 6.6 %collective-permute-start.11 = (bf16[384,256]{1,0:T(8,128)(2,1)S(1)}, bf16[384,256]{1,0:T(8,128)(2,1)S(1)}, u32[]{:S(2)}, u32[]{:S(2)}) collective-permute-start(bf16[384,256]{1,0:T(8,128)(2,1)S(1)} %get-tuple-element.42), channel_id=1, source_target_pairs={{0,3},{1,2},{2,1},{3,0},{4,7},{5,6},{6,5},{7,4},{8,11},{9,10},{10,... | collective-permute-start | bytes 589832 | tf_op jit(solution)/shard_map/ppermute | solution.py:409
  102.7 5.5 %collective-permute-start.19 = (bf16[192,768]{1,0:T(8,128)(2,1)S(1)}, bf16[192,768]{1,0:T(8,128)(2,1)S(1)}, u32[]{:S(2)}, u32[]{:S(2)}) collective-permute-start(bf16[192,768]{1,0:T(8,128)(2,1)S(1)} %get-tuple-element.53), channel_id=1, source_target_pairs={{0,4},{4,0},{8,12},{12,8},{16,20},{20,16},{24,28},{28,24},{1,5},{5... | collective-permute-start | bytes 884744 | tf_op jit(solution)/shard_map/ppermute | solution.py:402
  108.1 1.4 %collective-permute-start.18 = (bf16[192,256]{1,0:T(8,128)(2,1)S(1)}, bf16[192,256]{1,0:T(8,128)(2,1)S(1)}, u32[]{:S(2)}, u32[]{:S(2)}) collective-permute-start(bf16[192,256]{1,0:T(8,128)(2,1)S(1)} %get-tuple-element.52), channel_id=1, source_target_pairs={{0,4},{4,0},{8,12},{12,8},{16,20},{20,16},{24,28},{28,24},{1,5},{5... | collective-permute-start | bytes 294920 | tf_op jit(solution)/shard_map/ppermute | solution.py:402
  (5 other events, 36.1 us)
